TPU v7x, 1024 devices: a whole 8x8x8 slice. The times are simulated.
1024 devices in a mesh: ctx: 16 (over z_hi, y), exp: 64 (over z_lo, x, core).
Axes of the slice: x: 8, y: 8, z: 8 (z_hi: 2, z_lo: 4; z = z_hi * 4 + z_lo), core: 2. Of those that a mesh axis runs over, the one named last changes fastest.
Arguments:
- out_grad: bfloat16 [2048, 8192], P('ctx', 'exp'), may hold values from -6 to 6
- expert_rows: bfloat16 [16, 512, 8192], P('ctx', None, 'exp'), may hold values from -6 to 6
- expert_index: int32 [2048, 2], P('ctx'), may hold values from 0 to 15, all different within a row; in each aligned block of 128 rows (0 to 127, 128 to 255, ...) at most 32 rows name the same one
- combine: float32 [2048, 2], P('ctx'), may hold values from 0.2 to 1
- head_query: bfloat16 [2048, 8192], P('ctx', 'exp'), may hold values from -16 to 16
- head_key: bfloat16 [2048, 1024], P('ctx'), may hold values from -16 to 16
- head_value: bfloat16 [2048, 1024], P('ctx'), may hold values from -6 to 6
- out_weight: bfloat16 [8192, 8192], P('exp'), may hold values from -0.0625 to 0.0625
Outputs:
- residual_grad: bfloat16 [2048, 8192], P('ctx', 'exp')
- query_grad: bfloat16 [2048, 8192], P('ctx', 'exp')
- key_grad: bfloat16 [2048, 1024], P(('ctx', 'exp'))
- value_grad: bfloat16 [2048, 1024], P(('ctx', 'exp'))
Inputs may be any that keep to these rules, and one draw needn't show every extreme that they name: `expert_index`: each row names 2 different experts. Among the rows of one index of ctx (aligned blocks of 128 rows) no expert is named by more than 32 rows.
All inputs are finite; a program needn't handle non-finite values.
Results may differ from a plain program's by a relative error of at most 0.02.
Values may be sent and summed in bfloat16 or wider, within the bound.
No kernel may reach another device: no remote copies, remote signals or barrier semaphores. Data moves between devices by JAX's collectives and lax.ppermute only.
A program may use at most 32 MiB of HBM per device.

v0:
```python
import math

import jax
import jax.numpy as jnp
from jax import lax
from jax.sharding import PartitionSpec as P

HD = 128
TOP = 2
GROUP = 8


def folded_positions(row_ids, per_device, ctx_count):
    half_rows = per_device // 2
    device = row_ids // per_device
    within = row_ids % per_device
    block = jnp.where(within < half_rows, device, 2 * ctx_count - 1 - device)
    return block * half_rows + within % half_rows


def body(
    out_grad, expert_rows, expert_index, combine, head_query, head_key, head_value, out_weight
):
    ctx_count = lax.axis_size("ctx")
    ctx_place = lax.axis_index("ctx")
    exp_place = lax.axis_index("exp")
    row_count = out_grad.shape[0]
    width = out_grad.shape[1]
    kv_width = head_key.shape[1]
    head_count = width // HD
    kv_local = max(1, head_count // GROUP)
    group_local = head_count // kv_local
    kv_start = exp_place * head_count // GROUP
    score_scale = 1.0 / math.sqrt(HD)
    received = lax.all_to_all(expert_rows, "ctx", split_axis=1, concat_axis=0, tiled=True)
    expert_count = received.shape[0]
    capacity = received.shape[1]
    choices_flat = expert_index.reshape(-1)
    onehot = (choices_flat[:, None] == jnp.arange(expert_count, dtype=jnp.int32)[None, :]).astype(
        jnp.int32
    )
    earlier = jnp.cumsum(onehot, axis=0) - onehot
    slot_ids = jnp.sum(earlier * onehot, axis=1)
    slot_table = received.reshape(expert_count * capacity, width)
    picked = jnp.take(slot_table, choices_flat * capacity + slot_ids, axis=0).reshape(
        row_count, TOP, width
    )
    moe_grad = jnp.sum(combine[:, :, None] * picked.astype(jnp.float32), axis=1)
    residual_grad = (out_grad.astype(jnp.float32) + moe_grad).astype(jnp.bfloat16)
    context_grad = lax.dot_general(
        lax.all_gather(residual_grad, "exp", axis=1, tiled=True),
        out_weight,
        (((1,), (1,)), ((), ())),
        preferred_element_type=jnp.float32,
    ).astype(jnp.bfloat16)
    key_local = lax.dynamic_slice_in_dim(head_key, kv_start * HD, kv_local * HD, 1)
    value_local = lax.dynamic_slice_in_dim(head_value, kv_start * HD, kv_local * HD, 1)
    key_all, value_all = (
        lax.all_gather(key_local, "ctx", axis=0, tiled=True),
        lax.all_gather(value_local, "ctx", axis=0, tiled=True),
    )
    key_count = key_all.shape[0]
    my_position = folded_positions(
        ctx_place * row_count + jnp.arange(row_count, dtype=jnp.int32), row_count, ctx_count
    )
    all_position = folded_positions(jnp.arange(key_count, dtype=jnp.int32), row_count, ctx_count)
    query_heads = head_query.reshape(row_count, kv_local, group_local, HD)
    grad_heads = context_grad.reshape(row_count, kv_local, group_local, HD)
    key_heads = key_all.reshape(key_count, kv_local, HD)
    value_heads = value_all.reshape(key_count, kv_local, HD)
    allowed = all_position[None, :] <= my_position[:, None]
    scores = (
        jnp.einsum("qagd,kad->agqk", query_heads, key_heads, preferred_element_type=jnp.float32)
        * score_scale
    )
    masked = jnp.where(allowed[None, None], scores, -jnp.inf)
    row_max = jnp.max(masked, axis=3, keepdims=True)
    exponent = jnp.where(allowed[None, None], jnp.exp(masked - row_max), 0.0)
    row_sum = jnp.sum(exponent, axis=3, keepdims=True)
    probs = exponent / row_sum
    probs_low = probs.astype(jnp.bfloat16)
    head_out = jnp.einsum(
        "agqk,kad->qagd", probs_low, value_heads, preferred_element_type=jnp.float32
    )
    row_delta = jnp.sum(grad_heads.astype(jnp.float32) * head_out, axis=3)
    delta_term = jnp.transpose(row_delta, (1, 2, 0))[:, :, :, None]
    prob_grad = jnp.einsum(
        "qagd,kad->agqk", grad_heads, value_heads, preferred_element_type=jnp.float32
    )
    score_low = (probs * (prob_grad - delta_term)).astype(jnp.bfloat16)
    query_sum = (
        jnp.einsum("agqk,kad->qagd", score_low, key_heads, preferred_element_type=jnp.float32)
        * score_scale
    )
    query_grad = query_sum.astype(jnp.bfloat16).reshape(row_count, width)
    key_term = (
        jnp.einsum("agqk,qagd->kad", score_low, query_heads, preferred_element_type=jnp.float32)
        * score_scale
    )
    value_term = jnp.einsum(
        "agqk,qagd->kad", probs_low, grad_heads, preferred_element_type=jnp.float32
    )
    both_grads = lax.psum_scatter(
        jnp.concatenate(
            [
                key_term.reshape(lax.axis_size("ctx") * row_count, kv_local * HD),
                value_term.reshape(lax.axis_size("ctx") * row_count, kv_local * HD),
            ],
            axis=1,
        ).astype(jnp.bfloat16),
        "ctx",
        scatter_dimension=0,
        tiled=True,
    ).astype(jnp.float32)
    key_part = both_grads[:, : kv_local * HD]
    value_part = both_grads[:, kv_local * HD :]
    empty = jnp.zeros((row_count, kv_width), jnp.float32)
    key_spread = lax.dynamic_update_slice_in_dim(empty, key_part, kv_start * HD, 1)
    value_spread = lax.dynamic_update_slice_in_dim(empty, value_part, kv_start * HD, 1)
    key_total, value_total = (
        lax.psum_scatter(key_spread, "exp", scatter_dimension=0, tiled=True),
        lax.psum_scatter(value_spread, "exp", scatter_dimension=0, tiled=True),
    )
    return (
        residual_grad,
        query_grad,
        key_total.astype(jnp.bfloat16),
        value_total.astype(jnp.bfloat16),
    )


def solution(mesh):
    in_specs = (
        P("ctx", "exp"),
        P("ctx", None, "exp"),
        P("ctx", None),
        P("ctx", None),
        P("ctx", "exp"),
        P("ctx", None),
        P("ctx", None),
        P("exp", None),
    )
    out_specs = (P("ctx", "exp"), P("ctx", "exp"), P(("ctx", "exp"), None), P(("ctx", "exp"), None))
    return jax.shard_map(body, mesh=mesh, in_specs=in_specs, out_specs=out_specs, check_vma=False)
```

profile of v0, /device:TPU:16, one launch (start us, length us, event | category | flops | bytes accessed | tf_op | source)
XLA Modules:
  0.0 676.8 jit_solution(13157866912537187070)
XLA Ops:
  7.2 1.3 copy.62
  8.5 0.5 broadcast.316
  9.0 1.4 reduce.5
  10.4 0.7 reshape.289
  11.1 20.0 %all-to-all-start = ((bf16[16,2,2048]{2,1,0:T(2,128)(2,1)}), bf16[16,2,2048]{2,1,0:T(2,128)(2,1)S(1)}, u32[]{:S(2)}, u32[]{:S(2)}) async-start(bf16[16,2,2048]{2,1,0:T(2,128)(2,1)} %reshape.289), calls=%async_computation | async-start | bytes 262144 | tf_op jit(solution)/shard_map/all_to_all | solution.py:35
  31.1 0.7 broadcast_multiply_fusion
  31.8 0.8 copy.44
  33.1 0.6 reduce-window.6
  34.2 0.7 compare_and_fusion
  35.1 0.8 copy.43
  35.9 7.2 %all-to-all-done = bf16[16,2,2048]{2,1,0:T(2,128)(2,1)S(1)} async-done(((bf16[16,2,2048]{2,1,0:T(2,128)(2,1)}), bf16[16,2,2048]{2,1,0:T(2,128)(2,1)S(1)}, u32[]{:S(2)}, u32[]{:S(2)}) %all-to-all-start) | async-done | bytes 131104 | tf_op jit(solution)/shard_map/all_to_all | solution.py:35
  43.2 0.9 gather_fusion
  44.5 0.6 add_convert_fusion
  45.2 0.8 constant_dynamic-slice_fusion.1
  46.0 0.8 constant_dynamic-slice_fusion
  46.8 49.1 %all_gather.9 = bf16[2048,128]{1,0:T(8,128)(2,1)S(1)} all-gather(bf16[128,128]{1,0:T(8,128)(2,1)S(1)} %constant_dynamic-slice_fusion.1), channel_id=1, replica_groups=mesh['ctx'=16,'exp'=64] {'ctx'}, dimensions={0}, use_global_device_ids=true | all-gather | bytes 557056 | tf_op jit(solution)/shard_map/all_gather | solution.py:59
  95.8 0.4 fusion.38
  96.3 1.0 copy-done.1
  97.3 0.4 fusion.14
  97.7 50.2 %all_gather.10 = bf16[2048,128]{1,0:T(8,128)(2,1)S(1)} all-gather(bf16[128,128]{1,0:T(8,128)(2,1)S(1)} %constant_dynamic-slice_fusion), channel_id=1, replica_groups=mesh['ctx'=16,'exp'=64] {'ctx'}, dimensions={0}, use_global_device_ids=true | all-gather | bytes 557056 | tf_op jit(solution)/shard_map/all_gather | solution.py:60
  147.9 14.9 %all-gather.2.cloned.1.call-done = bf16[128,8192]{1,0:T(8,128)(2,1)} async-done(((bf16[128,128]{1,0:T(8,128)(2,1)}), bf16[128,8192]{1,0:T(8,128)(2,1)}) %all-gather.2.cloned.1.call-update) | async-done | bytes 2097168 | tf_op jit(solution)/shard_map/all_gather | solution.py:51
  162.8 2.4 convolution_convert_fusion.1
  165.2 0.7 fusion.7
  165.9 0.7 fusion.11
  166.6 1.4 fusion.8
  168.3 1.1 pad_maximum_fusion
  169.5 1.3 dynamic-slice
  171.7 0.7 copy.53
  172.5 220.9 %reduce-scatter.2.cloned.1.call-done = bf16[128,256]{1,0:T(8,128)(2,1)} async-done(((bf16[2048,256]{1,0:T(8,128)(2,1)}), bf16[128,256]{1,0:T(8,128)(2,1)}) %reduce-scatter.2.cloned.1.call-update) | async-done | bytes 65552 | tf_op jit(solution)/shard_map/reduce_scatter | solution.py:103
  393.3 0.8 convert_element_type.63
  394.3 274.3 %all-reduce.4 = (bf16[128,1024]{1,0:T(8,128)(2,1)S(1)}, bf16[128,1024]{1,0:T(8,128)(2,1)}) all-reduce(f32[128,1024]{1,0:T(8,128)S(1)} %slice_dynamic-update-slice_fusion.1, f32[128,1024]{1,0:T(8,128)S(1)} %slice_dynamic-update-slice_fusion), channel_id=3, replica_groups=mesh['ctx'=16,'exp'=64] {'exp'}, use_global_device_ids=true, to_apply=%region_8.9.clone | all-reduce | flops 262144 | bytes 1572864
  668.6 1.3 dynamic-slice_convert_fusion
  (40 shorter events, 2.6 us)
Async XLA Ops:
  7.2 155.7 %copy-start = (bf16[128,8192]{1,0:T(8,128)(2,1)S(1)}, bf16[128,8192]{1,0:T(8,128)(2,1)}, u32[]{:S(2)}) copy-start(bf16[128,8192]{1,0:T(8,128)(2,1)} %param.15) | copy-start | bytes 6291460
  7.2 37.3 %copy-start.5 = (bf16[128,128]{1,0:T(8,128)(2,1)S(1)}, bf16[128,128]{1,0:T(8,128)(2,1)}, u32[]{:S(2)}) copy-start(bf16[128,128]{1,0:T(8,128)(2,1)} %param.8) | copy-start | bytes 98308
  8.5 87.4 %copy-start.4 = (bf16[128,128]{1,0:T(8,128)(2,1)S(1)}, bf16[128,128]{1,0:T(8,128)(2,1)}, u32[]{:S(2)}) copy-start(bf16[128,128]{1,0:T(8,128)(2,1)} %param.12) | copy-start | bytes 98308
  11.1 32.0 %all-to-all-start = ((bf16[16,2,2048]{2,1,0:T(2,128)(2,1)}), bf16[16,2,2048]{2,1,0:T(2,128)(2,1)S(1)}, u32[]{:S(2)}, u32[]{:S(2)}) async-start(bf16[16,2,2048]{2,1,0:T(2,128)(2,1)} %reshape.289), calls=%async_computation | async-start | bytes 262144 | tf_op jit(solution)/shard_map/all_to_all | solution.py:35
  31.1 131.8 %all-gather.2.cloned.1.call-start = ((), (), s32[]{:S(2)}) async-start(), calls=%async_computation.2 | async-start | bytes 2129920 | tf_op jit(solution)/shard_map/all_gather | solution.py:51
  45.1 348.2 %reduce-scatter.2.cloned.1.call-start = ((), (), s32[]{:S(2)}) async-start(), calls=%async_computation.3 | async-start | bytes 1114112 | tf_op jit(solution)/shard_map/reduce_scatter | solution.py:103
  96.3 1.0 copy-start.1
  147.9 18.0 %copy-start.3 = (bf16[2048,128]{1,0:T(8,128)(2,1)}, bf16[2048,128]{1,0:T(8,128)(2,1)S(1)}, u32[]{:S(2)}) copy-start(bf16[2048,128]{1,0:T(8,128)(2,1)S(1)} %all_gather.10) | copy-start | bytes 1572868
  162.8 2.4 copy-start.2
Sparse Core Ops, SparseCore 0:
  45.2 117.5 all-gather.1
  169.6 223.7 reduce-scatter.1
where the time goes:
time: 678 us; the launch traced here: 677 us
  blocking collectives  374 us (55%)
  waiting for transfers between devices  243 us (36%)
  starting transfers between devices  20.1 us (3%)
  between operations  14.9 us (2%)
  local copies, waits for them, and re-layouts  12.1 us (2%)
  other arithmetic  6.92 us (1%)
    unnamed x1, blocking collectives  274 us
    reduce_scatter x1, waiting for transfers between devices, body(): lax.psum_scatter(jnp.concatenate([key_term.reshape(lax.axis_size('ctx') *...  221 us
    all_gather x1, blocking collectives, body(): lax.all_gather(value_local, 'ctx', axis=0, tiled=True)  50.2 us
    all_gather x1, blocking collectives, body(): lax.all_gather(key_local, 'ctx', axis=0, tiled=True)  49.1 us
    all_to_all x1, starting transfers between devices, body(): lax.all_to_all(expert_rows, 'ctx', split_axis=1, concat_axis=0, tiled=True)  20 us
    all_gather x1, waiting for transfers between devices, body(): lax.all_gather(residual_grad, 'exp', axis=1, tiled=True)  14.9 us
  transfers between devices with their start and end apart: 3, of which 3 were waited for; matrix products, arithmetic and copies ran while one was open for 1% of the time, Pallas kernels for 0%

commit v1 on v0

v1 whole, which is shorter than its diff:
```python
import math

import jax
import jax.numpy as jnp
from jax import lax
from jax.experimental import pallas as pl
from jax.experimental.pallas import tpu as pltpu
from jax.sharding import Mesh
from jax.sharding import PartitionSpec as P

HD = 128
SCALE = 1.0 / math.sqrt(HD)
LOW = -1e30
AXES = ("zh", "y", "zl", "xh", "xl", "core")
SIZES = (2, 8, 4, 2, 4, 2)
CTX = ("zh", "y")
EXP = ("zl", "xh", "xl", "core")
PEERS = ("zl", "xh", "xl")
N_CTX = 16
ROWS = 128
EXPERTS = 16
CAP = 32
N_PEERS = 32
HALF = 64
KEYS = N_CTX * HALF
F32 = jnp.float32
BF16 = jnp.bfloat16
VMEM = pl.BlockSpec(memory_space=pltpu.VMEM)
PARAMS = pltpu.CompilerParams(vmem_limit_bytes=40 * 1024 * 1024)


def call(kernel, outs, *operands):
    return pl.pallas_call(
        kernel,
        out_shape=[jax.ShapeDtypeStruct(shape, kind) for shape, kind in outs],
        in_specs=[VMEM] * len(operands),
        out_specs=[VMEM] * len(outs),
        compiler_params=PARAMS,
    )(*operands)


def dot(a, b, dims):
    return lax.dot_general(a, b, ((dims[:1], dims[1:]), ((), ())), preferred_element_type=F32)


def iota(shape, dim):
    return lax.broadcasted_iota(jnp.int32, shape, dim)


def key_row(number):
    xl, zl, xh, i = number // 16, (number // 4) % 4, (number // 2) % 2, number % 2
    return zl * 32 + xh * 16 + xl * 4 + lax.axis_index("core") * 2 + i


def position(block, row):
    return jnp.where(row < 64, block, 2 * N_CTX - 1 - block) * 64 + row % 64


def keys_kernel(key_ref, value_ref, out_ref):
    group = lax.axis_index("zl") * 2 + lax.axis_index("xh")
    columns = pl.ds(pl.multiple_of(group * HD, HD), HD)
    select = (iota((HALF, ROWS), 1) == key_row(iota((HALF, ROWS), 0))).astype(BF16)
    chosen = jnp.concatenate(
        [
            dot(select, key_ref[:, columns], (1, 0)),
            dot(select, value_ref[:, columns], (1, 0)),
        ],
        axis=1,
    ).astype(BF16)
    for c in range(N_CTX):
        out_ref[c] = chosen


def weight_kernel(weight_ref, query_ref, own_ref, send_ref):
    core = lax.axis_index("core")
    for b in range(N_PEERS):
        there = slice(b * HD, (b + 1) * HD)
        own_ref[:, there] = weight_ref[:, pl.ds(pl.multiple_of((2 * b + core) * HD, HD), HD)]
        send_ref[:, there] = weight_ref[:, pl.ds(pl.multiple_of((2 * b + 1 - core) * HD, HD), HD)]
    send_ref[:, N_PEERS * HD :] = query_ref[...]


def slots_kernel(index_ref, out_ref):
    index = index_ref[...]
    experts = iota((ROWS, HD), 1)
    named = [index[:, k : k + 1] == experts for k in range(2)]
    both = (named[0] | named[1]).astype(BF16)
    before = (iota((ROWS, ROWS), 1) < iota((ROWS, ROWS), 0)).astype(BF16)
    earlier = dot(before, both, (1, 0))
    for k in range(2):
        slot = jnp.sum(jnp.where(named[k], earlier, 0.0), axis=1, keepdims=True).astype(jnp.int32)
        place = index[:, k : k + 1] * CAP + slot
        wide = iota((ROWS, EXPERTS * CAP), 1) == place
        out_ref[k * ROWS : (k + 1) * ROWS] = wide.astype(BF16)


def residual_kernel(grad_ref, rows_ref, onehot_ref, combine_ref, out_ref, send_ref):
    rows = rows_ref[...].reshape(EXPERTS * CAP, HD)
    picked = dot(onehot_ref[...], rows, (1, 0))
    combine = combine_ref[...]
    moe = combine[:, 0:1] * picked[:ROWS] + combine[:, 1:2] * picked[ROWS:]
    residual = (grad_ref[...].astype(F32) + moe).astype(BF16)
    out_ref[...] = residual
    for b in range(N_PEERS):
        send_ref[b] = residual


def forward_kernel(query_ref, mate_ref, kv_ref, probs_ref, stat_ref):
    block = lax.axis_index("zh") * 8 + lax.axis_index("y")
    query = jnp.concatenate([query_ref[...], mate_ref[:, N_PEERS * HD :]], axis=0)
    kv = kv_ref[...].reshape(KEYS, 2 * HD)
    row = iota((2 * ROWS, 1), 0) % ROWS
    number = iota((1, KEYS), 1)
    allowed = position(number // HALF, key_row(number % HALF)) <= position(block, row)
    scores = jnp.where(allowed, dot(query, kv[:, :HD], (1, 1)) * SCALE, LOW)
    top = jnp.max(scores, axis=1, keepdims=True)
    probs = jnp.where(allowed, jnp.exp(scores - top), 0.0)
    total = jnp.sum(probs, axis=1, keepdims=True)
    probs_ref[...] = probs
    stat_ref[:, :HD] = dot(probs.astype(BF16), kv[:, HD:], (1, 0))
    stat_ref[:, HD:] = jnp.where(iota((2 * ROWS, HD), 1) < HALF, top, total)


def project_kernel(blocks_ref, own_ref, mate_ref, out_ref):
    total = [jnp.zeros((ROWS, HD), F32)] * 2
    for a in range(0, N_PEERS, 8):
        part = jnp.concatenate([blocks_ref[b] for b in range(a, a + 8)], axis=1)
        there = slice(a * HD, (a + 8) * HD)
        total = [
            total[0] + dot(part, own_ref[:, there], (1, 1)),
            total[1] + dot(part, mate_ref[:, there], (1, 1)),
        ]
    out_ref[:, :HD] = total[0]
    out_ref[:, HD:] = total[1]


def backward_kernel(
    part_ref, other_ref, query_ref, mate_ref, kv_ref, probs_ref, stat_ref, seen_ref,
    kv_grad_ref, own_ref, send_ref,
):
    grad = jnp.concatenate(
        [
            part_ref[:, :HD] + other_ref[:, HD:],
            part_ref[:, HD:] + other_ref[:, :HD],
        ],
        axis=0,
    ).astype(BF16)
    query = jnp.concatenate([query_ref[...], mate_ref[:, N_PEERS * HD :]], axis=0)
    kv = kv_ref[...].reshape(KEYS, 2 * HD)
    mine = stat_ref[...]
    seen = jnp.concatenate([seen_ref[ROWS:], seen_ref[:ROWS]], axis=0)
    top_mine, top_seen = mine[:, HD : HD + 1], seen[:, HD : HD + 1]
    top = jnp.maximum(top_mine, top_seen)
    mine_gain, seen_gain = jnp.exp(top_mine - top), jnp.exp(top_seen - top)
    total = mine[:, HD + HALF : HD + HALF + 1] * mine_gain + seen[:, HD + HALF : HD + HALF + 1] * seen_gain
    mine_gain, seen_gain = mine_gain / total, seen_gain / total
    head_out = mine[:, :HD] * mine_gain + seen[:, :HD] * seen_gain
    delta = jnp.sum(grad.astype(F32) * head_out, axis=1, keepdims=True)
    probs = probs_ref[...] * mine_gain
    score_grad = (probs * (dot(grad, kv[:, HD:], (1, 1)) - delta)).astype(BF16)
    kv_grad_ref[:, :, :HD] = (dot(score_grad, query, (0, 0)) * SCALE).astype(BF16).reshape(HALF, 16, HD)
    kv_grad_ref[:, :, HD:] = dot(probs.astype(BF16), grad, (0, 0)).astype(BF16).reshape(HALF, 16, HD)
    query_grad = dot(score_grad, kv[:, :HD], (1, 0)) * SCALE
    own_ref[...] = query_grad[:ROWS]
    send_ref[...] = query_grad[ROWS:]


def sum_kernel(parts_ref, out_ref):
    out_ref[...] = jnp.sum(parts_ref[...].astype(F32), axis=0).astype(BF16)


def swap(array):
    return lax.ppermute(array, "core", [(0, 1), (1, 0)])


def body(out_grad, expert_rows, expert_index, combine, head_query, head_key, head_value, out_weight):
    received = lax.all_to_all(
        expert_rows.reshape(N_CTX, CAP, HD), CTX, split_axis=0, concat_axis=0, tiled=True
    )
    (kv_send,) = call(keys_kernel, [((N_CTX, HALF, 2 * HD), BF16)], head_key, head_value)
    kv_all = lax.all_to_all(kv_send, CTX, split_axis=0, concat_axis=0, tiled=True)
    own_weight, send_weight = call(
        weight_kernel,
        [((ROWS, N_PEERS * HD), BF16), ((ROWS, (N_PEERS + 1) * HD), BF16)],
        out_weight,
        head_query,
    )
    mate = swap(send_weight)
    (onehot,) = call(slots_kernel, [((2 * ROWS, EXPERTS * CAP), BF16)], expert_index)
    residual_grad, residual_send = call(
        residual_kernel,
        [((ROWS, HD), BF16), ((N_PEERS, ROWS, HD), BF16)],
        out_grad,
        received,
        onehot,
        combine,
    )
    blocks = lax.all_to_all(residual_send, PEERS, split_axis=0, concat_axis=0, tiled=True)
    probs, stat = call(
        forward_kernel,
        [((2 * ROWS, KEYS), F32), ((2 * ROWS, 2 * HD), F32)],
        head_query,
        mate,
        kv_all,
    )
    seen = swap(stat)
    (part,) = call(project_kernel, [((ROWS, 2 * HD), F32)], blocks, own_weight, mate)
    other = swap(part)
    kv_grad, own_grad, send_grad = call(
        backward_kernel,
        [((HALF, 16, 2 * HD), BF16), ((ROWS, HD), F32), ((ROWS, HD), F32)],
        part,
        other,
        head_query,
        mate,
        kv_all,
        probs,
        stat,
        seen,
    )
    kv_parts = lax.all_to_all(kv_grad, ("zh", "y", "xl"), split_axis=0, concat_axis=0, tiled=True)
    query_grad = (own_grad + swap(send_grad)).astype(BF16)
    (kv_sum,) = call(sum_kernel, [((16, 2 * HD), BF16)], kv_parts)
    final = lax.all_to_all(
        kv_sum.reshape(8, 2, 2 * HD), ("zl", "xh"), split_axis=0, concat_axis=0, tiled=True
    )
    final = jnp.transpose(final, (1, 0, 2))
    key_grad = final[:, :, :HD].reshape(2, 8 * HD)
    value_grad = final[:, :, HD:].reshape(2, 8 * HD)
    return residual_grad, query_grad, key_grad, value_grad


def solution(mesh):
    fine = Mesh(mesh.devices.reshape(SIZES), AXES)
    in_specs = (
        P(CTX, EXP),
        P(CTX, None, EXP),
        P(CTX, None),
        P(CTX, None),
        P(CTX, EXP),
        P(CTX, None),
        P(CTX, None),
        P(EXP, None),
    )
    out_specs = (P(CTX, EXP), P(CTX, EXP), P(CTX + EXP, None), P(CTX + EXP, None))
    return jax.shard_map(body, mesh=fine, in_specs=in_specs, out_specs=out_specs, check_vma=False)
```

time: 678 us -> 149 us (0.22)
  blocking collectives: 374 us -> 0 us
  waiting for transfers between devices: 243 us -> 73.4 us
  starting transfers between devices: 20.1 us -> 58.9 us
  between operations: 14.9 us -> 0.78 us
    unnamed x1 -> x0, blocking collectives: 274 us -> none
    reduce_scatter x1 -> x0, waiting for transfers between devices: 221 us -> none  [body(): lax.psum_scatter(jnp.concatenate([key_term.reshape(lax.axis_size('ctx') *...]
    all_gather x2 -> x0, blocking collectives: 99.3 us -> none  [the longest x1 50.2 us: body(): lax.all_gather(value_local, 'ctx', axis=0, tiled=True)]
    all_to_all x1 -> x5, waiting for transfers between devices: 7.19 us -> 69.4 us  [the longest x1 20.7 us: body(): lax.all_to_all(kv_grad, ('zh', 'y', 'xl'), split_axis=0, concat_axis=0, t...]
    all_to_all x1 -> x5, starting transfers between devices: 20 us -> 51.1 us  [the longest x1 20 us: body(): lax.all_to_all(expert_rows.reshape(N_CTX, CAP, HD), CTX, split_axis=0, co...]
    all_gather x1 -> x0, waiting for transfers between devices: 14.9 us -> none  [body(): lax.all_gather(residual_grad, 'exp', axis=1, tiled=True)]
    ppermute x0 -> x4, starting transfers between devices: none -> 7.78 us  [swap(): return lax.ppermute(array, 'core', [(0, 1), (1, 0)])]
  transfers between devices with their start and end apart: 3 -> 9, of which waited for: 3 -> 7; matrix products, arithmetic and copies ran while one was open for 1% -> 1% of each run, Pallas kernels for 0% -> 3%
where the time goes in v1:
time: 149 us; the launch traced here: 148 us
  waiting for transfers between devices  73.4 us (49%)
  starting transfers between devices  58.9 us (40%)
  local copies, waits for them, and re-layouts  8.08 us (5%)
  Pallas kernels  6.52 us (4%)
    all_to_all x1, waiting for transfers between devices, body(): lax.all_to_all(kv_grad, ('zh', 'y', 'xl'), split_axis=0, concat_axis=0, t...  20.7 us
    all_to_all x1, starting transfers between devices, body(): lax.all_to_all(expert_rows.reshape(N_CTX, CAP, HD), CTX, split_axis=0, co...  20 us
    all_to_all x1, waiting for transfers between devices, body(): lax.all_to_all(kv_send, CTX, split_axis=0, concat_axis=0, tiled=True)  15.8 us
    all_to_all x1, waiting for transfers between devices, body(): lax.all_to_all(residual_send, PEERS, split_axis=0, concat_axis=0, tiled=T...  14 us
    all_to_all x1, starting transfers between devices, body(): lax.all_to_all(residual_send, PEERS, split_axis=0, concat_axis=0, tiled=T...  12.5 us
    all_to_all x1, waiting for transfers between devices, body(): lax.all_to_all(kv_sum.reshape(8, 2, 2 * HD), ('zl', 'xh'), split_axis=0,...  9.78 us
    all_to_all x1, starting transfers between devices, body(): lax.all_to_all(kv_grad, ('zh', 'y', 'xl'), split_axis=0, concat_axis=0, t...  9.27 us
    all_to_all x1, waiting for transfers between devices, body(): lax.all_to_all(expert_rows.reshape(N_CTX, CAP, HD), CTX, split_axis=0, co...  9.13 us
  transfers between devices with their start and end apart: 9, of which 7 were waited for; matrix products, arithmetic and copies ran while one was open for 1% of the time, Pallas kernels for 3%

profile of v1, /device:TPU:16, one launch (start us, length us, event | category | flops | bytes accessed | tf_op | source)
XLA Modules:
  0.0 148.3 jit_solution(12779028483171768231)
XLA Ops:
  0.6 20.0 %all-to-all-start = ((bf16[16,32,128]{2,1,0:T(8,128)(2,1)}), bf16[16,32,128]{2,1,0:T(8,128)(2,1)S(1)}, u32[]{:S(2)}, u32[]{:S(2)}) async-start(bf16[16,32,128]{2,1,0:T(8,128)(2,1)} %bitcast.6), calls=%async_computation | async-start | bytes 262144 | tf_op jit(solution)/shard_map/all_to_all | solution.py:177
  20.6 0.9 copy-done.6
  21.6 0.9 copy-done.7
  22.5 1.0 shard_map.115
  23.5 9.1 %all-to-all-done.rows_ref = bf16[16,32,128]{2,1,0:T(8,128)(2,1)S(1)} async-done(((bf16[16,32,128]{2,1,0:T(8,128)(2,1)}), bf16[16,32,128]{2,1,0:T(8,128)(2,1)S(1)}, u32[]{:S(2)}, u32[]{:S(2)}) %all-to-all-start) | async-done | bytes 131104 | tf_op jit(solution)/shard_map/all_to_all | solution.py:177
  32.7 3.9 %all-to-all-start.2 = ((bf16[16,64,256]{2,1,0:T(8,128)(2,1)}), bf16[16,64,256]{2,1,0:T(8,128)(2,1)S(1)}, u32[]{:S(2)}, u32[]{:S(2)}) async-start(bf16[16,64,256]{2,1,0:T(8,128)(2,1)} %shard_map.115), calls=%async_computation.2 | async-start | bytes 1048576 | tf_op jit(solution)/shard_map/all_to_all | solution.py:181
  36.7 0.4 shard_map.111.onehot_ref
  37.3 1.3 shard_map.112
  38.6 15.8 %all-to-all-done.2.kv_ref = bf16[16,64,256]{2,1,0:T(8,128)(2,1)S(1)} async-done(((bf16[16,64,256]{2,1,0:T(8,128)(2,1)}), bf16[16,64,256]{2,1,0:T(8,128)(2,1)S(1)}, u32[]{:S(2)}, u32[]{:S(2)}) %all-to-all-start.2) | async-done | bytes 524320 | tf_op jit(solution)/shard_map/all_to_all | solution.py:181
  54.3 12.5 %all-to-all-start.1 = ((bf16[32,128,128]{2,1,0:T(8,128)(2,1)}), bf16[32,128,128]{2,1,0:T(8,128)(2,1)S(1)}, u32[]{:S(2)}, u32[]{:S(2)}) async-start(bf16[32,128,128]{2,1,0:T(8,128)(2,1)} %get-tuple-element.14), calls=%async_computation.1 | async-start | bytes 2097152 | tf_op jit(solution)/shard_map/all_to_all | solution.py:198
  66.8 1.6 %copy-done = bf16[128,8192]{1,0:T(8,128)(2,1)S(1)} copy-done((bf16[128,8192]{1,0:T(8,128)(2,1)S(1)}, bf16[128,8192]{1,0:T(8,128)(2,1)}, u32[]{:S(2)}) %copy-start) | copy-done | bytes 2097176
  68.4 0.5 shard_map.113
  69.0 0.9 copy-done.1
  69.9 1.9 %collective-permute-start = (bf16[128,4224]{1,0:T(8,128)(2,1)S(1)}, bf16[128,4224]{1,0:T(8,128)(2,1)S(1)}, u32[]{:S(2)}, u32[]{:S(2)}) collective-permute-start(bf16[128,4224]{1,0:T(8,128)(2,1)S(1)} %get-tuple-element.16), channel_id=1, source_target_pairs={{0,1},{1,0},{2,3},{3,2},{4,5},{5,4},{6,7},{7,6},{8,9},{9,8},{10,11... | collective-permute-start | bytes 3244040 | tf_op jit(solution)/shard_map/ppermute | solution.py:173
  71.9 2.7 %collective-permute-done.mate_ref = bf16[128,4224]{1,0:T(8,128)(2,1)S(1)} collective-permute-done((bf16[128,4224]{1,0:T(8,128)(2,1)S(1)}, bf16[128,4224]{1,0:T(8,128)(2,1)S(1)}, u32[]{:S(2)}, u32[]{:S(2)}) %collective-permute-start) | collective-permute-done | bytes 1081376 | tf_op jit(solution)/shard_map/ppermute | solution.py:173
  74.5 0.8 shard_map.116
  75.3 1.0 copy-done.3
  76.3 2.0 %collective-permute-start.2 = (f32[256,256]{1,0:T(8,128)S(1)}, f32[256,256]{1,0:T(8,128)S(1)}, u32[]{:S(2)}, u32[]{:S(2)}) collective-permute-start(f32[256,256]{1,0:T(8,128)S(1)} %get-tuple-element.18.stat_ref), channel_id=1, source_target_pairs={{0,1},{1,0},{2,3},{3,2},{4,5},{5,4},{6,7},{7,6},{8,9},{9,8},{10,11... | collective-permute-start | bytes 786440 | tf_op jit(solution)/shard_map/ppermute | solution.py:173
  78.3 14.0 %all-to-all-done.1.blocks_ref = bf16[32,128,128]{2,1,0:T(8,128)(2,1)S(1)} async-done(((bf16[32,128,128]{2,1,0:T(8,128)(2,1)}), bf16[32,128,128]{2,1,0:T(8,128)(2,1)S(1)}, u32[]{:S(2)}, u32[]{:S(2)}) %all-to-all-start.1) | async-done | bytes 1048608 | tf_op jit(solution)/shard_map/all_to_all | solution.py:198
  92.4 1.2 copy-done.2
  93.6 0.7 shard_map.114.part_ref
  94.3 1.9 %collective-permute-start.1 = (f32[128,256]{1,0:T(8,128)S(1)}, f32[128,256]{1,0:T(8,128)S(1)}, u32[]{:S(2)}, u32[]{:S(2)}) collective-permute-start(f32[128,256]{1,0:T(8,128)S(1)} %shard_map.114.part_ref), channel_id=1, source_target_pairs={{0,1},{1,0},{2,3},{3,2},{4,5},{5,4},{6,7},{7,6},{8,9},{9,8},{10,11... | collective-permute-start | bytes 393224 | tf_op jit(solution)/shard_map/ppermute | solution.py:173
  96.2 1.3 collective-permute-done.1.other_ref
  97.5 1.7 %shard_map.117 = (bf16[64,16,256]{2,1,0:T(8,128)(2,1)}, f32[128,128]{1,0:T(8,128)S(1)}, f32[128,128]{1,0:T(8,128)S(1)}) custom-call(f32[128,256]{1,0:T(8,128)S(1)} %shard_map.114.part_ref, f32[128,256]{1,0:T(8,128)S(1)} %collective-permute-done.1.other_ref, bf16[128,128]{1,0:T(8,128)(2,1)S(1)} %copy-done.5, ...), custom_call_target="tpu_custom_call" | custom-call | tf_op jit(solution)/shard_map/pallas_call | solution.py:33
  99.2 9.3 %all-to-all-start.3 = ((bf16[64,16,256]{2,1,0:T(8,128)(2,1)}), bf16[64,16,256]{2,1,0:T(8,128)(2,1)S(1)}, u32[]{:S(2)}, u32[]{:S(2)}) async-start(bf16[64,16,256]{2,1,0:T(8,128)(2,1)} %get-tuple-element.21), calls=%async_computation.3 | async-start | bytes 1048576 | tf_op jit(solution)/shard_map/all_to_all | solution.py:221
  108.5 1.9 %collective-permute-start.3 = (f32[128,128]{1,0:T(8,128)S(1)}, f32[128,128]{1,0:T(8,128)S(1)}, u32[]{:S(2)}, u32[]{:S(2)}) collective-permute-start(f32[128,128]{1,0:T(8,128)S(1)} %get-tuple-element.20), channel_id=1, source_target_pairs={{0,1},{1,0},{2,3},{3,2},{4,5},{5,4},{6,7},{7,6},{8,9},{9,8},{10,11... | collective-permute-start | bytes 196616 | tf_op jit(solution)/shard_map/ppermute | solution.py:173
  110.4 20.7 %all-to-all-done.3.parts_ref = bf16[64,16,256]{2,1,0:T(8,128)(2,1)S(1)} async-done(((bf16[64,16,256]{2,1,0:T(8,128)(2,1)}), bf16[64,16,256]{2,1,0:T(8,128)(2,1)S(1)}, u32[]{:S(2)}, u32[]{:S(2)}) %all-to-all-start.3) | async-done | bytes 524320 | tf_op jit(solution)/shard_map/all_to_all | solution.py:221
  131.2 0.6 reshape.21
  131.8 5.4 %all-to-all-start.4 = ((bf16[8,2,256]{2,1,0:T(2,128)(2,1)}), bf16[8,2,256]{2,1,0:T(2,128)(2,1)S(1)}, u32[]{:S(2)}, u32[]{:S(2)}) async-start(bf16[8,2,256]{2,1,0:T(2,128)(2,1)} %reshape.21), calls=%async_computation.4 | async-start | bytes 16384 | tf_op jit(solution)/shard_map/all_to_all | solution.py:224
  137.3 0.6 add_convert_fusion
  137.9 9.8 %all-to-all-done.4 = bf16[8,2,256]{2,1,0:T(2,128)(2,1)S(1)} async-done(((bf16[8,2,256]{2,1,0:T(2,128)(2,1)}), bf16[8,2,256]{2,1,0:T(2,128)(2,1)S(1)}, u32[]{:S(2)}, u32[]{:S(2)}) %all-to-all-start.4) | async-done | bytes 8224 | tf_op jit(solution)/shard_map/all_to_all | solution.py:224
  147.7 0.6 slice_bitcast_fusion
  (21 shorter events, 0.4 us)
Async XLA Ops:
  0.6 32.0 %all-to-all-start = ((bf16[16,32,128]{2,1,0:T(8,128)(2,1)}), bf16[16,32,128]{2,1,0:T(8,128)(2,1)S(1)}, u32[]{:S(2)}, u32[]{:S(2)}) async-start(bf16[16,32,128]{2,1,0:T(8,128)(2,1)} %bitcast.6), calls=%async_computation | async-start | bytes 262144 | tf_op jit(solution)/shard_map/all_to_all | solution.py:177
  20.6 0.9 copy-start.6
  21.6 0.9 copy-start.7
  22.5 14.1 %copy-start.9 = (s32[128,2]{0,1:T(2,128)S(1)}, s32[128,2]{0,1:T(2,128)}, u32[]{:S(2)}) copy-start(s32[128,2]{0,1:T(2,128)} %param.10) | copy-start | bytes 3076
  22.5 14.6 %copy-start.10 = (f32[128,2]{0,1:T(2,128)S(1)}, f32[128,2]{0,1:T(2,128)}, u32[]{:S(2)}) copy-start(f32[128,2]{0,1:T(2,128)} %param.11) | copy-start | bytes 3076
  22.5 14.7 %copy-start.8 = (bf16[128,128]{1,0:T(8,128)(2,1)S(1)}, bf16[128,128]{1,0:T(8,128)(2,1)}, u32[]{:S(2)}) copy-start(bf16[128,128]{1,0:T(8,128)(2,1)} %grad_ref.1) | copy-start | bytes 98308
  32.7 21.7 %all-to-all-start.2 = ((bf16[16,64,256]{2,1,0:T(8,128)(2,1)}), bf16[16,64,256]{2,1,0:T(8,128)(2,1)S(1)}, u32[]{:S(2)}, u32[]{:S(2)}) async-start(bf16[16,64,256]{2,1,0:T(8,128)(2,1)} %shard_map.115), calls=%async_computation.2 | async-start | bytes 1048576 | tf_op jit(solution)/shard_map/all_to_all | solution.py:181
  38.6 28.3 %copy-start.5 = (bf16[128,128]{1,0:T(8,128)(2,1)S(1)}, bf16[128,128]{1,0:T(8,128)(2,1)}, u32[]{:S(2)}) copy-start(bf16[128,128]{1,0:T(8,128)(2,1)} %query_ref.5) | copy-start | bytes 98308
  54.3 38.0 %all-to-all-start.1 = ((bf16[32,128,128]{2,1,0:T(8,128)(2,1)}), bf16[32,128,128]{2,1,0:T(8,128)(2,1)S(1)}, u32[]{:S(2)}, u32[]{:S(2)}) async-start(bf16[32,128,128]{2,1,0:T(8,128)(2,1)} %get-tuple-element.14), calls=%async_computation.1 | async-start | bytes 2097152 | tf_op jit(solution)/shard_map/all_to_all | solution.py:198
  66.8 1.6 %copy-start = (bf16[128,8192]{1,0:T(8,128)(2,1)S(1)}, bf16[128,8192]{1,0:T(8,128)(2,1)}, u32[]{:S(2)}) copy-start(bf16[128,8192]{1,0:T(8,128)(2,1)} %weight_ref.1) | copy-start | bytes 6291460
  69.0 1.0 copy-start.1
  69.9 4.6 %collective-permute-start = (bf16[128,4224]{1,0:T(8,128)(2,1)S(1)}, bf16[128,4224]{1,0:T(8,128)(2,1)S(1)}, u32[]{:S(2)}, u32[]{:S(2)}) collective-permute-start(bf16[128,4224]{1,0:T(8,128)(2,1)S(1)} %get-tuple-element.16), channel_id=1, source_target_pairs={{0,1},{1,0},{2,3},{3,2},{4,5},{5,4},{6,7},{7,6},{8,9},{9,8},{10,11... | collective-permute-start | bytes 3244040 | tf_op jit(solution)/shard_map/ppermute | solution.py:173
  75.3 1.0 copy-start.3
  76.3 19.9 %collective-permute-start.2 = (f32[256,256]{1,0:T(8,128)S(1)}, f32[256,256]{1,0:T(8,128)S(1)}, u32[]{:S(2)}, u32[]{:S(2)}) collective-permute-start(f32[256,256]{1,0:T(8,128)S(1)} %get-tuple-element.18.stat_ref), channel_id=1, source_target_pairs={{0,1},{1,0},{2,3},{3,2},{4,5},{5,4},{6,7},{7,6},{8,9},{9,8},{10,11... | collective-permute-start | bytes 786440 | tf_op jit(solution)/shard_map/ppermute | solution.py:173
  92.3 1.2 copy-start.2
  93.6 3.9 %copy-start.4 = (f32[256,1024]{1,0:T(8,128)S(1)}, f32[256,1024]{1,0:T(8,128)}, u32[]{:S(2)}) copy-start(f32[256,1024]{1,0:T(8,128)} %copy-done.3) | copy-start | bytes 3145732
  94.3 3.2 %collective-permute-start.1 = (f32[128,256]{1,0:T(8,128)S(1)}, f32[128,256]{1,0:T(8,128)S(1)}, u32[]{:S(2)}, u32[]{:S(2)}) collective-permute-start(f32[128,256]{1,0:T(8,128)S(1)} %shard_map.114.part_ref), channel_id=1, source_target_pairs={{0,1},{1,0},{2,3},{3,2},{4,5},{5,4},{6,7},{7,6},{8,9},{9,8},{10,11... | collective-permute-start | bytes 393224 | tf_op jit(solution)/shard_map/ppermute | solution.py:173
  99.2 31.9 %all-to-all-start.3 = ((bf16[64,16,256]{2,1,0:T(8,128)(2,1)}), bf16[64,16,256]{2,1,0:T(8,128)(2,1)S(1)}, u32[]{:S(2)}, u32[]{:S(2)}) async-start(bf16[64,16,256]{2,1,0:T(8,128)(2,1)} %get-tuple-element.21), calls=%async_computation.3 | async-start | bytes 1048576 | tf_op jit(solution)/shard_map/all_to_all | solution.py:221
  108.5 28.8 %collective-permute-start.3 = (f32[128,128]{1,0:T(8,128)S(1)}, f32[128,128]{1,0:T(8,128)S(1)}, u32[]{:S(2)}, u32[]{:S(2)}) collective-permute-start(f32[128,128]{1,0:T(8,128)S(1)} %get-tuple-element.20), channel_id=1, source_target_pairs={{0,1},{1,0},{2,3},{3,2},{4,5},{5,4},{6,7},{7,6},{8,9},{9,8},{10,11... | collective-permute-start | bytes 196616 | tf_op jit(solution)/shard_map/ppermute | solution.py:173
  131.8 15.9 %all-to-all-start.4 = ((bf16[8,2,256]{2,1,0:T(2,128)(2,1)}), bf16[8,2,256]{2,1,0:T(2,128)(2,1)S(1)}, u32[]{:S(2)}, u32[]{:S(2)}) async-start(bf16[8,2,256]{2,1,0:T(2,128)(2,1)} %reshape.21), calls=%async_computation.4 | async-start | bytes 16384 | tf_op jit(solution)/shard_map/all_to_all | solution.py:224

commit v2 on v1

--- a/solution.py
+++ b/solution.py
@@ -23,10 +23,11 @@
 N_PEERS = 32
 HALF = 64
 KEYS = N_CTX * HALF
+PACK = CAP + 2 * HALF
 F32 = jnp.float32
 BF16 = jnp.bfloat16
 VMEM = pl.BlockSpec(memory_space=pltpu.VMEM)
-PARAMS = pltpu.CompilerParams(vmem_limit_bytes=40 * 1024 * 1024)
+PARAMS = pltpu.CompilerParams(vmem_limit_bytes=16 * 1024 * 1024)
 
 
 def call(kernel, outs, *operands):
@@ -56,19 +57,31 @@
     return jnp.where(row < 64, block, 2 * N_CTX - 1 - block) * 64 + row % 64
 
 
-def keys_kernel(key_ref, value_ref, out_ref):
+def received_kv(pack_ref):
+    return (
+        pack_ref[:, CAP : CAP + HALF].reshape(KEYS, HD),
+        pack_ref[:, CAP + HALF :].reshape(KEYS, HD),
+    )
+
+
+def pack_kernel(rows_ref, key_ref, value_ref, out_ref, key_own, value_own, sems):
     group = lax.axis_index("zl") * 2 + lax.axis_index("xh")
     columns = pl.ds(pl.multiple_of(group * HD, HD), HD)
+    copies = [
+        pltpu.make_async_copy(key_ref.at[:, columns], key_own, sems.at[0]),
+        pltpu.make_async_copy(value_ref.at[:, columns], value_own, sems.at[1]),
+    ]
+    for copy in copies:
+        copy.start()
+    out_ref[:, :CAP] = rows_ref[...]
     select = (iota((HALF, ROWS), 1) == key_row(iota((HALF, ROWS), 0))).astype(BF16)
-    chosen = jnp.concatenate(
-        [
-            dot(select, key_ref[:, columns], (1, 0)),
-            dot(select, value_ref[:, columns], (1, 0)),
-        ],
-        axis=1,
-    ).astype(BF16)
+    for copy in copies:
+        copy.wait()
+    keys = dot(select, key_own[...], (1, 0)).astype(BF16)
+    values = dot(select, value_own[...], (1, 0)).astype(BF16)
     for c in range(N_CTX):
-        out_ref[c] = chosen
+        out_ref[c, CAP : CAP + HALF] = keys
+        out_ref[c, CAP + HALF :] = values
 
 
 def weight_kernel(weight_ref, query_ref, own_ref, send_ref):
@@ -94,8 +107,8 @@
         out_ref[k * ROWS : (k + 1) * ROWS] = wide.astype(BF16)
 
 
-def residual_kernel(grad_ref, rows_ref, onehot_ref, combine_ref, out_ref, send_ref):
-    rows = rows_ref[...].reshape(EXPERTS * CAP, HD)
+def residual_kernel(grad_ref, pack_ref, onehot_ref, combine_ref, out_ref, send_ref):
+    rows = pack_ref[:, :CAP].reshape(EXPERTS * CAP, HD)
     picked = dot(onehot_ref[...], rows, (1, 0))
     combine = combine_ref[...]
     moe = combine[:, 0:1] * picked[:ROWS] + combine[:, 1:2] * picked[ROWS:]
@@ -105,19 +118,19 @@
         send_ref[b] = residual
 
 
-def forward_kernel(query_ref, mate_ref, kv_ref, probs_ref, stat_ref):
+def forward_kernel(query_ref, mate_ref, pack_ref, probs_ref, stat_ref):
     block = lax.axis_index("zh") * 8 + lax.axis_index("y")
     query = jnp.concatenate([query_ref[...], mate_ref[:, N_PEERS * HD :]], axis=0)
-    kv = kv_ref[...].reshape(KEYS, 2 * HD)
+    keys, values = received_kv(pack_ref)
     row = iota((2 * ROWS, 1), 0) % ROWS
     number = iota((1, KEYS), 1)
     allowed = position(number // HALF, key_row(number % HALF)) <= position(block, row)
-    scores = jnp.where(allowed, dot(query, kv[:, :HD], (1, 1)) * SCALE, LOW)
+    scores = jnp.where(allowed, dot(query, keys, (1, 1)) * SCALE, LOW)
     top = jnp.max(scores, axis=1, keepdims=True)
     probs = jnp.where(allowed, jnp.exp(scores - top), 0.0)
     total = jnp.sum(probs, axis=1, keepdims=True)
     probs_ref[...] = probs
-    stat_ref[:, :HD] = dot(probs.astype(BF16), kv[:, HD:], (1, 0))
+    stat_ref[:, :HD] = dot(probs.astype(BF16), values, (1, 0))
     stat_ref[:, HD:] = jnp.where(iota((2 * ROWS, HD), 1) < HALF, top, total)
 
 
@@ -135,7 +148,7 @@
 
 
 def backward_kernel(
-    part_ref, other_ref, query_ref, mate_ref, kv_ref, probs_ref, stat_ref, seen_ref,
+    part_ref, other_ref, query_ref, mate_ref, pack_ref, probs_ref, stat_ref, seen_ref,
     kv_grad_ref, own_ref, send_ref,
 ):
     grad = jnp.concatenate(
@@ -146,7 +159,7 @@
         axis=0,
     ).astype(BF16)
     query = jnp.concatenate([query_ref[...], mate_ref[:, N_PEERS * HD :]], axis=0)
-    kv = kv_ref[...].reshape(KEYS, 2 * HD)
+    keys, values = received_kv(pack_ref)
     mine = stat_ref[...]
     seen = jnp.concatenate([seen_ref[ROWS:], seen_ref[:ROWS]], axis=0)
     top_mine, top_seen = mine[:, HD : HD + 1], seen[:, HD : HD + 1]
@@ -157,28 +170,58 @@
     head_out = mine[:, :HD] * mine_gain + seen[:, :HD] * seen_gain
     delta = jnp.sum(grad.astype(F32) * head_out, axis=1, keepdims=True)
     probs = probs_ref[...] * mine_gain
-    score_grad = (probs * (dot(grad, kv[:, HD:], (1, 1)) - delta)).astype(BF16)
-    kv_grad_ref[:, :, :HD] = (dot(score_grad, query, (0, 0)) * SCALE).astype(BF16).reshape(HALF, 16, HD)
-    kv_grad_ref[:, :, HD:] = dot(probs.astype(BF16), grad, (0, 0)).astype(BF16).reshape(HALF, 16, HD)
-    query_grad = dot(score_grad, kv[:, :HD], (1, 0)) * SCALE
+    score_grad = (probs * (dot(grad, values, (1, 1)) - delta)).astype(BF16)
+    key_grad = (dot(score_grad, query, (0, 0)) * SCALE).astype(BF16).reshape(2, 32, 16, HD)
+    value_grad = dot(probs.astype(BF16), grad, (0, 0)).astype(BF16).reshape(2, 32, 16, HD)
+    for zh in range(2):
+        kv_grad_ref[:, zh * 16 : (zh + 1) * 16, :HD] = key_grad[zh]
+        kv_grad_ref[:, zh * 16 : (zh + 1) * 16, HD:] = value_grad[zh]
+    query_grad = dot(score_grad, keys, (1, 0)) * SCALE
     own_ref[...] = query_grad[:ROWS]
     send_ref[...] = query_grad[ROWS:]
 
 
 def sum_kernel(parts_ref, out_ref):
-    out_ref[...] = jnp.sum(parts_ref[...].astype(F32), axis=0).astype(BF16)
+    total = parts_ref[0].astype(F32)
+    for b in range(1, 32):
+        total = total + parts_ref[b].astype(F32)
+    low = total.astype(BF16)
+    row, source = iota((64, 32), 0), iota((64, 32), 1)
+    place = row // 4 * 2 + row % 2
+    pick_key = ((place == source) & (row // 2 % 2 == 0)).astype(BF16)
+    pick_value = ((place == source) & (row // 2 % 2 == 1)).astype(BF16)
+    out_ref[...] = (dot(pick_key, low[:, :HD], (1, 0)) + dot(pick_value, low[:, HD:], (1, 0))).astype(BF16)
+
+
+def last_kernel(parts_ref, key_ref, value_ref):
+    parts = parts_ref[...].astype(F32)
+    total = parts[:32] + parts[32:]
+    key_ref[...] = jnp.concatenate([total[4 * g : 4 * g + 2] for g in range(8)], axis=1).astype(BF16)
+    value_ref[...] = jnp.concatenate([total[4 * g + 2 : 4 * g + 4] for g in range(8)], axis=1).astype(BF16)
 
 
 def swap(array):
     return lax.ppermute(array, "core", [(0, 1), (1, 0)])
 
 
+def exchange(array, axes):
+    return lax.all_to_all(array, axes, split_axis=0, concat_axis=0, tiled=True)
+
+
 def body(out_grad, expert_rows, expert_index, combine, head_query, head_key, head_value, out_weight):
-    received = lax.all_to_all(
-        expert_rows.reshape(N_CTX, CAP, HD), CTX, split_axis=0, concat_axis=0, tiled=True
-    )
-    (kv_send,) = call(keys_kernel, [((N_CTX, HALF, 2 * HD), BF16)], head_key, head_value)
-    kv_all = lax.all_to_all(kv_send, CTX, split_axis=0, concat_axis=0, tiled=True)
+    packed = pl.pallas_call(
+        pack_kernel,
+        out_shape=jax.ShapeDtypeStruct((N_CTX, PACK, HD), BF16),
+        in_specs=[VMEM, pl.BlockSpec(memory_space=pl.ANY), pl.BlockSpec(memory_space=pl.ANY)],
+        out_specs=VMEM,
+        scratch_shapes=[
+            pltpu.VMEM((ROWS, HD), BF16),
+            pltpu.VMEM((ROWS, HD), BF16),
+            pltpu.SemaphoreType.DMA((2,)),
+        ],
+        compiler_params=PARAMS,
+    )(expert_rows.reshape(N_CTX, CAP, HD), head_key, head_value)
+    received = exchange(packed, CTX)
     own_weight, send_weight = call(
         weight_kernel,
         [((ROWS, N_PEERS * HD), BF16), ((ROWS, (N_PEERS + 1) * HD), BF16)],
@@ -195,38 +238,36 @@
         onehot,
         combine,
     )
-    blocks = lax.all_to_all(residual_send, PEERS, split_axis=0, concat_axis=0, tiled=True)
+    blocks = exchange(residual_send, PEERS)
     probs, stat = call(
         forward_kernel,
         [((2 * ROWS, KEYS), F32), ((2 * ROWS, 2 * HD), F32)],
         head_query,
         mate,
-        kv_all,
+        received,
     )
     seen = swap(stat)
     (part,) = call(project_kernel, [((ROWS, 2 * HD), F32)], blocks, own_weight, mate)
     other = swap(part)
     kv_grad, own_grad, send_grad = call(
         backward_kernel,
-        [((HALF, 16, 2 * HD), BF16), ((ROWS, HD), F32), ((ROWS, HD), F32)],
+        [((32, 32, 2 * HD), BF16), ((ROWS, HD), F32), ((ROWS, HD), F32)],
         part,
         other,
         head_query,
         mate,
-        kv_all,
+        received,
         probs,
         stat,
         seen,
     )
-    kv_parts = lax.all_to_all(kv_grad, ("zh", "y", "xl"), split_axis=0, concat_axis=0, tiled=True)
+    kv_parts = exchange(kv_grad, ("y", "xl"))
     query_grad = (own_grad + swap(send_grad)).astype(BF16)
-    (kv_sum,) = call(sum_kernel, [((16, 2 * HD), BF16)], kv_parts)
-    final = lax.all_to_all(
-        kv_sum.reshape(8, 2, 2 * HD), ("zl", "xh"), split_axis=0, concat_axis=0, tiled=True
-    )
-    final = jnp.transpose(final, (1, 0, 2))
-    key_grad = final[:, :, :HD].reshape(2, 8 * HD)
-    value_grad = final[:, :, HD:].reshape(2, 8 * HD)
+    (kv_sum,) = call(sum_kernel, [((64, HD), BF16)], kv_parts)
+    final = exchange(kv_sum.reshape(16, 4, HD), ("zh", "zl", "xh"))
+    key_grad, value_grad = call(
+        last_kernel, [((2, 8 * HD), BF16), ((2, 8 * HD), BF16)], final.reshape(64, HD)
+    )
     return residual_grad, query_grad, key_grad, value_grad
 
 

time: 149 us -> 139 us (0.933)
  starting transfers between devices: 58.9 us -> 52.9 us
  waiting for transfers between devices: 73.4 us -> 68.5 us
    all_to_all x5 -> x4, starting transfers between devices: 51.1 us -> 45.2 us  [exchange(): return lax.all_to_all(array, axes, split_axis=0, concat_axis=0, tiled=True)]
    all_to_all x5 -> x4, waiting for transfers between devices: 69.4 us -> 64.5 us  [exchange(): return lax.all_to_all(array, axes, split_axis=0, concat_axis=0, tiled=True)]
    unnamed x24 -> x26, local copies, waits for them, and re-layouts: 6.87 us -> 7.79 us
  transfers between devices with their start and end apart: 9 -> 8, of which waited for: 7 -> 6; matrix products, arithmetic and copies ran while one was open for 1% -> 1% of each run, Pallas kernels for 3% -> 2%
where the time goes in v2:
time: 139 us
  waiting for transfers between devices  68.5 us (49%)
  starting transfers between devices  52.9 us (38%)
  Pallas kernels  7.95 us (6%)
  local copies, waits for them, and re-layouts  7.79 us (6%)
    all_to_all x4, waiting for transfers between devices, exchange(): return lax.all_to_all(array, axes, split_axis=0, concat_axis=0, tiled=True)  64.5 us
    all_to_all x4, starting transfers between devices, exchange(): return lax.all_to_all(array, axes, split_axis=0, concat_axis=0, tiled=True)  45.2 us
    unnamed x26, local copies, waits for them, and re-layouts  7.79 us
    ppermute x4, starting transfers between devices, swap(): return lax.ppermute(array, 'core', [(0, 1), (1, 0)])  7.78 us
    pallas_call x8, Pallas kernels, call(): pl.pallas_call(kernel, out_shape=[jax.ShapeDtypeStruct(shape, kind) for s...  6.87 us
    ppermute x4, waiting for transfers between devices, swap(): return lax.ppermute(array, 'core', [(0, 1), (1, 0)])  3.98 us
  transfers between devices with their start and end apart: 8, of which 6 were waited for; matrix products, arithmetic and copies ran while one was open for 1% of the time, Pallas kernels for 2%

profile of v2, /device:TPU:16, one launch (start us, length us, event | category | flops | bytes accessed | tf_op | source)
XLA Modules:
  0.0 138.6 jit_solution(6733736090158852227)
XLA Ops:
  0.6 0.9 copy-done.6
  1.6 0.9 copy-done.7
  2.5 0.9 copy-done.8
  3.4 1.1 shard_map.111
  4.6 20.0 %all-to-all-start = ((bf16[16,160,128]{2,1,0:T(8,128)(2,1)}), bf16[16,160,128]{2,1,0:T(8,128)(2,1)S(1)}, u32[]{:S(2)}, u32[]{:S(2)}) async-start(bf16[16,160,128]{2,1,0:T(8,128)(2,1)} %shard_map.111), calls=%async_computation | async-start | bytes 1310720 | tf_op jit(solution)/shard_map/all_to_all | solution.py:208
  24.6 0.1 copy.12.index_ref
  24.7 0.4 shard_map.112.onehot_ref
  25.2 20.8 %all-to-all-done.pack_ref = bf16[16,160,128]{2,1,0:T(8,128)(2,1)S(1)} async-done(((bf16[16,160,128]{2,1,0:T(8,128)(2,1)}), bf16[16,160,128]{2,1,0:T(8,128)(2,1)S(1)}, u32[]{:S(2)}, u32[]{:S(2)}) %all-to-all-start) | async-done | bytes 655392 | tf_op jit(solution)/shard_map/all_to_all | solution.py:208
  46.0 1.3 shard_map.113
  47.4 12.4 %all-to-all-start.1 = ((bf16[32,128,128]{2,1,0:T(8,128)(2,1)}), bf16[32,128,128]{2,1,0:T(8,128)(2,1)S(1)}, u32[]{:S(2)}, u32[]{:S(2)}) async-start(bf16[32,128,128]{2,1,0:T(8,128)(2,1)} %get-tuple-element.16), calls=%async_computation.1 | async-start | bytes 2097152 | tf_op jit(solution)/shard_map/all_to_all | solution.py:208
  59.8 1.6 %copy-done = bf16[128,8192]{1,0:T(8,128)(2,1)S(1)} copy-done((bf16[128,8192]{1,0:T(8,128)(2,1)S(1)}, bf16[128,8192]{1,0:T(8,128)(2,1)}, u32[]{:S(2)}) %copy-start) | copy-done | bytes 2097176
  61.4 0.6 shard_map.114
  62.0 0.9 copy-done.3
  62.9 1.9 %collective-permute-start = (bf16[128,4224]{1,0:T(8,128)(2,1)S(1)}, bf16[128,4224]{1,0:T(8,128)(2,1)S(1)}, u32[]{:S(2)}, u32[]{:S(2)}) collective-permute-start(bf16[128,4224]{1,0:T(8,128)(2,1)S(1)} %get-tuple-element.18), channel_id=1, source_target_pairs={{0,1},{1,0},{2,3},{3,2},{4,5},{5,4},{6,7},{7,6},{8,9},{9,8},{10,11... | collective-permute-start | bytes 3244040 | tf_op jit(solution)/shard_map/ppermute | solution.py:204
  64.8 2.7 %collective-permute-done.mate_ref = bf16[128,4224]{1,0:T(8,128)(2,1)S(1)} collective-permute-done((bf16[128,4224]{1,0:T(8,128)(2,1)S(1)}, bf16[128,4224]{1,0:T(8,128)(2,1)S(1)}, u32[]{:S(2)}, u32[]{:S(2)}) %collective-permute-start) | collective-permute-done | bytes 1081376 | tf_op jit(solution)/shard_map/ppermute | solution.py:204
  67.5 0.8 shard_map.116
  68.3 1.0 copy-done.1
  69.3 2.0 %collective-permute-start.2 = (f32[256,256]{1,0:T(8,128)S(1)}, f32[256,256]{1,0:T(8,128)S(1)}, u32[]{:S(2)}, u32[]{:S(2)}) collective-permute-start(f32[256,256]{1,0:T(8,128)S(1)} %get-tuple-element.20.stat_ref), channel_id=1, source_target_pairs={{0,1},{1,0},{2,3},{3,2},{4,5},{5,4},{6,7},{7,6},{8,9},{9,8},{10,11... | collective-permute-start | bytes 786440 | tf_op jit(solution)/shard_map/ppermute | solution.py:204
  71.3 16.1 %all-to-all-done.1.blocks_ref = bf16[32,128,128]{2,1,0:T(8,128)(2,1)S(1)} async-done(((bf16[32,128,128]{2,1,0:T(8,128)(2,1)}), bf16[32,128,128]{2,1,0:T(8,128)(2,1)S(1)}, u32[]{:S(2)}, u32[]{:S(2)}) %all-to-all-start.1) | async-done | bytes 1048608 | tf_op jit(solution)/shard_map/all_to_all | solution.py:208
  87.5 1.2 copy-done.4
  88.7 0.7 shard_map.115.part_ref
  89.4 1.9 %collective-permute-start.1 = (f32[128,256]{1,0:T(8,128)S(1)}, f32[128,256]{1,0:T(8,128)S(1)}, u32[]{:S(2)}, u32[]{:S(2)}) collective-permute-start(f32[128,256]{1,0:T(8,128)S(1)} %shard_map.115.part_ref), channel_id=1, source_target_pairs={{0,1},{1,0},{2,3},{3,2},{4,5},{5,4},{6,7},{7,6},{8,9},{9,8},{10,11... | collective-permute-start | bytes 393224 | tf_op jit(solution)/shard_map/ppermute | solution.py:204
  91.3 1.3 collective-permute-done.1.other_ref
  92.6 1.7 %shard_map.117 = (bf16[32,32,256]{2,1,0:T(8,128)(2,1)}, f32[128,128]{1,0:T(8,128)S(1)}, f32[128,128]{1,0:T(8,128)S(1)}) custom-call(f32[128,256]{1,0:T(8,128)S(1)} %shard_map.115.part_ref, f32[128,256]{1,0:T(8,128)S(1)} %collective-permute-done.1.other_ref, bf16[128,128]{1,0:T(8,128)(2,1)S(1)} %copy-done.5, ...), custom_call_target="tpu_custom_call" | custom-call | tf_op jit(solution)/shard_map/pallas_call | solution.py:34
  94.3 7.7 %all-to-all-start.2 = ((bf16[32,32,256]{2,1,0:T(8,128)(2,1)}), bf16[32,32,256]{2,1,0:T(8,128)(2,1)S(1)}, u32[]{:S(2)}, u32[]{:S(2)}) async-start(bf16[32,32,256]{2,1,0:T(8,128)(2,1)} %get-tuple-element.23), calls=%async_computation.2 | async-start | bytes 1048576 | tf_op jit(solution)/shard_map/all_to_all | solution.py:208
  102.0 1.9 %collective-permute-start.3 = (f32[128,128]{1,0:T(8,128)S(1)}, f32[128,128]{1,0:T(8,128)S(1)}, u32[]{:S(2)}, u32[]{:S(2)}) collective-permute-start(f32[128,128]{1,0:T(8,128)S(1)} %get-tuple-element.22), channel_id=1, source_target_pairs={{0,1},{1,0},{2,3},{3,2},{4,5},{5,4},{6,7},{7,6},{8,9},{9,8},{10,11... | collective-permute-start | bytes 196616 | tf_op jit(solution)/shard_map/ppermute | solution.py:204
  103.9 15.8 %all-to-all-done.2.parts_ref = bf16[32,32,256]{2,1,0:T(8,128)(2,1)S(1)} async-done(((bf16[32,32,256]{2,1,0:T(8,128)(2,1)}), bf16[32,32,256]{2,1,0:T(8,128)(2,1)S(1)}, u32[]{:S(2)}, u32[]{:S(2)}) %all-to-all-start.2) | async-done | bytes 524320 | tf_op jit(solution)/shard_map/all_to_all | solution.py:208
  119.7 0.8 shard_map.118
  120.5 5.1 %all-to-all-start.3 = ((bf16[16,4,128]{2,1,0:T(4,128)(2,1)}), bf16[16,4,128]{2,1,0:T(4,128)(2,1)S(1)}, u32[]{:S(2)}, u32[]{:S(2)}) async-start(bf16[16,4,128]{2,1,0:T(4,128)(2,1)} %bitcast.1), calls=%async_computation.3 | async-start | bytes 32768 | tf_op jit(solution)/shard_map/all_to_all | solution.py:208
  125.6 0.6 add_convert_fusion
  126.2 11.8 %all-to-all-done.3 = bf16[16,4,128]{2,1,0:T(4,128)(2,1)S(1)} async-done(((bf16[16,4,128]{2,1,0:T(4,128)(2,1)}), bf16[16,4,128]{2,1,0:T(4,128)(2,1)S(1)}, u32[]{:S(2)}, u32[]{:S(2)}) %all-to-all-start.3) | async-done | bytes 16416 | tf_op jit(solution)/shard_map/all_to_all | solution.py:208
  138.0 0.6 shard_map.119
  (20 shorter events, 0.2 us)
Async XLA Ops:
  0.6 1.0 copy-start.6
  1.6 0.9 copy-start.7
  2.5 0.9 copy-start.8
  3.4 21.1 %copy-start.10 = (s32[128,2]{0,1:T(2,128)S(1)}, s32[128,2]{0,1:T(2,128)}, u32[]{:S(2)}) copy-start(s32[128,2]{0,1:T(2,128)} %param.10) | copy-start | bytes 3076
  4.5 20.6 %copy-start.11 = (f32[128,2]{0,1:T(2,128)S(1)}, f32[128,2]{0,1:T(2,128)}, u32[]{:S(2)}) copy-start(f32[128,2]{0,1:T(2,128)} %param.11) | copy-start | bytes 3076
  4.5 41.5 %copy-start.9 = (bf16[128,128]{1,0:T(8,128)(2,1)S(1)}, bf16[128,128]{1,0:T(8,128)(2,1)}, u32[]{:S(2)}) copy-start(bf16[128,128]{1,0:T(8,128)(2,1)} %grad_ref.1) | copy-start | bytes 98308
  4.6 41.5 %all-to-all-start = ((bf16[16,160,128]{2,1,0:T(8,128)(2,1)}), bf16[16,160,128]{2,1,0:T(8,128)(2,1)S(1)}, u32[]{:S(2)}, u32[]{:S(2)}) async-start(bf16[16,160,128]{2,1,0:T(8,128)(2,1)} %shard_map.111), calls=%async_computation | async-start | bytes 1310720 | tf_op jit(solution)/shard_map/all_to_all | solution.py:208
  47.4 12.4 %copy-start.5 = (bf16[128,128]{1,0:T(8,128)(2,1)S(1)}, bf16[128,128]{1,0:T(8,128)(2,1)}, u32[]{:S(2)}) copy-start(bf16[128,128]{1,0:T(8,128)(2,1)} %query_ref.5) | copy-start | bytes 98308
  47.4 40.1 %all-to-all-start.1 = ((bf16[32,128,128]{2,1,0:T(8,128)(2,1)}), bf16[32,128,128]{2,1,0:T(8,128)(2,1)S(1)}, u32[]{:S(2)}, u32[]{:S(2)}) async-start(bf16[32,128,128]{2,1,0:T(8,128)(2,1)} %get-tuple-element.16), calls=%async_computation.1 | async-start | bytes 2097152 | tf_op jit(solution)/shard_map/all_to_all | solution.py:208
  59.8 1.6 %copy-start = (bf16[128,8192]{1,0:T(8,128)(2,1)S(1)}, bf16[128,8192]{1,0:T(8,128)(2,1)}, u32[]{:S(2)}) copy-start(bf16[128,8192]{1,0:T(8,128)(2,1)} %weight_ref.1) | copy-start | bytes 6291460
  62.0 1.0 copy-start.3
  62.9 4.6 %collective-permute-start = (bf16[128,4224]{1,0:T(8,128)(2,1)S(1)}, bf16[128,4224]{1,0:T(8,128)(2,1)S(1)}, u32[]{:S(2)}, u32[]{:S(2)}) collective-permute-start(bf16[128,4224]{1,0:T(8,128)(2,1)S(1)} %get-tuple-element.18), channel_id=1, source_target_pairs={{0,1},{1,0},{2,3},{3,2},{4,5},{5,4},{6,7},{7,6},{8,9},{9,8},{10,11... | collective-permute-start | bytes 3244040 | tf_op jit(solution)/shard_map/ppermute | solution.py:204
  68.3 1.0 copy-start.1
  69.3 22.0 %collective-permute-start.2 = (f32[256,256]{1,0:T(8,128)S(1)}, f32[256,256]{1,0:T(8,128)S(1)}, u32[]{:S(2)}, u32[]{:S(2)}) collective-permute-start(f32[256,256]{1,0:T(8,128)S(1)} %get-tuple-element.20.stat_ref), channel_id=1, source_target_pairs={{0,1},{1,0},{2,3},{3,2},{4,5},{5,4},{6,7},{7,6},{8,9},{9,8},{10,11... | collective-permute-start | bytes 786440 | tf_op jit(solution)/shard_map/ppermute | solution.py:204
  87.5 1.2 copy-start.4
  88.7 3.9 %copy-start.2 = (f32[256,1024]{1,0:T(8,128)S(1)}, f32[256,1024]{1,0:T(8,128)}, u32[]{:S(2)}) copy-start(f32[256,1024]{1,0:T(8,128)} %copy-done.1) | copy-start | bytes 3145732
  89.4 3.2 %collective-permute-start.1 = (f32[128,256]{1,0:T(8,128)S(1)}, f32[128,256]{1,0:T(8,128)S(1)}, u32[]{:S(2)}, u32[]{:S(2)}) collective-permute-start(f32[128,256]{1,0:T(8,128)S(1)} %shard_map.115.part_ref), channel_id=1, source_target_pairs={{0,1},{1,0},{2,3},{3,2},{4,5},{5,4},{6,7},{7,6},{8,9},{9,8},{10,11... | collective-permute-start | bytes 393224 | tf_op jit(solution)/shard_map/ppermute | solution.py:204
  94.3 25.4 %all-to-all-start.2 = ((bf16[32,32,256]{2,1,0:T(8,128)(2,1)}), bf16[32,32,256]{2,1,0:T(8,128)(2,1)S(1)}, u32[]{:S(2)}, u32[]{:S(2)}) async-start(bf16[32,32,256]{2,1,0:T(8,128)(2,1)} %get-tuple-element.23), calls=%async_computation.2 | async-start | bytes 1048576 | tf_op jit(solution)/shard_map/all_to_all | solution.py:208
  102.0 23.6 %collective-permute-start.3 = (f32[128,128]{1,0:T(8,128)S(1)}, f32[128,128]{1,0:T(8,128)S(1)}, u32[]{:S(2)}, u32[]{:S(2)}) collective-permute-start(f32[128,128]{1,0:T(8,128)S(1)} %get-tuple-element.22), channel_id=1, source_target_pairs={{0,1},{1,0},{2,3},{3,2},{4,5},{5,4},{6,7},{7,6},{8,9},{9,8},{10,11... | collective-permute-start | bytes 196616 | tf_op jit(solution)/shard_map/ppermute | solution.py:204
  120.5 17.5 %all-to-all-start.3 = ((bf16[16,4,128]{2,1,0:T(4,128)(2,1)}), bf16[16,4,128]{2,1,0:T(4,128)(2,1)S(1)}, u32[]{:S(2)}, u32[]{:S(2)}) async-start(bf16[16,4,128]{2,1,0:T(4,128)(2,1)} %bitcast.1), calls=%async_computation.3 | async-start | bytes 32768 | tf_op jit(solution)/shard_map/all_to_all | solution.py:208

commit v3 on v2

--- a/solution.py
+++ b/solution.py
@@ -23,10 +23,12 @@
 N_PEERS = 32
 HALF = 64
 KEYS = N_CTX * HALF
-PACK = CAP + 2 * HALF
+QUARTER = 32
+PACK = CAP + 2 * QUARTER
 F32 = jnp.float32
 BF16 = jnp.bfloat16
 VMEM = pl.BlockSpec(memory_space=pltpu.VMEM)
+HBM = pl.BlockSpec(memory_space=pltpu.HBM)
 PARAMS = pltpu.CompilerParams(vmem_limit_bytes=16 * 1024 * 1024)
 
 
@@ -57,11 +59,22 @@
     return jnp.where(row < 64, block, 2 * N_CTX - 1 - block) * 64 + row % 64
 
 
-def received_kv(pack_ref):
-    return (
-        pack_ref[:, CAP : CAP + HALF].reshape(KEYS, HD),
-        pack_ref[:, CAP + HALF :].reshape(KEYS, HD),
-    )
+def half_of(part):
+    mine = lax.axis_index("xl") % 2
+    return part + mine - 2 * part * mine
+
+
+def joined_kv(pack_ref, seen_ref):
+    return [
+        jnp.concatenate(
+            [
+                pack_ref[:, CAP + at : CAP + at + QUARTER].reshape(KEYS // 2, HD),
+                seen_ref[:, at : at + QUARTER].reshape(KEYS // 2, HD),
+            ],
+            axis=0,
+        )
+        for at in (0, QUARTER)
+    ]
 
 
 def pack_kernel(rows_ref, key_ref, value_ref, out_ref, key_own, value_own, sems):
@@ -70,27 +83,27 @@
     copies = [
         pltpu.make_async_copy(key_ref.at[:, columns], key_own, sems.at[0]),
         pltpu.make_async_copy(value_ref.at[:, columns], value_own, sems.at[1]),
+        pltpu.make_async_copy(rows_ref, out_ref.at[:, :CAP], sems.at[2]),
     ]
     for copy in copies:
         copy.start()
-    out_ref[:, :CAP] = rows_ref[...]
-    select = (iota((HALF, ROWS), 1) == key_row(iota((HALF, ROWS), 0))).astype(BF16)
-    for copy in copies:
-        copy.wait()
+    number = half_of(0) * QUARTER + iota((QUARTER, ROWS), 0)
+    select = (iota((QUARTER, ROWS), 1) == key_row(number)).astype(BF16)
+    copies[0].wait()
+    copies[1].wait()
     keys = dot(select, key_own[...], (1, 0)).astype(BF16)
     values = dot(select, value_own[...], (1, 0)).astype(BF16)
     for c in range(N_CTX):
-        out_ref[c, CAP : CAP + HALF] = keys
-        out_ref[c, CAP + HALF :] = values
-
-
-def weight_kernel(weight_ref, query_ref, own_ref, send_ref):
+        out_ref[c, CAP : CAP + QUARTER] = keys
+        out_ref[c, CAP + QUARTER :] = values
+    copies[2].wait()
+
+
+def weight_kernel(weight_ref, send_ref):
     core = lax.axis_index("core")
     for b in range(N_PEERS):
         there = slice(b * HD, (b + 1) * HD)
-        own_ref[:, there] = weight_ref[:, pl.ds(pl.multiple_of((2 * b + core) * HD, HD), HD)]
         send_ref[:, there] = weight_ref[:, pl.ds(pl.multiple_of((2 * b + 1 - core) * HD, HD), HD)]
-    send_ref[:, N_PEERS * HD :] = query_ref[...]
 
 
 def slots_kernel(index_ref, out_ref):
@@ -118,13 +131,15 @@
         send_ref[b] = residual
 
 
-def forward_kernel(query_ref, mate_ref, pack_ref, probs_ref, stat_ref):
+def forward_kernel(query_ref, mate_ref, pack_ref, other_ref, probs_ref, stat_ref):
     block = lax.axis_index("zh") * 8 + lax.axis_index("y")
-    query = jnp.concatenate([query_ref[...], mate_ref[:, N_PEERS * HD :]], axis=0)
-    keys, values = received_kv(pack_ref)
+    query = jnp.concatenate([query_ref[...], mate_ref[...]], axis=0)
+    keys, values = joined_kv(pack_ref, other_ref)
     row = iota((2 * ROWS, 1), 0) % ROWS
     number = iota((1, KEYS), 1)
-    allowed = position(number // HALF, key_row(number % HALF)) <= position(block, row)
+    source = number % (KEYS // 2) // QUARTER
+    held = half_of(number // (KEYS // 2)) * QUARTER + number % QUARTER
+    allowed = position(source, key_row(held)) <= position(block, row)
     scores = jnp.where(allowed, dot(query, keys, (1, 1)) * SCALE, LOW)
     top = jnp.max(scores, axis=1, keepdims=True)
     probs = jnp.where(allowed, jnp.exp(scores - top), 0.0)
@@ -134,21 +149,46 @@
     stat_ref[:, HD:] = jnp.where(iota((2 * ROWS, HD), 1) < HALF, top, total)
 
 
-def project_kernel(blocks_ref, own_ref, mate_ref, out_ref):
+def project_kernel(blocks_ref, weight_ref, mate_ref, out_ref, own, seen, own_sems, seen_sems):
+    core = lax.axis_index("core")
+    span = 8
+    own_copies = [
+        pltpu.make_async_copy(
+            weight_ref.at[:, pl.ds(pl.multiple_of((2 * b + core) * HD, HD), HD)],
+            own.at[:, b * HD : (b + 1) * HD],
+            own_sems.at[b],
+        )
+        for b in range(N_PEERS)
+    ]
+    seen_copies = [
+        pltpu.make_async_copy(
+            mate_ref.at[:, a * HD : (a + span) * HD],
+            seen.at[:, a * HD : (a + span) * HD],
+            seen_sems.at[a // span],
+        )
+        for a in range(0, N_PEERS, span)
+    ]
+    for a in range(0, N_PEERS, span):
+        seen_copies[a // span].start()
+        for b in range(a, a + span):
+            own_copies[b].start()
     total = [jnp.zeros((ROWS, HD), F32)] * 2
-    for a in range(0, N_PEERS, 8):
-        part = jnp.concatenate([blocks_ref[b] for b in range(a, a + 8)], axis=1)
-        there = slice(a * HD, (a + 8) * HD)
+    for a in range(0, N_PEERS, span):
+        part = jnp.concatenate([blocks_ref[b] for b in range(a, a + span)], axis=1)
+        there = slice(a * HD, (a + span) * HD)
+        seen_copies[a // span].wait()
+        for b in range(a, a + span):
+            own_copies[b].wait()
         total = [
-            total[0] + dot(part, own_ref[:, there], (1, 1)),
-            total[1] + dot(part, mate_ref[:, there], (1, 1)),
+            total[0] + dot(part, own[:, there], (1, 1)),
+            total[1] + dot(part, seen[:, there], (1, 1)),
         ]
     out_ref[:, :HD] = total[0]
     out_ref[:, HD:] = total[1]
 
 
 def backward_kernel(
-    part_ref, other_ref, query_ref, mate_ref, pack_ref, probs_ref, stat_ref, seen_ref,
+    part_ref, other_ref, query_ref, mate_ref, pack_ref, near_ref, probs_ref, stat_ref, seen_ref,
     kv_grad_ref, own_ref, send_ref,
 ):
     grad = jnp.concatenate(
@@ -158,8 +198,8 @@
         ],
         axis=0,
     ).astype(BF16)
-    query = jnp.concatenate([query_ref[...], mate_ref[:, N_PEERS * HD :]], axis=0)
-    keys, values = received_kv(pack_ref)
+    query = jnp.concatenate([query_ref[...], mate_ref[...]], axis=0)
+    keys, values = joined_kv(pack_ref, near_ref)
     mine = stat_ref[...]
     seen = jnp.concatenate([seen_ref[ROWS:], seen_ref[:ROWS]], axis=0)
     top_mine, top_seen = mine[:, HD : HD + 1], seen[:, HD : HD + 1]
@@ -171,11 +211,14 @@
     delta = jnp.sum(grad.astype(F32) * head_out, axis=1, keepdims=True)
     probs = probs_ref[...] * mine_gain
     score_grad = (probs * (dot(grad, values, (1, 1)) - delta)).astype(BF16)
-    key_grad = (dot(score_grad, query, (0, 0)) * SCALE).astype(BF16).reshape(2, 32, 16, HD)
-    value_grad = dot(probs.astype(BF16), grad, (0, 0)).astype(BF16).reshape(2, 32, 16, HD)
-    for zh in range(2):
-        kv_grad_ref[:, zh * 16 : (zh + 1) * 16, :HD] = key_grad[zh]
-        kv_grad_ref[:, zh * 16 : (zh + 1) * 16, HD:] = value_grad[zh]
+    key_grad = (dot(score_grad, query, (0, 0)) * SCALE).astype(BF16).reshape(2, 2, 8, 2, 16, HD)
+    value_grad = dot(probs.astype(BF16), grad, (0, 0)).astype(BF16).reshape(2, 2, 8, 2, 16, HD)
+    for part in range(2):
+        half = half_of(part)
+        for zh in range(2):
+            there = slice(zh * 16, (zh + 1) * 16)
+            kv_grad_ref[:, half, :, there, :HD] = key_grad[part, zh]
+            kv_grad_ref[:, half, :, there, HD:] = value_grad[part, zh]
     query_grad = dot(score_grad, keys, (1, 0)) * SCALE
     own_ref[...] = query_grad[:ROWS]
     send_ref[...] = query_grad[ROWS:]
@@ -212,23 +255,19 @@
     packed = pl.pallas_call(
         pack_kernel,
         out_shape=jax.ShapeDtypeStruct((N_CTX, PACK, HD), BF16),
-        in_specs=[VMEM, pl.BlockSpec(memory_space=pl.ANY), pl.BlockSpec(memory_space=pl.ANY)],
+        in_specs=[HBM] * 3,
         out_specs=VMEM,
         scratch_shapes=[
             pltpu.VMEM((ROWS, HD), BF16),
             pltpu.VMEM((ROWS, HD), BF16),
-            pltpu.SemaphoreType.DMA((2,)),
+            pltpu.SemaphoreType.DMA((3,)),
         ],
         compiler_params=PARAMS,
     )(expert_rows.reshape(N_CTX, CAP, HD), head_key, head_value)
     received = exchange(packed, CTX)
-    own_weight, send_weight = call(
-        weight_kernel,
-        [((ROWS, N_PEERS * HD), BF16), ((ROWS, (N_PEERS + 1) * HD), BF16)],
-        out_weight,
-        head_query,
-    )
-    mate = swap(send_weight)
+    (send_weight,) = call(weight_kernel, [((ROWS, N_PEERS * HD), BF16)], out_weight)
+    mate_weight = swap(send_weight)
+    mate_query = swap(head_query)
     (onehot,) = call(slots_kernel, [((2 * ROWS, EXPERTS * CAP), BF16)], expert_index)
     residual_grad, residual_send = call(
         residual_kernel,
@@ -238,30 +277,45 @@
         onehot,
         combine,
     )
+    near = lax.ppermute(received[:, CAP:], "xl", [(0, 1), (1, 0), (2, 3), (3, 2)])
     blocks = exchange(residual_send, PEERS)
     probs, stat = call(
         forward_kernel,
         [((2 * ROWS, KEYS), F32), ((2 * ROWS, 2 * HD), F32)],
         head_query,
-        mate,
+        mate_query,
         received,
+        near,
     )
     seen = swap(stat)
-    (part,) = call(project_kernel, [((ROWS, 2 * HD), F32)], blocks, own_weight, mate)
+    part = pl.pallas_call(
+        project_kernel,
+        out_shape=jax.ShapeDtypeStruct((ROWS, 2 * HD), F32),
+        in_specs=[VMEM, HBM, HBM],
+        out_specs=VMEM,
+        scratch_shapes=[
+            pltpu.VMEM((ROWS, N_PEERS * HD), BF16),
+            pltpu.VMEM((ROWS, N_PEERS * HD), BF16),
+            pltpu.SemaphoreType.DMA((N_PEERS,)),
+            pltpu.SemaphoreType.DMA((4,)),
+        ],
+        compiler_params=PARAMS,
+    )(blocks, out_weight, mate_weight)
     other = swap(part)
     kv_grad, own_grad, send_grad = call(
         backward_kernel,
-        [((32, 32, 2 * HD), BF16), ((ROWS, HD), F32), ((ROWS, HD), F32)],
+        [((8, 2, 2, 32, 2 * HD), BF16), ((ROWS, HD), F32), ((ROWS, HD), F32)],
         part,
         other,
         head_query,
-        mate,
+        mate_query,
         received,
+        near,
         probs,
         stat,
         seen,
     )
-    kv_parts = exchange(kv_grad, ("y", "xl"))
+    kv_parts = exchange(kv_grad.reshape(32, 32, 2 * HD), ("y", "xl"))
     query_grad = (own_grad + swap(send_grad)).astype(BF16)
     (kv_sum,) = call(sum_kernel, [((64, HD), BF16)], kv_parts)
     final = exchange(kv_sum.reshape(16, 4, HD), ("zh", "zl", "xh"))

time: 139 us -> 146 us (1.050)
  starting transfers between devices: 52.9 us -> 61.9 us
  waiting for transfers between devices: 68.5 us -> 63.5 us
  Pallas kernels: 7.95 us -> 9.97 us
    all_to_all x4, waiting for transfers between devices: 64.5 us -> 42.8 us  [exchange(): return lax.all_to_all(array, axes, split_axis=0, concat_axis=0, tiled=True)]
    ppermute x0 -> x1, waiting for transfers between devices: none -> 18.8 us  [body(): lax.ppermute(received[:, CAP:], 'xl', [(0, 1), (1, 0), (2, 3), (3, 2)])]
    ppermute x0 -> x1, starting transfers between devices: none -> 3.7 us  [body(): lax.ppermute(received[:, CAP:], 'xl', [(0, 1), (1, 0), (2, 3), (3, 2)])]
    all_to_all x4, starting transfers between devices: 45.2 us -> 48 us  [exchange(): return lax.all_to_all(array, axes, split_axis=0, concat_axis=0, tiled=True)]
    ppermute x4 -> x5, starting transfers between devices: 7.78 us -> 10.3 us  [swap(): return lax.ppermute(array, 'core', [(0, 1), (1, 0)])]
    ppermute x4 -> x5, waiting for transfers between devices: 3.98 us -> 1.93 us  [swap(): return lax.ppermute(array, 'core', [(0, 1), (1, 0)])]
    pallas_call x0 -> x1, Pallas kernels: none -> 1.71 us  [body(): pl.pallas_call(project_kernel, out_shape=jax.ShapeDtypeStruct((ROWS, 2 *...]
    pallas_call x8 -> x7, Pallas kernels: 6.87 us -> 7.26 us  [call(): pl.pallas_call(kernel, out_shape=[jax.ShapeDtypeStruct(shape, kind) for s...]
  transfers between devices with their start and end apart: 8 -> 10, of which waited for: 6 -> 6; matrix products, arithmetic and copies ran while one was open for 1% -> 1% of each run, Pallas kernels for 2% -> 3%
where the time goes in v3:
time: 146 us; the launch traced here: 145 us
  waiting for transfers between devices  63.5 us (43%)
  starting transfers between devices  61.9 us (42%)
  Pallas kernels  9.97 us (7%)
  local copies, waits for them, and re-layouts  7.93 us (5%)
    all_to_all x4, starting transfers between devices, exchange(): return lax.all_to_all(array, axes, split_axis=0, concat_axis=0, tiled=True)  48 us
    all_to_all x4, waiting for transfers between devices, exchange(): return lax.all_to_all(array, axes, split_axis=0, concat_axis=0, tiled=True)  42.8 us
    ppermute x1, waiting for transfers between devices, body(): lax.ppermute(received[:, CAP:], 'xl', [(0, 1), (1, 0), (2, 3), (3, 2)])  18.8 us
    ppermute x5, starting transfers between devices, swap(): return lax.ppermute(array, 'core', [(0, 1), (1, 0)])  10.3 us
    unnamed x36, local copies, waits for them, and re-layouts  7.91 us
    pallas_call x7, Pallas kernels, call(): pl.pallas_call(kernel, out_shape=[jax.ShapeDtypeStruct(shape, kind) for s...  7.26 us
    ppermute x1, starting transfers between devices, body(): lax.ppermute(received[:, CAP:], 'xl', [(0, 1), (1, 0), (2, 3), (3, 2)])  3.7 us
  transfers between devices with their start and end apart: 10, of which 6 were waited for; matrix products, arithmetic and copies ran while one was open for 1% of the time, Pallas kernels for 3%

profile of v3, /device:TPU:16, one launch (start us, length us, event | category | flops | bytes accessed | tf_op | source)
XLA Modules:
  0.0 144.8 jit_solution(10647629382927980559)
XLA Ops:
  0.7 0.9 copy-done.8
  1.6 0.9 copy-done.9
  2.6 0.9 copy-done.14
  3.5 1.0 shard_map.111
  4.5 20.1 %all-to-all-start = ((bf16[16,96,128]{2,1,0:T(8,128)(2,1)}), bf16[16,96,128]{2,1,0:T(8,128)(2,1)S(1)}, u32[]{:S(2)}, u32[]{:S(2)}) async-start(bf16[16,96,128]{2,1,0:T(8,128)(2,1)} %shard_map.111), calls=%async_computation | async-start | bytes 786432 | tf_op jit(solution)/shard_map/all_to_all | solution.py:251
  24.6 0.8 copy.12.index_ref
  25.9 15.0 %all-to-all-done.pack_ref = bf16[16,96,128]{2,1,0:T(8,128)(2,1)S(1)} async-done(((bf16[16,96,128]{2,1,0:T(8,128)(2,1)}), bf16[16,96,128]{2,1,0:T(8,128)(2,1)S(1)}, u32[]{:S(2)}, u32[]{:S(2)}) %all-to-all-start) | async-done | bytes 393248 | tf_op jit(solution)/shard_map/all_to_all | solution.py:251
  40.9 0.9 shard_map.113
  41.9 1.0 copy-done.1
  42.8 12.6 %all-to-all-start.1 = ((bf16[32,128,128]{2,1,0:T(8,128)(2,1)}), bf16[32,128,128]{2,1,0:T(8,128)(2,1)S(1)}, u32[]{:S(2)}, u32[]{:S(2)}) async-start(bf16[32,128,128]{2,1,0:T(8,128)(2,1)} %copy-done.1), calls=%async_computation.1 | async-start | bytes 2097152 | tf_op jit(solution)/shard_map/all_to_all | solution.py:251
  55.7 1.9 %collective-permute-start = (bf16[128,4096]{1,0:T(8,128)(2,1)S(1)}, bf16[128,4096]{1,0:T(8,128)(2,1)S(1)}, u32[]{:S(2)}, u32[]{:S(2)}) collective-permute-start(bf16[128,4096]{1,0:T(8,128)(2,1)S(1)} %shard_map.114), channel_id=1, source_target_pairs={{0,1},{1,0},{2,3},{3,2},{4,5},{5,4},{6,7},{7,6},{8,9},{9,8},{10,11... | collective-permute-start | bytes 3145736 | tf_op jit(solution)/shard_map/ppermute | solution.py:247
  57.7 3.7 %collective-permute-start.3 = (bf16[16,64,128]{2,1,0:T(8,128)(2,1)S(1)}, bf16[16,64,128]{2,1,0:T(8,128)(2,1)S(1)}, u32[]{:S(2)}, u32[]{:S(2)}) collective-permute-start(bf16[16,64,128]{2,1,0:T(8,128)(2,1)S(1)} %slice.4), channel_id=1, source_target_pairs={{0,2},{2,0},{4,6},{6,4},{1,3},{3,1},{5,7},{7,5},{8,10},{10,8},{12,... | collective-permute-start | bytes 786440 | tf_op jit(solution)/shard_map/ppermute | solution.py:280
  61.4 2.1 %collective-permute-start.2 = (bf16[128,128]{1,0:T(8,128)(2,1)S(1)}, bf16[128,128]{1,0:T(8,128)(2,1)S(1)}, u32[]{:S(2)}, u32[]{:S(2)}) collective-permute-start(bf16[128,128]{1,0:T(8,128)(2,1)S(1)} %copy-done.10), channel_id=1, source_target_pairs={{0,1},{1,0},{2,3},{3,2},{4,5},{5,4},{6,7},{7,6},{8,9},{9,8},{10,11... | collective-permute-start | bytes 98312 | tf_op jit(solution)/shard_map/ppermute | solution.py:247
  63.5 1.0 collective-permute-done.2.mate_ref
  64.5 18.8 %collective-permute-done.3.other_ref.near_ref = bf16[16,64,128]{2,1,0:T(8,128)(2,1)S(1)} collective-permute-done((bf16[16,64,128]{2,1,0:T(8,128)(2,1)S(1)}, bf16[16,64,128]{2,1,0:T(8,128)(2,1)S(1)}, u32[]{:S(2)}, u32[]{:S(2)}) %collective-permute-start.3) | collective-permute-done | bytes 262176 | tf_op jit(solution)/shard_map/ppermute | solution.py:280
  83.3 1.5 %shard_map.116 = (f32[256,1024]{1,0:T(8,128)S(1)}, f32[256,256]{1,0:T(8,128)}) custom-call(bf16[128,128]{1,0:T(8,128)(2,1)S(1)} %copy-done.10, bf16[128,128]{1,0:T(8,128)(2,1)S(1)} %collective-permute-done.2.mate_ref, bf16[16,96,128]{2,1,0:T(8,128)(2,1)S(1)} %all-to-all-done.pack_ref, bf16[16,64,128]{2,1,0:T(8,128)(2,1)S(1)} %collective-permute-done.3.other_ref.near_ref), custom_call_target="tpu_custom_call" | custom-call | tf_op jit(solution)/shard_map/pallas_call | solution.py:36
  84.8 1.0 copy-done.2
  85.7 1.9 %collective-permute-start.4 = (f32[256,256]{1,0:T(8,128)}, f32[256,256]{1,0:T(8,128)}, u32[]{:S(2)}, u32[]{:S(2)}) collective-permute-start(f32[256,256]{1,0:T(8,128)} %get-tuple-element.16.stat_ref), channel_id=1, source_target_pairs={{0,1},{1,0},{2,3},{3,2},{4,5},{5,4},{6,7},{7,6},{8,9},{9,8},{10,11... | collective-permute-start | bytes 786440 | tf_op jit(solution)/shard_map/ppermute | solution.py:247
  87.7 1.0 copy-done.6
  88.7 1.2 copy-done.7
  89.9 1.7 %shard_map.115.part_ref = f32[128,256]{1,0:T(8,128)S(1)} custom-call(bf16[32,128,128]{2,1,0:T(8,128)(2,1)S(1)} %all-to-all-done.1.blocks_ref, bf16[128,8192]{1,0:T(8,128)(2,1)S(1)} %copy-done, bf16[128,4096]{1,0:T(8,128)(2,1)S(1)} %copy-done.7), custom_call_target="tpu_custom_call" | custom-call | tf_op jit(solution)/shard_map/pallas_call | solution.py:291
  91.6 2.4 %collective-permute-start.1 = (f32[128,256]{1,0:T(8,128)S(1)}, f32[128,256]{1,0:T(8,128)S(1)}, u32[]{:S(2)}, u32[]{:S(2)}) collective-permute-start(f32[128,256]{1,0:T(8,128)S(1)} %shard_map.115.part_ref), channel_id=1, source_target_pairs={{0,1},{1,0},{2,3},{3,2},{4,5},{5,4},{6,7},{7,6},{8,9},{9,8},{10,11... | collective-permute-start | bytes 393224 | tf_op jit(solution)/shard_map/ppermute | solution.py:247
  94.1 1.0 collective-permute-done.1.other_ref
  95.0 2.7 %shard_map.117 = (bf16[8,2,2,32,256]{4,3,2,1,0:T(8,128)(2,1)}, f32[128,128]{1,0:T(8,128)S(1)}, f32[128,128]{1,0:T(8,128)S(1)}) custom-call(f32[128,256]{1,0:T(8,128)S(1)} %shard_map.115.part_ref, f32[128,256]{1,0:T(8,128)S(1)} %collective-permute-done.1.other_ref, bf16[128,128]{1,0:T(8,128)(2,1)S(1)} %copy-done.11, bf16[128,128]{1,0:T(8,128)(2,1)S(1)} %copy-done.13, ...), custom_call_target="tpu_custom_call" | custom-call | tf_op jit(solution)/shard_map/pallas_call | solution.py:36
  97.8 7.7 %all-to-all-start.2 = ((bf16[32,32,256]{2,1,0:T(8,128)(2,1)}), bf16[32,32,256]{2,1,0:T(8,128)(2,1)S(1)}, u32[]{:S(2)}, u32[]{:S(2)}) async-start(bf16[32,32,256]{2,1,0:T(8,128)(2,1)} %bitcast.1), calls=%async_computation.2 | async-start | bytes 1048576 | tf_op jit(solution)/shard_map/all_to_all | solution.py:251
  105.4 1.9 %collective-permute-start.5 = (f32[128,128]{1,0:T(8,128)S(1)}, f32[128,128]{1,0:T(8,128)S(1)}, u32[]{:S(2)}, u32[]{:S(2)}) collective-permute-start(f32[128,128]{1,0:T(8,128)S(1)} %get-tuple-element.18), channel_id=1, source_target_pairs={{0,1},{1,0},{2,3},{3,2},{4,5},{5,4},{6,7},{7,6},{8,9},{9,8},{10,11... | collective-permute-start | bytes 196616 | tf_op jit(solution)/shard_map/ppermute | solution.py:247
  107.4 16.0 %all-to-all-done.2.parts_ref = bf16[32,32,256]{2,1,0:T(8,128)(2,1)S(1)} async-done(((bf16[32,32,256]{2,1,0:T(8,128)(2,1)}), bf16[32,32,256]{2,1,0:T(8,128)(2,1)S(1)}, u32[]{:S(2)}, u32[]{:S(2)}) %all-to-all-start.2) | async-done | bytes 524320 | tf_op jit(solution)/shard_map/all_to_all | solution.py:251
  123.3 0.8 shard_map.118
  124.1 7.6 %all-to-all-start.3 = ((bf16[16,4,128]{2,1,0:T(4,128)(2,1)}), bf16[16,4,128]{2,1,0:T(4,128)(2,1)S(1)}, u32[]{:S(2)}, u32[]{:S(2)}) async-start(bf16[16,4,128]{2,1,0:T(4,128)(2,1)} %bitcast.2), calls=%async_computation.3 | async-start | bytes 32768 | tf_op jit(solution)/shard_map/all_to_all | solution.py:251
  131.7 0.6 add_convert_fusion
  132.4 11.8 %all-to-all-done.3 = bf16[16,4,128]{2,1,0:T(4,128)(2,1)S(1)} async-done(((bf16[16,4,128]{2,1,0:T(4,128)(2,1)}), bf16[16,4,128]{2,1,0:T(4,128)(2,1)S(1)}, u32[]{:S(2)}, u32[]{:S(2)}) %all-to-all-start.3) | async-done | bytes 16416 | tf_op jit(solution)/shard_map/all_to_all | solution.py:251
  144.2 0.6 shard_map.119
  (35 shorter events, 0.9 us)
Async XLA Ops:
  0.6 25.2 %copy-start.16 = (f32[128,2]{0,1:T(2,128)S(1)}, f32[128,2]{0,1:T(2,128)}, u32[]{:S(2)}) copy-start(f32[128,2]{0,1:T(2,128)} %param.11) | copy-start | bytes 3076
  0.6 1.0 copy-start.8
  1.6 0.9 copy-start.9
  2.5 0.9 copy-start.14
  3.5 37.5 %copy-start.15 = (bf16[128,128]{1,0:T(8,128)(2,1)S(1)}, bf16[128,128]{1,0:T(8,128)(2,1)}, u32[]{:S(2)}) copy-start(bf16[128,128]{1,0:T(8,128)(2,1)} %grad_ref.1) | copy-start | bytes 98308
  4.5 51.0 %copy-start = (bf16[128,8192]{1,0:T(8,128)(2,1)S(1)}, bf16[128,8192]{1,0:T(8,128)(2,1)}, u32[]{:S(2)}) copy-start(bf16[128,8192]{1,0:T(8,128)(2,1)} %weight_ref.3) | copy-start | bytes 6291460
  4.5 36.5 %all-to-all-start = ((bf16[16,96,128]{2,1,0:T(8,128)(2,1)}), bf16[16,96,128]{2,1,0:T(8,128)(2,1)S(1)}, u32[]{:S(2)}, u32[]{:S(2)}) async-start(bf16[16,96,128]{2,1,0:T(8,128)(2,1)} %shard_map.111), calls=%async_computation | async-start | bytes 786432 | tf_op jit(solution)/shard_map/all_to_all | solution.py:251
  41.9 1.0 copy-start.1
  42.8 45.8 %all-to-all-start.1 = ((bf16[32,128,128]{2,1,0:T(8,128)(2,1)}), bf16[32,128,128]{2,1,0:T(8,128)(2,1)S(1)}, u32[]{:S(2)}, u32[]{:S(2)}) async-start(bf16[32,128,128]{2,1,0:T(8,128)(2,1)} %copy-done.1), calls=%async_computation.1 | async-start | bytes 2097152 | tf_op jit(solution)/shard_map/all_to_all | solution.py:251
  55.4 6.0 %copy-start.10 = (bf16[128,128]{1,0:T(8,128)(2,1)S(1)}, bf16[128,128]{1,0:T(8,128)(2,1)}, u32[]{:S(2)}) copy-start(bf16[128,128]{1,0:T(8,128)(2,1)} %query_ref.3) | copy-start | bytes 98308
  55.7 31.9 %collective-permute-start = (bf16[128,4096]{1,0:T(8,128)(2,1)S(1)}, bf16[128,4096]{1,0:T(8,128)(2,1)S(1)}, u32[]{:S(2)}, u32[]{:S(2)}) collective-permute-start(bf16[128,4096]{1,0:T(8,128)(2,1)S(1)} %shard_map.114), channel_id=1, source_target_pairs={{0,1},{1,0},{2,3},{3,2},{4,5},{5,4},{6,7},{7,6},{8,9},{9,8},{10,11... | collective-permute-start | bytes 3145736 | tf_op jit(solution)/shard_map/ppermute | solution.py:247
  57.7 25.6 %collective-permute-start.3 = (bf16[16,64,128]{2,1,0:T(8,128)(2,1)S(1)}, bf16[16,64,128]{2,1,0:T(8,128)(2,1)S(1)}, u32[]{:S(2)}, u32[]{:S(2)}) collective-permute-start(bf16[16,64,128]{2,1,0:T(8,128)(2,1)S(1)} %slice.4), channel_id=1, source_target_pairs={{0,2},{2,0},{4,6},{6,4},{1,3},{3,1},{5,7},{7,5},{8,10},{10,8},{12,... | collective-permute-start | bytes 786440 | tf_op jit(solution)/shard_map/ppermute | solution.py:280
  61.4 3.1 %collective-permute-start.2 = (bf16[128,128]{1,0:T(8,128)(2,1)S(1)}, bf16[128,128]{1,0:T(8,128)(2,1)S(1)}, u32[]{:S(2)}, u32[]{:S(2)}) collective-permute-start(bf16[128,128]{1,0:T(8,128)(2,1)S(1)} %copy-done.10), channel_id=1, source_target_pairs={{0,1},{1,0},{2,3},{3,2},{4,5},{5,4},{6,7},{7,6},{8,9},{9,8},{10,11... | collective-permute-start | bytes 98312 | tf_op jit(solution)/shard_map/ppermute | solution.py:247
  64.5 23.1 %copy-start.12 = (bf16[128,128]{1,0:T(8,128)(2,1)}, bf16[128,128]{1,0:T(8,128)(2,1)S(1)}, u32[]{:S(2)}) copy-start(bf16[128,128]{1,0:T(8,128)(2,1)S(1)} %collective-permute-done.2.mate_ref) | copy-start | bytes 98308
  83.3 4.4 %copy-start.4 = (bf16[16,64,128]{2,1,0:T(8,128)(2,1)}, bf16[16,64,128]{2,1,0:T(8,128)(2,1)S(1)}, u32[]{:S(2)}) copy-start(bf16[16,64,128]{2,1,0:T(8,128)(2,1)S(1)} %collective-permute-done.3.other_ref.near_ref) | copy-start | bytes 786436
  84.8 1.0 copy-start.2
  85.7 8.3 %collective-permute-start.4 = (f32[256,256]{1,0:T(8,128)}, f32[256,256]{1,0:T(8,128)}, u32[]{:S(2)}, u32[]{:S(2)}) collective-permute-start(f32[256,256]{1,0:T(8,128)} %get-tuple-element.16.stat_ref), channel_id=1, source_target_pairs={{0,1},{1,0},{2,3},{3,2},{4,5},{5,4},{6,7},{7,6},{8,9},{9,8},{10,11... | collective-permute-start | bytes 786440 | tf_op jit(solution)/shard_map/ppermute | solution.py:247
  87.7 1.0 copy-start.6
  88.7 1.2 copy-start.7
  89.9 5.1 %copy-start.3 = (f32[256,1024]{1,0:T(8,128)S(1)}, f32[256,1024]{1,0:T(8,128)}, u32[]{:S(2)}) copy-start(f32[256,1024]{1,0:T(8,128)} %copy-done.2) | copy-start | bytes 3145732
  89.9 5.1 %copy-start.5 = (bf16[16,64,128]{2,1,0:T(8,128)(2,1)S(1)}, bf16[16,64,128]{2,1,0:T(8,128)(2,1)}, u32[]{:S(2)}) copy-start(bf16[16,64,128]{2,1,0:T(8,128)(2,1)} %copy-done.4) | copy-start | bytes 786436
  89.9 5.1 %copy-start.11 = (bf16[128,128]{1,0:T(8,128)(2,1)S(1)}, bf16[128,128]{1,0:T(8,128)(2,1)}, u32[]{:S(2)}) copy-start(bf16[128,128]{1,0:T(8,128)(2,1)} %query_ref.3) | copy-start | bytes 98308
  89.9 5.1 %copy-start.13 = (bf16[128,128]{1,0:T(8,128)(2,1)S(1)}, bf16[128,128]{1,0:T(8,128)(2,1)}, u32[]{:S(2)}) copy-start(bf16[128,128]{1,0:T(8,128)(2,1)} %copy-done.12) | copy-start | bytes 98308
  91.6 3.4 %collective-permute-start.1 = (f32[128,256]{1,0:T(8,128)S(1)}, f32[128,256]{1,0:T(8,128)S(1)}, u32[]{:S(2)}, u32[]{:S(2)}) collective-permute-start(f32[128,256]{1,0:T(8,128)S(1)} %shard_map.115.part_ref), channel_id=1, source_target_pairs={{0,1},{1,0},{2,3},{3,2},{4,5},{5,4},{6,7},{7,6},{8,9},{9,8},{10,11... | collective-permute-start | bytes 393224 | tf_op jit(solution)/shard_map/ppermute | solution.py:247
  97.8 25.6 %all-to-all-start.2 = ((bf16[32,32,256]{2,1,0:T(8,128)(2,1)}), bf16[32,32,256]{2,1,0:T(8,128)(2,1)S(1)}, u32[]{:S(2)}, u32[]{:S(2)}) async-start(bf16[32,32,256]{2,1,0:T(8,128)(2,1)} %bitcast.1), calls=%async_computation.2 | async-start | bytes 1048576 | tf_op jit(solution)/shard_map/all_to_all | solution.py:251
  105.4 26.3 %collective-permute-start.5 = (f32[128,128]{1,0:T(8,128)S(1)}, f32[128,128]{1,0:T(8,128)S(1)}, u32[]{:S(2)}, u32[]{:S(2)}) collective-permute-start(f32[128,128]{1,0:T(8,128)S(1)} %get-tuple-element.18), channel_id=1, source_target_pairs={{0,1},{1,0},{2,3},{3,2},{4,5},{5,4},{6,7},{7,6},{8,9},{9,8},{10,11... | collective-permute-start | bytes 196616 | tf_op jit(solution)/shard_map/ppermute | solution.py:247
  124.1 20.1 %all-to-all-start.3 = ((bf16[16,4,128]{2,1,0:T(4,128)(2,1)}), bf16[16,4,128]{2,1,0:T(4,128)(2,1)S(1)}, u32[]{:S(2)}, u32[]{:S(2)}) async-start(bf16[16,4,128]{2,1,0:T(4,128)(2,1)} %bitcast.2), calls=%async_computation.3 | async-start | bytes 32768 | tf_op jit(solution)/shard_map/all_to_all | solution.py:251

commit v4 on v3

--- a/solution.py
+++ b/solution.py
@@ -32,14 +32,22 @@
 PARAMS = pltpu.CompilerParams(vmem_limit_bytes=16 * 1024 * 1024)
 
 
-def call(kernel, outs, *operands):
+def in_hbm(array):
+    return pltpu.with_memory_space_constraint(array, pltpu.HBM)
+
+
+def call(kernel, outs, *operands, far=(), far_outs=(), scratch=()):
     return pl.pallas_call(
         kernel,
-        out_shape=[jax.ShapeDtypeStruct(shape, kind) for shape, kind in outs],
-        in_specs=[VMEM] * len(operands),
-        out_specs=[VMEM] * len(outs),
+        out_shape=[
+            pltpu.HBM(shape, kind) if n in far_outs else jax.ShapeDtypeStruct(shape, kind)
+            for n, (shape, kind) in enumerate(outs)
+        ],
+        in_specs=[HBM if n in far else VMEM for n in range(len(operands))],
+        out_specs=[HBM if n in far_outs else VMEM for n in range(len(outs))],
+        scratch_shapes=scratch,
         compiler_params=PARAMS,
-    )(*operands)
+    )(*[in_hbm(operand) if n in far else operand for n, operand in enumerate(operands)])
 
 
 def dot(a, b, dims):
@@ -60,7 +68,7 @@
 
 
 def half_of(part):
-    mine = lax.axis_index("xl") % 2
+    mine = lax.axis_index("y") % 2
     return part + mine - 2 * part * mine
 
 
@@ -77,33 +85,53 @@
     ]
 
 
-def pack_kernel(rows_ref, key_ref, value_ref, out_ref, key_own, value_own, sems):
+def start_all(copies):
+    for copy in copies:
+        copy.start()
+
+
+def wait_all(copies):
+    for copy in copies:
+        copy.wait()
+
+
+def pack_kernel(rows_ref, key_ref, value_ref, out_ref, key_own, value_own, chosen, in_sems, out_sems):
     group = lax.axis_index("zl") * 2 + lax.axis_index("xh")
     columns = pl.ds(pl.multiple_of(group * HD, HD), HD)
-    copies = [
-        pltpu.make_async_copy(key_ref.at[:, columns], key_own, sems.at[0]),
-        pltpu.make_async_copy(value_ref.at[:, columns], value_own, sems.at[1]),
-        pltpu.make_async_copy(rows_ref, out_ref.at[:, :CAP], sems.at[2]),
-    ]
-    for copy in copies:
-        copy.start()
-    number = half_of(0) * QUARTER + iota((QUARTER, ROWS), 0)
-    select = (iota((QUARTER, ROWS), 1) == key_row(number)).astype(BF16)
-    copies[0].wait()
-    copies[1].wait()
+    rows = pltpu.make_async_copy(rows_ref, out_ref.at[:, :CAP], in_sems.at[2])
+    loads = [
+        pltpu.make_async_copy(key_ref.at[:, columns], key_own, in_sems.at[0]),
+        pltpu.make_async_copy(value_ref.at[:, columns], value_own, in_sems.at[1]),
+    ]
+    start_all(loads + [rows])
+    select = (iota((HALF, ROWS), 1) == key_row(iota((HALF, ROWS), 0))).astype(BF16)
+    wait_all(loads)
     keys = dot(select, key_own[...], (1, 0)).astype(BF16)
     values = dot(select, value_own[...], (1, 0)).astype(BF16)
-    for c in range(N_CTX):
-        out_ref[c, CAP : CAP + QUARTER] = keys
-        out_ref[c, CAP + QUARTER :] = values
-    copies[2].wait()
-
-
-def weight_kernel(weight_ref, send_ref):
+    for half in range(2):
+        there = slice(half * QUARTER, (half + 1) * QUARTER)
+        chosen[half, :QUARTER] = keys[there]
+        chosen[half, QUARTER:] = values[there]
+    stores = [
+        pltpu.make_async_copy(chosen.at[c % 2], out_ref.at[c, CAP:], out_sems.at[c])
+        for c in range(N_CTX)
+    ]
+    start_all(stores)
+    wait_all(stores + [rows])
+
+
+def weight_kernel(weight_ref, send_ref, sems):
     core = lax.axis_index("core")
-    for b in range(N_PEERS):
-        there = slice(b * HD, (b + 1) * HD)
-        send_ref[:, there] = weight_ref[:, pl.ds(pl.multiple_of((2 * b + 1 - core) * HD, HD), HD)]
+    copies = [
+        pltpu.make_async_copy(
+            weight_ref.at[:, pl.ds(pl.multiple_of((2 * b + 1 - core) * HD, HD), HD)],
+            send_ref.at[:, b * HD : (b + 1) * HD],
+            sems.at[b],
+        )
+        for b in range(N_PEERS)
+    ]
+    start_all(copies)
+    wait_all(copies)
 
 
 def slots_kernel(index_ref, out_ref):
@@ -120,15 +148,15 @@
         out_ref[k * ROWS : (k + 1) * ROWS] = wide.astype(BF16)
 
 
-def residual_kernel(grad_ref, pack_ref, onehot_ref, combine_ref, out_ref, send_ref):
+def residual_kernel(grad_ref, pack_ref, onehot_ref, combine_ref, out_ref, send_ref, sems):
     rows = pack_ref[:, :CAP].reshape(EXPERTS * CAP, HD)
     picked = dot(onehot_ref[...], rows, (1, 0))
     combine = combine_ref[...]
     moe = combine[:, 0:1] * picked[:ROWS] + combine[:, 1:2] * picked[ROWS:]
-    residual = (grad_ref[...].astype(F32) + moe).astype(BF16)
-    out_ref[...] = residual
-    for b in range(N_PEERS):
-        send_ref[b] = residual
+    out_ref[...] = (grad_ref[...].astype(F32) + moe).astype(BF16)
+    copies = [pltpu.make_async_copy(out_ref, send_ref.at[b], sems.at[b]) for b in range(N_PEERS)]
+    start_all(copies)
+    wait_all(copies)
 
 
 def forward_kernel(query_ref, mate_ref, pack_ref, other_ref, probs_ref, stat_ref):
@@ -252,20 +280,31 @@
 
 
 def body(out_grad, expert_rows, expert_index, combine, head_query, head_key, head_value, out_weight):
-    packed = pl.pallas_call(
+    (packed,) = call(
         pack_kernel,
-        out_shape=jax.ShapeDtypeStruct((N_CTX, PACK, HD), BF16),
-        in_specs=[HBM] * 3,
-        out_specs=VMEM,
-        scratch_shapes=[
+        [((N_CTX, PACK, HD), BF16)],
+        expert_rows.reshape(N_CTX, CAP, HD),
+        head_key,
+        head_value,
+        far=(0, 1, 2),
+        far_outs=(0,),
+        scratch=[
             pltpu.VMEM((ROWS, HD), BF16),
             pltpu.VMEM((ROWS, HD), BF16),
+            pltpu.VMEM((2, 2 * QUARTER, HD), BF16),
             pltpu.SemaphoreType.DMA((3,)),
+            pltpu.SemaphoreType.DMA((N_CTX,)),
         ],
-        compiler_params=PARAMS,
-    )(expert_rows.reshape(N_CTX, CAP, HD), head_key, head_value)
+    )
     received = exchange(packed, CTX)
-    (send_weight,) = call(weight_kernel, [((ROWS, N_PEERS * HD), BF16)], out_weight)
+    (send_weight,) = call(
+        weight_kernel,
+        [((ROWS, N_PEERS * HD), BF16)],
+        out_weight,
+        far=(0,),
+        far_outs=(0,),
+        scratch=[pltpu.SemaphoreType.DMA((N_PEERS,))],
+    )
     mate_weight = swap(send_weight)
     mate_query = swap(head_query)
     (onehot,) = call(slots_kernel, [((2 * ROWS, EXPERTS * CAP), BF16)], expert_index)
@@ -276,8 +315,10 @@
         received,
         onehot,
         combine,
-    )
-    near = lax.ppermute(received[:, CAP:], "xl", [(0, 1), (1, 0), (2, 3), (3, 2)])
+        far_outs=(1,),
+        scratch=[pltpu.SemaphoreType.DMA((N_PEERS,))],
+    )
+    near = lax.ppermute(received[:, CAP:], "y", [(n, n ^ 1) for n in range(8)])
     blocks = exchange(residual_send, PEERS)
     probs, stat = call(
         forward_kernel,
@@ -288,19 +329,20 @@
         near,
     )
     seen = swap(stat)
-    part = pl.pallas_call(
+    (part,) = call(
         project_kernel,
-        out_shape=jax.ShapeDtypeStruct((ROWS, 2 * HD), F32),
-        in_specs=[VMEM, HBM, HBM],
-        out_specs=VMEM,
-        scratch_shapes=[
+        [((ROWS, 2 * HD), F32)],
+        blocks,
+        out_weight,
+        mate_weight,
+        far=(1, 2),
+        scratch=[
             pltpu.VMEM((ROWS, N_PEERS * HD), BF16),
             pltpu.VMEM((ROWS, N_PEERS * HD), BF16),
             pltpu.SemaphoreType.DMA((N_PEERS,)),
             pltpu.SemaphoreType.DMA((4,)),
         ],
-        compiler_params=PARAMS,
-    )(blocks, out_weight, mate_weight)
+    )
     other = swap(part)
     kv_grad, own_grad, send_grad = call(
         backward_kernel,

time: 146 us -> 161 us (1.10)
  Pallas kernels: 9.97 us -> 47.5 us
  waiting for transfers between devices: 63.5 us -> 50 us
  local copies, waits for them, and re-layouts: 7.93 us -> 0.93 us
  starting transfers between devices: 61.9 us -> 59.9 us
    pallas_call x9, Pallas kernels: 9.97 us -> 47.5 us  [call(): pl.pallas_call(kernel, out_shape=[pltpu.HBM(shape, kind) if n in far_outs...]
    ppermute x1, waiting for transfers between devices: 18.8 us -> 5.25 us  [body(): near = lax.ppermute(received[:, CAP:], 'y', [(n, n ^ 1) for n in range(8)])]
    unnamed x36 -> x8, local copies, waits for them, and re-layouts: 7.91 us -> 0.91 us
  transfers between devices with their start and end apart: 10 -> 10, of which waited for: 6 -> 6; matrix products, arithmetic and copies ran while one was open for 1% -> 1% of each run, Pallas kernels for 3% -> 24%
where the time goes in v4:
time: 161 us; the launch traced here: 160 us
  starting transfers between devices  59.9 us (37%)
  waiting for transfers between devices  50 us (31%)
  Pallas kernels  47.5 us (30%)
    pallas_call x9, Pallas kernels, call(): pl.pallas_call(kernel, out_shape=[pltpu.HBM(shape, kind) if n in far_outs...  47.5 us
    all_to_all x4, starting transfers between devices, exchange(): return lax.all_to_all(array, axes, split_axis=0, concat_axis=0, tiled=True)  47.4 us
    all_to_all x4, waiting for transfers between devices, exchange(): return lax.all_to_all(array, axes, split_axis=0, concat_axis=0, tiled=True)  42.8 us
    ppermute x5, starting transfers between devices, swap(): return lax.ppermute(array, 'core', [(0, 1), (1, 0)])  10.3 us
    ppermute x1, waiting for transfers between devices, body(): near = lax.ppermute(received[:, CAP:], 'y', [(n, n ^ 1) for n in range(8)])  5.25 us
  transfers between devices with their start and end apart: 10, of which 6 were waited for; matrix products, arithmetic and copies ran while one was open for 1% of the time, Pallas kernels for 24%

profile of v4, /device:TPU:16, one launch (start us, length us, event | category | flops | bytes accessed | tf_op | source)
XLA Modules:
  0.0 159.8 jit_solution(16616289194302906519)
XLA Ops:
  0.7 5.3 %shard_map.111 = bf16[16,96,128]{2,1,0:T(8,128)(2,1)} custom-call(bf16[16,32,128]{2,1,0:T(8,128)(2,1)} %bitcast.5, bf16[128,1024]{1,0:T(8,128)(2,1)} %key_ref.1, bf16[128,1024]{1,0:T(8,128)(2,1)} %value_ref.1), custom_call_target="tpu_custom_call" | custom-call | tf_op jit(solution)/shard_map/pallas_call | solution.py:40
  5.9 20.0 %all-to-all-start = ((bf16[16,96,128]{2,1,0:T(8,128)(2,1)}), bf16[16,96,128]{2,1,0:T(8,128)(2,1)S(1)}, u32[]{:S(2)}, u32[]{:S(2)}) async-start(bf16[16,96,128]{2,1,0:T(8,128)(2,1)} %shard_map.111), calls=%async_computation | async-start | bytes 786432 | tf_op jit(solution)/shard_map/all_to_all | solution.py:279
  25.9 0.8 copy.12.index_ref
  26.7 0.4 shard_map.112.onehot_ref
  27.1 0.1 copy.13.combine_ref
  27.3 15.0 %all-to-all-done.pack_ref = bf16[16,96,128]{2,1,0:T(8,128)(2,1)S(1)} async-done(((bf16[16,96,128]{2,1,0:T(8,128)(2,1)}), bf16[16,96,128]{2,1,0:T(8,128)(2,1)S(1)}, u32[]{:S(2)}, u32[]{:S(2)}) %all-to-all-start) | async-done | bytes 393248 | tf_op jit(solution)/shard_map/all_to_all | solution.py:279
  42.2 2.1 %shard_map.113 = (bf16[128,128]{1,0:T(8,128)(2,1)}, bf16[32,128,128]{2,1,0:T(8,128)(2,1)}) custom-call(bf16[128,128]{1,0:T(8,128)(2,1)S(1)} %copy-done.1, bf16[16,96,128]{2,1,0:T(8,128)(2,1)S(1)} %all-to-all-done.pack_ref, bf16[256,512]{1,0:T(8,128)(2,1)S(1)} %shard_map.112.onehot_ref, f32[128,2]{1,0:T(8,128)S(1)} %copy.13.combine_ref), custom_call_target="tpu_custom_call" | custom-call | tf_op jit(solution)/shard_map/pallas_call | solution.py:40
  44.4 12.6 %all-to-all-start.1 = ((bf16[32,128,128]{2,1,0:T(8,128)(2,1)}), bf16[32,128,128]{2,1,0:T(8,128)(2,1)S(1)}, u32[]{:S(2)}, u32[]{:S(2)}) async-start(bf16[32,128,128]{2,1,0:T(8,128)(2,1)} %get-tuple-element.14), calls=%async_computation.1 | async-start | bytes 2097152 | tf_op jit(solution)/shard_map/all_to_all | solution.py:279
  57.0 0.0 copy-start
  57.0 33.2 %shard_map.114 = bf16[128,4096]{1,0:T(8,128)(2,1)} custom-call(bf16[128,8192]{1,0:T(8,128)(2,1)} %weight_ref.3), custom_call_target="tpu_custom_call" | custom-call | tf_op jit(solution)/shard_map/pallas_call | solution.py:40
  90.1 1.9 %collective-permute-start = (bf16[128,4096]{1,0:T(8,128)(2,1)}, bf16[128,4096]{1,0:T(8,128)(2,1)}, u32[]{:S(2)}, u32[]{:S(2)}) collective-permute-start(bf16[128,4096]{1,0:T(8,128)(2,1)} %shard_map.114), channel_id=1, source_target_pairs={{0,1},{1,0},{2,3},{3,2},{4,5},{5,4},{6,7},{7,6},{8,9},{9,8},{10,11... | collective-permute-start | bytes 3145736 | tf_op jit(solution)/shard_map/ppermute | solution.py:275
  92.1 2.2 %collective-permute-start.3 = (bf16[16,64,128]{2,1,0:T(8,128)(2,1)S(1)}, bf16[16,64,128]{2,1,0:T(8,128)(2,1)S(1)}, u32[]{:S(2)}, u32[]{:S(2)}) collective-permute-start(bf16[16,64,128]{2,1,0:T(8,128)(2,1)S(1)} %slice.4), channel_id=1, source_target_pairs={{0,64},{64,0},{128,192},{192,128},{256,320},{320,256},{384,448},{4... | collective-permute-start | bytes 786440 | tf_op jit(solution)/shard_map/ppermute | solution.py:321
  94.3 2.1 %collective-permute-start.2 = (bf16[128,128]{1,0:T(8,128)(2,1)S(1)}, bf16[128,128]{1,0:T(8,128)(2,1)S(1)}, u32[]{:S(2)}, u32[]{:S(2)}) collective-permute-start(bf16[128,128]{1,0:T(8,128)(2,1)S(1)} %copy-done), channel_id=1, source_target_pairs={{0,1},{1,0},{2,3},{3,2},{4,5},{5,4},{6,7},{7,6},{8,9},{9,8},{10,11... | collective-permute-start | bytes 98312 | tf_op jit(solution)/shard_map/ppermute | solution.py:275
  96.5 1.0 collective-permute-done.2.mate_ref
  97.4 5.3 %collective-permute-done.3.other_ref.near_ref = bf16[16,64,128]{2,1,0:T(8,128)(2,1)S(1)} collective-permute-done((bf16[16,64,128]{2,1,0:T(8,128)(2,1)S(1)}, bf16[16,64,128]{2,1,0:T(8,128)(2,1)S(1)}, u32[]{:S(2)}, u32[]{:S(2)}) %collective-permute-start.3) | collective-permute-done | bytes 262176 | tf_op jit(solution)/shard_map/ppermute | solution.py:321
  102.7 0.8 shard_map.116
  103.5 1.9 %collective-permute-start.4 = (f32[256,256]{1,0:T(8,128)S(1)}, f32[256,256]{1,0:T(8,128)S(1)}, u32[]{:S(2)}, u32[]{:S(2)}) collective-permute-start(f32[256,256]{1,0:T(8,128)S(1)} %get-tuple-element.16.stat_ref), channel_id=1, source_target_pairs={{0,1},{1,0},{2,3},{3,2},{4,5},{5,4},{6,7},{7,6},{8,9},{9,8},{10,11... | collective-permute-start | bytes 786440 | tf_op jit(solution)/shard_map/ppermute | solution.py:275
  105.4 0.0 all-to-all-done.1.blocks_ref
  105.5 2.7 %shard_map.115.part_ref = f32[128,256]{1,0:T(8,128)S(1)} custom-call(bf16[32,128,128]{2,1,0:T(8,128)(2,1)S(1)} %all-to-all-done.1.blocks_ref, bf16[128,8192]{1,0:T(8,128)(2,1)} %weight_ref.3, bf16[128,4096]{1,0:T(8,128)(2,1)} %collective-permute-done.mate_ref), custom_call_target="tpu_custom_call" | custom-call | tf_op jit(solution)/shard_map/pallas_call | solution.py:40
  108.1 2.4 %collective-permute-start.1 = (f32[128,256]{1,0:T(8,128)S(1)}, f32[128,256]{1,0:T(8,128)S(1)}, u32[]{:S(2)}, u32[]{:S(2)}) collective-permute-start(f32[128,256]{1,0:T(8,128)S(1)} %shard_map.115.part_ref), channel_id=1, source_target_pairs={{0,1},{1,0},{2,3},{3,2},{4,5},{5,4},{6,7},{7,6},{8,9},{9,8},{10,11... | collective-permute-start | bytes 393224 | tf_op jit(solution)/shard_map/ppermute | solution.py:275
  110.6 0.0 collective-permute-done.4.seen_ref
  110.6 1.0 collective-permute-done.1.other_ref
  111.5 1.7 %shard_map.117 = (bf16[8,2,2,32,256]{4,3,2,1,0:T(8,128)(2,1)}, f32[128,128]{1,0:T(8,128)S(1)}, f32[128,128]{1,0:T(8,128)S(1)}) custom-call(f32[128,256]{1,0:T(8,128)S(1)} %shard_map.115.part_ref, f32[128,256]{1,0:T(8,128)S(1)} %collective-permute-done.1.other_ref, bf16[128,128]{1,0:T(8,128)(2,1)S(1)} %copy-done, ...), custom_call_target="tpu_custom_call" | custom-call | tf_op jit(solution)/shard_map/pallas_call | solution.py:40
  113.2 8.0 %all-to-all-start.2 = ((bf16[32,32,256]{2,1,0:T(8,128)(2,1)}), bf16[32,32,256]{2,1,0:T(8,128)(2,1)S(1)}, u32[]{:S(2)}, u32[]{:S(2)}) async-start(bf16[32,32,256]{2,1,0:T(8,128)(2,1)} %bitcast.1), calls=%async_computation.2 | async-start | bytes 1048576 | tf_op jit(solution)/shard_map/all_to_all | solution.py:279
  121.2 1.9 %collective-permute-start.5 = (f32[128,128]{1,0:T(8,128)S(1)}, f32[128,128]{1,0:T(8,128)S(1)}, u32[]{:S(2)}, u32[]{:S(2)}) collective-permute-start(f32[128,128]{1,0:T(8,128)S(1)} %get-tuple-element.18), channel_id=1, source_target_pairs={{0,1},{1,0},{2,3},{3,2},{4,5},{5,4},{6,7},{7,6},{8,9},{9,8},{10,11... | collective-permute-start | bytes 196616 | tf_op jit(solution)/shard_map/ppermute | solution.py:275
  123.1 16.0 %all-to-all-done.2.parts_ref = bf16[32,32,256]{2,1,0:T(8,128)(2,1)S(1)} async-done(((bf16[32,32,256]{2,1,0:T(8,128)(2,1)}), bf16[32,32,256]{2,1,0:T(8,128)(2,1)S(1)}, u32[]{:S(2)}, u32[]{:S(2)}) %all-to-all-start.2) | async-done | bytes 524320 | tf_op jit(solution)/shard_map/all_to_all | solution.py:279
  139.0 0.8 shard_map.118
  139.8 6.8 %all-to-all-start.3 = ((bf16[16,4,128]{2,1,0:T(4,128)(2,1)}), bf16[16,4,128]{2,1,0:T(4,128)(2,1)S(1)}, u32[]{:S(2)}, u32[]{:S(2)}) async-start(bf16[16,4,128]{2,1,0:T(4,128)(2,1)} %bitcast.2), calls=%async_computation.3 | async-start | bytes 32768 | tf_op jit(solution)/shard_map/all_to_all | solution.py:279
  146.7 0.0 collective-permute-done.5
  146.7 0.6 add_convert_fusion
  147.3 11.8 %all-to-all-done.3 = bf16[16,4,128]{2,1,0:T(4,128)(2,1)S(1)} async-done(((bf16[16,4,128]{2,1,0:T(4,128)(2,1)}), bf16[16,4,128]{2,1,0:T(4,128)(2,1)S(1)}, u32[]{:S(2)}, u32[]{:S(2)}) %all-to-all-start.3) | async-done | bytes 16416 | tf_op jit(solution)/shard_map/all_to_all | solution.py:279
  159.2 0.6 shard_map.119
  (7 shorter events, 0.0 us)
Async XLA Ops:
  0.6 26.5 %copy-start.2 = (f32[128,2]{0,1:T(2,128)S(1)}, f32[128,2]{0,1:T(2,128)}, u32[]{:S(2)}) copy-start(f32[128,2]{0,1:T(2,128)} %param.11) | copy-start | bytes 3076
  0.6 41.6 %copy-start.1 = (bf16[128,128]{1,0:T(8,128)(2,1)S(1)}, bf16[128,128]{1,0:T(8,128)(2,1)}, u32[]{:S(2)}) copy-start(bf16[128,128]{1,0:T(8,128)(2,1)} %grad_ref.1) | copy-start | bytes 98308
  5.9 36.3 %all-to-all-start = ((bf16[16,96,128]{2,1,0:T(8,128)(2,1)}), bf16[16,96,128]{2,1,0:T(8,128)(2,1)S(1)}, u32[]{:S(2)}, u32[]{:S(2)}) async-start(bf16[16,96,128]{2,1,0:T(8,128)(2,1)} %shard_map.111), calls=%async_computation | async-start | bytes 786432 | tf_op jit(solution)/shard_map/all_to_all | solution.py:279
  44.4 61.1 %all-to-all-start.1 = ((bf16[32,128,128]{2,1,0:T(8,128)(2,1)}), bf16[32,128,128]{2,1,0:T(8,128)(2,1)S(1)}, u32[]{:S(2)}, u32[]{:S(2)}) async-start(bf16[32,128,128]{2,1,0:T(8,128)(2,1)} %get-tuple-element.14), calls=%async_computation.1 | async-start | bytes 2097152 | tf_op jit(solution)/shard_map/all_to_all | solution.py:279
  57.0 37.4 %copy-start = (bf16[128,128]{1,0:T(8,128)(2,1)S(1)}, bf16[128,128]{1,0:T(8,128)(2,1)}, u32[]{:S(2)}) copy-start(bf16[128,128]{1,0:T(8,128)(2,1)} %query_ref.3) | copy-start | bytes 98308
  90.1 15.3 %collective-permute-start = (bf16[128,4096]{1,0:T(8,128)(2,1)}, bf16[128,4096]{1,0:T(8,128)(2,1)}, u32[]{:S(2)}, u32[]{:S(2)}) collective-permute-start(bf16[128,4096]{1,0:T(8,128)(2,1)} %shard_map.114), channel_id=1, source_target_pairs={{0,1},{1,0},{2,3},{3,2},{4,5},{5,4},{6,7},{7,6},{8,9},{9,8},{10,11... | collective-permute-start | bytes 3145736 | tf_op jit(solution)/shard_map/ppermute | solution.py:275
  92.1 10.6 %collective-permute-start.3 = (bf16[16,64,128]{2,1,0:T(8,128)(2,1)S(1)}, bf16[16,64,128]{2,1,0:T(8,128)(2,1)S(1)}, u32[]{:S(2)}, u32[]{:S(2)}) collective-permute-start(bf16[16,64,128]{2,1,0:T(8,128)(2,1)S(1)} %slice.4), channel_id=1, source_target_pairs={{0,64},{64,0},{128,192},{192,128},{256,320},{320,256},{384,448},{4... | collective-permute-start | bytes 786440 | tf_op jit(solution)/shard_map/ppermute | solution.py:321
  94.3 3.1 %collective-permute-start.2 = (bf16[128,128]{1,0:T(8,128)(2,1)S(1)}, bf16[128,128]{1,0:T(8,128)(2,1)S(1)}, u32[]{:S(2)}, u32[]{:S(2)}) collective-permute-start(bf16[128,128]{1,0:T(8,128)(2,1)S(1)} %copy-done), channel_id=1, source_target_pairs={{0,1},{1,0},{2,3},{3,2},{4,5},{5,4},{6,7},{7,6},{8,9},{9,8},{10,11... | collective-permute-start | bytes 98312 | tf_op jit(solution)/shard_map/ppermute | solution.py:275
  103.5 7.1 %collective-permute-start.4 = (f32[256,256]{1,0:T(8,128)S(1)}, f32[256,256]{1,0:T(8,128)S(1)}, u32[]{:S(2)}, u32[]{:S(2)}) collective-permute-start(f32[256,256]{1,0:T(8,128)S(1)} %get-tuple-element.16.stat_ref), channel_id=1, source_target_pairs={{0,1},{1,0},{2,3},{3,2},{4,5},{5,4},{6,7},{7,6},{8,9},{9,8},{10,11... | collective-permute-start | bytes 786440 | tf_op jit(solution)/shard_map/ppermute | solution.py:275
  108.1 3.4 %collective-permute-start.1 = (f32[128,256]{1,0:T(8,128)S(1)}, f32[128,256]{1,0:T(8,128)S(1)}, u32[]{:S(2)}, u32[]{:S(2)}) collective-permute-start(f32[128,256]{1,0:T(8,128)S(1)} %shard_map.115.part_ref), channel_id=1, source_target_pairs={{0,1},{1,0},{2,3},{3,2},{4,5},{5,4},{6,7},{7,6},{8,9},{9,8},{10,11... | collective-permute-start | bytes 393224 | tf_op jit(solution)/shard_map/ppermute | solution.py:275
  113.2 25.8 %all-to-all-start.2 = ((bf16[32,32,256]{2,1,0:T(8,128)(2,1)}), bf16[32,32,256]{2,1,0:T(8,128)(2,1)S(1)}, u32[]{:S(2)}, u32[]{:S(2)}) async-start(bf16[32,32,256]{2,1,0:T(8,128)(2,1)} %bitcast.1), calls=%async_computation.2 | async-start | bytes 1048576 | tf_op jit(solution)/shard_map/all_to_all | solution.py:279
  121.2 25.6 %collective-permute-start.5 = (f32[128,128]{1,0:T(8,128)S(1)}, f32[128,128]{1,0:T(8,128)S(1)}, u32[]{:S(2)}, u32[]{:S(2)}) collective-permute-start(f32[128,128]{1,0:T(8,128)S(1)} %get-tuple-element.18), channel_id=1, source_target_pairs={{0,1},{1,0},{2,3},{3,2},{4,5},{5,4},{6,7},{7,6},{8,9},{9,8},{10,11... | collective-permute-start | bytes 196616 | tf_op jit(solution)/shard_map/ppermute | solution.py:275
  139.8 19.3 %all-to-all-start.3 = ((bf16[16,4,128]{2,1,0:T(4,128)(2,1)}), bf16[16,4,128]{2,1,0:T(4,128)(2,1)S(1)}, u32[]{:S(2)}, u32[]{:S(2)}) async-start(bf16[16,4,128]{2,1,0:T(4,128)(2,1)} %bitcast.2), calls=%async_computation.3 | async-start | bytes 32768 | tf_op jit(solution)/shard_map/all_to_all | solution.py:279

commit v5 on v4

--- a/solution.py
+++ b/solution.py
@@ -23,8 +23,9 @@
 N_PEERS = 32
 HALF = 64
 KEYS = N_CTX * HALF
-QUARTER = 32
-PACK = CAP + 2 * QUARTER
+SPLIT = 2
+SHARE = HALF // SPLIT
+PACK = CAP + 2 * SHARE
 F32 = jnp.float32
 BF16 = jnp.bfloat16
 VMEM = pl.BlockSpec(memory_space=pltpu.VMEM)
@@ -67,21 +68,18 @@
     return jnp.where(row < 64, block, 2 * N_CTX - 1 - block) * 64 + row % 64
 
 
-def half_of(part):
-    mine = lax.axis_index("y") % 2
-    return part + mine - 2 * part * mine
-
-
-def joined_kv(pack_ref, seen_ref):
+def share_of(part):
+    return lax.bitwise_xor(lax.axis_index("y") % SPLIT, part)
+
+
+def joined_kv(pack_ref, *near_refs):
     return [
         jnp.concatenate(
-            [
-                pack_ref[:, CAP + at : CAP + at + QUARTER].reshape(KEYS // 2, HD),
-                seen_ref[:, at : at + QUARTER].reshape(KEYS // 2, HD),
-            ],
+            [pack_ref[:, CAP + at : CAP + at + SHARE].reshape(N_CTX * SHARE, HD)]
+            + [near_ref[:, at : at + SHARE].reshape(N_CTX * SHARE, HD) for near_ref in near_refs],
             axis=0,
         )
-        for at in (0, QUARTER)
+        for at in (0, SHARE)
     ]
 
 
@@ -95,43 +93,54 @@
         copy.wait()
 
 
-def pack_kernel(rows_ref, key_ref, value_ref, out_ref, key_own, value_own, chosen, in_sems, out_sems):
+def pack_kernel(rows_ref, key_ref, value_ref, out_ref, key_own, value_own, packed, sems):
     group = lax.axis_index("zl") * 2 + lax.axis_index("xh")
     columns = pl.ds(pl.multiple_of(group * HD, HD), HD)
-    rows = pltpu.make_async_copy(rows_ref, out_ref.at[:, :CAP], in_sems.at[2])
+    rows = pltpu.make_async_copy(rows_ref, packed.at[:, :CAP], sems.at[2])
     loads = [
-        pltpu.make_async_copy(key_ref.at[:, columns], key_own, in_sems.at[0]),
-        pltpu.make_async_copy(value_ref.at[:, columns], value_own, in_sems.at[1]),
+        pltpu.make_async_copy(key_ref.at[:, columns], key_own, sems.at[0]),
+        pltpu.make_async_copy(value_ref.at[:, columns], value_own, sems.at[1]),
     ]
     start_all(loads + [rows])
     select = (iota((HALF, ROWS), 1) == key_row(iota((HALF, ROWS), 0))).astype(BF16)
     wait_all(loads)
     keys = dot(select, key_own[...], (1, 0)).astype(BF16)
     values = dot(select, value_own[...], (1, 0)).astype(BF16)
-    for half in range(2):
-        there = slice(half * QUARTER, (half + 1) * QUARTER)
-        chosen[half, :QUARTER] = keys[there]
-        chosen[half, QUARTER:] = values[there]
+    for c in range(N_CTX):
+        there = slice(c % SPLIT * SHARE, (c % SPLIT + 1) * SHARE)
+        packed[c, CAP : CAP + SHARE] = keys[there]
+        packed[c, CAP + SHARE :] = values[there]
+    rows.wait()
+    store = pltpu.make_async_copy(packed, out_ref, sems.at[3])
+    store.start()
+    store.wait()
+
+
+def weight_kernel(weight_ref, own_ref, send_ref, whole, parted, sems):
+    core = lax.axis_index("core")
+    span = 8
+    loads = [
+        pltpu.make_async_copy(
+            weight_ref.at[:, 2 * a * HD : 2 * (a + span) * HD],
+            whole.at[:, 2 * a * HD : 2 * (a + span) * HD],
+            sems.at[a // span],
+        )
+        for a in range(0, N_PEERS, span)
+    ]
+    start_all(loads)
+    for a in range(0, N_PEERS, span):
+        loads[a // span].wait()
+        for b in range(a, a + span):
+            there = slice(b * HD, (b + 1) * HD)
+            for kind in range(2):
+                column = 2 * b + (core if kind == 0 else 1 - core)
+                parted[kind, :, there] = whole[:, pl.ds(pl.multiple_of(column * HD, HD), HD)]
     stores = [
-        pltpu.make_async_copy(chosen.at[c % 2], out_ref.at[c, CAP:], out_sems.at[c])
-        for c in range(N_CTX)
+        pltpu.make_async_copy(parted.at[0], own_ref, sems.at[4]),
+        pltpu.make_async_copy(parted.at[1], send_ref, sems.at[5]),
     ]
     start_all(stores)
-    wait_all(stores + [rows])
-
-
-def weight_kernel(weight_ref, send_ref, sems):
-    core = lax.axis_index("core")
-    copies = [
-        pltpu.make_async_copy(
-            weight_ref.at[:, pl.ds(pl.multiple_of((2 * b + 1 - core) * HD, HD), HD)],
-            send_ref.at[:, b * HD : (b + 1) * HD],
-            sems.at[b],
-        )
-        for b in range(N_PEERS)
-    ]
-    start_all(copies)
-    wait_all(copies)
+    wait_all(stores)
 
 
 def slots_kernel(index_ref, out_ref):
@@ -148,25 +157,33 @@
         out_ref[k * ROWS : (k + 1) * ROWS] = wide.astype(BF16)
 
 
-def residual_kernel(grad_ref, pack_ref, onehot_ref, combine_ref, out_ref, send_ref, sems):
+def residual_kernel(grad_ref, pack_ref, onehot_ref, combine_ref, out_ref, send_ref, copied, sems):
     rows = pack_ref[:, :CAP].reshape(EXPERTS * CAP, HD)
     picked = dot(onehot_ref[...], rows, (1, 0))
     combine = combine_ref[...]
     moe = combine[:, 0:1] * picked[:ROWS] + combine[:, 1:2] * picked[ROWS:]
-    out_ref[...] = (grad_ref[...].astype(F32) + moe).astype(BF16)
-    copies = [pltpu.make_async_copy(out_ref, send_ref.at[b], sems.at[b]) for b in range(N_PEERS)]
+    residual = (grad_ref[...].astype(F32) + moe).astype(BF16)
+    span = copied.shape[0]
+    for b in range(span):
+        copied[b] = residual
+    copies = [
+        pltpu.make_async_copy(copied, send_ref.at[a : a + span], sems.at[a // span])
+        for a in range(0, N_PEERS, span)
+    ]
     start_all(copies)
+    out_ref[...] = residual
     wait_all(copies)
 
 
-def forward_kernel(query_ref, mate_ref, pack_ref, other_ref, probs_ref, stat_ref):
+def forward_kernel(query_ref, mate_ref, pack_ref, *refs):
+    *near_refs, probs_ref, stat_ref = refs
     block = lax.axis_index("zh") * 8 + lax.axis_index("y")
     query = jnp.concatenate([query_ref[...], mate_ref[...]], axis=0)
-    keys, values = joined_kv(pack_ref, other_ref)
+    keys, values = joined_kv(pack_ref, *near_refs)
     row = iota((2 * ROWS, 1), 0) % ROWS
     number = iota((1, KEYS), 1)
-    source = number % (KEYS // 2) // QUARTER
-    held = half_of(number // (KEYS // 2)) * QUARTER + number % QUARTER
+    source = number % (KEYS // SPLIT) // SHARE
+    held = share_of(number // (KEYS // SPLIT)) * SHARE + number % SHARE
     allowed = position(source, key_row(held)) <= position(block, row)
     scores = jnp.where(allowed, dot(query, keys, (1, 1)) * SCALE, LOW)
     top = jnp.max(scores, axis=1, keepdims=True)
@@ -177,48 +194,33 @@
     stat_ref[:, HD:] = jnp.where(iota((2 * ROWS, HD), 1) < HALF, top, total)
 
 
-def project_kernel(blocks_ref, weight_ref, mate_ref, out_ref, own, seen, own_sems, seen_sems):
-    core = lax.axis_index("core")
+def project_kernel(blocks_ref, own_ref, mate_ref, out_ref, own, mate, sems):
     span = 8
-    own_copies = [
+    copies = [
         pltpu.make_async_copy(
-            weight_ref.at[:, pl.ds(pl.multiple_of((2 * b + core) * HD, HD), HD)],
-            own.at[:, b * HD : (b + 1) * HD],
-            own_sems.at[b],
-        )
-        for b in range(N_PEERS)
-    ]
-    seen_copies = [
-        pltpu.make_async_copy(
-            mate_ref.at[:, a * HD : (a + span) * HD],
-            seen.at[:, a * HD : (a + span) * HD],
-            seen_sems.at[a // span],
+            far.at[:, a * HD : (a + span) * HD], near.at[:, a * HD : (a + span) * HD], sems.at[k, a // span]
         )
         for a in range(0, N_PEERS, span)
-    ]
-    for a in range(0, N_PEERS, span):
-        seen_copies[a // span].start()
-        for b in range(a, a + span):
-            own_copies[b].start()
+        for k, (far, near) in enumerate(((own_ref, own), (mate_ref, mate)))
+    ]
+    start_all(copies)
     total = [jnp.zeros((ROWS, HD), F32)] * 2
     for a in range(0, N_PEERS, span):
         part = jnp.concatenate([blocks_ref[b] for b in range(a, a + span)], axis=1)
         there = slice(a * HD, (a + span) * HD)
-        seen_copies[a // span].wait()
-        for b in range(a, a + span):
-            own_copies[b].wait()
+        wait_all(copies[a // span * 2 : a // span * 2 + 2])
         total = [
             total[0] + dot(part, own[:, there], (1, 1)),
-            total[1] + dot(part, seen[:, there], (1, 1)),
+            total[1] + dot(part, mate[:, there], (1, 1)),
         ]
     out_ref[:, :HD] = total[0]
     out_ref[:, HD:] = total[1]
 
 
 def backward_kernel(
-    part_ref, other_ref, query_ref, mate_ref, pack_ref, near_ref, probs_ref, stat_ref, seen_ref,
-    kv_grad_ref, own_ref, send_ref,
+    part_ref, other_ref, query_ref, mate_ref, probs_ref, stat_ref, seen_ref, pack_ref, *refs
 ):
+    *near_refs, kv_grad_ref, own_ref, send_ref = refs
     grad = jnp.concatenate(
         [
             part_ref[:, :HD] + other_ref[:, HD:],
@@ -227,7 +229,7 @@
         axis=0,
     ).astype(BF16)
     query = jnp.concatenate([query_ref[...], mate_ref[...]], axis=0)
-    keys, values = joined_kv(pack_ref, near_ref)
+    keys, values = joined_kv(pack_ref, *near_refs)
     mine = stat_ref[...]
     seen = jnp.concatenate([seen_ref[ROWS:], seen_ref[:ROWS]], axis=0)
     top_mine, top_seen = mine[:, HD : HD + 1], seen[:, HD : HD + 1]
@@ -239,14 +241,15 @@
     delta = jnp.sum(grad.astype(F32) * head_out, axis=1, keepdims=True)
     probs = probs_ref[...] * mine_gain
     score_grad = (probs * (dot(grad, values, (1, 1)) - delta)).astype(BF16)
-    key_grad = (dot(score_grad, query, (0, 0)) * SCALE).astype(BF16).reshape(2, 2, 8, 2, 16, HD)
-    value_grad = dot(probs.astype(BF16), grad, (0, 0)).astype(BF16).reshape(2, 2, 8, 2, 16, HD)
-    for part in range(2):
-        half = half_of(part)
+    shape = (SPLIT, 2, 8, 4 // SPLIT, 16, HD)
+    key_grad = (dot(score_grad, query, (0, 0)) * SCALE).astype(BF16).reshape(shape)
+    value_grad = dot(probs.astype(BF16), grad, (0, 0)).astype(BF16).reshape(shape)
+    for part in range(SPLIT):
+        share = share_of(part)
         for zh in range(2):
             there = slice(zh * 16, (zh + 1) * 16)
-            kv_grad_ref[:, half, :, there, :HD] = key_grad[part, zh]
-            kv_grad_ref[:, half, :, there, HD:] = value_grad[part, zh]
+            kv_grad_ref[:, share, :, there, :HD] = key_grad[part, zh]
+            kv_grad_ref[:, share, :, there, HD:] = value_grad[part, zh]
     query_grad = dot(score_grad, keys, (1, 0)) * SCALE
     own_ref[...] = query_grad[:ROWS]
     send_ref[...] = query_grad[ROWS:]
@@ -291,19 +294,22 @@
         scratch=[
             pltpu.VMEM((ROWS, HD), BF16),
             pltpu.VMEM((ROWS, HD), BF16),
-            pltpu.VMEM((2, 2 * QUARTER, HD), BF16),
-            pltpu.SemaphoreType.DMA((3,)),
-            pltpu.SemaphoreType.DMA((N_CTX,)),
+            pltpu.VMEM((N_CTX, PACK, HD), BF16),
+            pltpu.SemaphoreType.DMA((4,)),
         ],
     )
     received = exchange(packed, CTX)
-    (send_weight,) = call(
+    own_weight, send_weight = call(
         weight_kernel,
-        [((ROWS, N_PEERS * HD), BF16)],
+        [((ROWS, N_PEERS * HD), BF16)] * 2,
         out_weight,
         far=(0,),
-        far_outs=(0,),
-        scratch=[pltpu.SemaphoreType.DMA((N_PEERS,))],
+        far_outs=(0, 1),
+        scratch=[
+            pltpu.VMEM((ROWS, 2 * N_PEERS * HD), BF16),
+            pltpu.VMEM((2, ROWS, N_PEERS * HD), BF16),
+            pltpu.SemaphoreType.DMA((6,)),
+        ],
     )
     mate_weight = swap(send_weight)
     mate_query = swap(head_query)
@@ -316,9 +322,10 @@
         onehot,
         combine,
         far_outs=(1,),
-        scratch=[pltpu.SemaphoreType.DMA((N_PEERS,))],
-    )
-    near = lax.ppermute(received[:, CAP:], "y", [(n, n ^ 1) for n in range(8)])
+        scratch=[pltpu.VMEM((8, ROWS, HD), BF16), pltpu.SemaphoreType.DMA((4,))],
+    )
+    held = received[:, CAP:]
+    near = [lax.ppermute(held, "y", [(n, n ^ p) for n in range(8)]) for p in range(1, SPLIT)]
     blocks = exchange(residual_send, PEERS)
     probs, stat = call(
         forward_kernel,
@@ -326,36 +333,35 @@
         head_query,
         mate_query,
         received,
-        near,
+        *near,
     )
     seen = swap(stat)
     (part,) = call(
         project_kernel,
         [((ROWS, 2 * HD), F32)],
         blocks,
-        out_weight,
+        own_weight,
         mate_weight,
         far=(1, 2),
         scratch=[
             pltpu.VMEM((ROWS, N_PEERS * HD), BF16),
             pltpu.VMEM((ROWS, N_PEERS * HD), BF16),
-            pltpu.SemaphoreType.DMA((N_PEERS,)),
-            pltpu.SemaphoreType.DMA((4,)),
+            pltpu.SemaphoreType.DMA((2, 4)),
         ],
     )
     other = swap(part)
     kv_grad, own_grad, send_grad = call(
         backward_kernel,
-        [((8, 2, 2, 32, 2 * HD), BF16), ((ROWS, HD), F32), ((ROWS, HD), F32)],
+        [((8, SPLIT, 4 // SPLIT, 32, 2 * HD), BF16), ((ROWS, HD), F32), ((ROWS, HD), F32)],
         part,
         other,
         head_query,
         mate_query,
-        received,
-        near,
         probs,
         stat,
         seen,
+        received,
+        *near,
     )
     kv_parts = exchange(kv_grad.reshape(32, 32, 2 * HD), ("y", "xl"))
     query_grad = (own_grad + swap(send_grad)).astype(BF16)

time: 161 us -> 132 us (0.82)
  Pallas kernels: 47.5 us -> 13.1 us
  waiting for transfers between devices: 50 us -> 58.7 us
  starting transfers between devices: 59.9 us -> 56.7 us
    pallas_call x9, Pallas kernels: 47.5 us -> 13.1 us  [call(): pl.pallas_call(kernel, out_shape=[pltpu.HBM(shape, kind) if n in far_outs...]
    all_to_all x4, waiting for transfers between devices: 42.8 us -> 51.2 us  [exchange(): return lax.all_to_all(array, axes, split_axis=0, concat_axis=0, tiled=True)]
    all_to_all x4, starting transfers between devices: 47.4 us -> 44.6 us  [exchange(): return lax.all_to_all(array, axes, split_axis=0, concat_axis=0, tiled=True)]
  transfers between devices with their start and end apart: 10 -> 10, of which waited for: 6 -> 7; matrix products, arithmetic and copies ran while one was open for 1% -> 1% of each run, Pallas kernels for 24% -> 5%
where the time goes in v5:
time: 132 us; the launch traced here: 131 us
  waiting for transfers between devices  58.7 us (44%)
  starting transfers between devices  56.7 us (43%)
  Pallas kernels  13.1 us (10%)
    all_to_all x4, waiting for transfers between devices, exchange(): return lax.all_to_all(array, axes, split_axis=0, concat_axis=0, tiled=True)  51.2 us
    all_to_all x4, starting transfers between devices, exchange(): return lax.all_to_all(array, axes, split_axis=0, concat_axis=0, tiled=True)  44.6 us
    pallas_call x9, Pallas kernels, call(): pl.pallas_call(kernel, out_shape=[pltpu.HBM(shape, kind) if n in far_outs...  13.1 us
    ppermute x5, starting transfers between devices, swap(): return lax.ppermute(array, 'core', [(0, 1), (1, 0)])  9.81 us
    ppermute x1, waiting for transfers between devices, body(): lax.ppermute(held, 'y', [(n, n ^ p) for n in range(8)])  5.25 us
  transfers between devices with their start and end apart: 10, of which 7 were waited for; matrix products, arithmetic and copies ran while one was open for 1% of the time, Pallas kernels for 5%

profile of v5, /device:TPU:16, one launch (start us, length us, event | category | flops | bytes accessed | tf_op | source)
XLA Modules:
  0.0 130.8 jit_solution(440556101314813940)
XLA Ops:
  0.7 1.7 %shard_map.111 = bf16[16,96,128]{2,1,0:T(8,128)(2,1)} custom-call(bf16[16,32,128]{2,1,0:T(8,128)(2,1)} %bitcast.5, bf16[128,1024]{1,0:T(8,128)(2,1)} %key_ref.1, bf16[128,1024]{1,0:T(8,128)(2,1)} %value_ref.1), custom_call_target="tpu_custom_call" | custom-call | tf_op jit(solution)/shard_map/pallas_call | solution.py:41
  2.4 20.0 %all-to-all-start = ((bf16[16,96,128]{2,1,0:T(8,128)(2,1)}), bf16[16,96,128]{2,1,0:T(8,128)(2,1)S(1)}, u32[]{:S(2)}, u32[]{:S(2)}) async-start(bf16[16,96,128]{2,1,0:T(8,128)(2,1)} %shard_map.111), calls=%async_computation | async-start | bytes 786432 | tf_op jit(solution)/shard_map/all_to_all | solution.py:282
  22.4 0.8 copy.12.index_ref
  23.2 0.4 shard_map.112.onehot_ref
  23.6 0.1 copy.13.combine_ref
  23.7 15.0 %all-to-all-done.pack_ref = bf16[16,96,128]{2,1,0:T(8,128)(2,1)S(1)} async-done(((bf16[16,96,128]{2,1,0:T(8,128)(2,1)}), bf16[16,96,128]{2,1,0:T(8,128)(2,1)S(1)}, u32[]{:S(2)}, u32[]{:S(2)}) %all-to-all-start) | async-done | bytes 393248 | tf_op jit(solution)/shard_map/all_to_all | solution.py:282
  38.7 1.9 %shard_map.113 = (bf16[128,128]{1,0:T(8,128)(2,1)}, bf16[32,128,128]{2,1,0:T(8,128)(2,1)}) custom-call(bf16[128,128]{1,0:T(8,128)(2,1)S(1)} %copy-done.1, bf16[16,96,128]{2,1,0:T(8,128)(2,1)S(1)} %all-to-all-done.pack_ref, bf16[256,512]{1,0:T(8,128)(2,1)S(1)} %shard_map.112.onehot_ref, f32[128,2]{1,0:T(8,128)S(1)} %copy.13.combine_ref), custom_call_target="tpu_custom_call" | custom-call | tf_op jit(solution)/shard_map/pallas_call | solution.py:41
  40.6 0.0 copy-start
  40.6 12.6 %all-to-all-start.1 = ((bf16[32,128,128]{2,1,0:T(8,128)(2,1)}), bf16[32,128,128]{2,1,0:T(8,128)(2,1)S(1)}, u32[]{:S(2)}, u32[]{:S(2)}) async-start(bf16[32,128,128]{2,1,0:T(8,128)(2,1)} %get-tuple-element.16), calls=%async_computation.1 | async-start | bytes 2097152 | tf_op jit(solution)/shard_map/all_to_all | solution.py:282
  53.2 3.0 %shard_map.114 = (bf16[128,4096]{1,0:T(8,128)(2,1)}, bf16[128,4096]{1,0:T(8,128)(2,1)}) custom-call(bf16[128,8192]{1,0:T(8,128)(2,1)} %weight_ref.1), custom_call_target="tpu_custom_call" | custom-call | tf_op jit(solution)/shard_map/pallas_call | solution.py:41
  56.3 1.9 %collective-permute-start = (bf16[128,4096]{1,0:T(8,128)(2,1)}, bf16[128,4096]{1,0:T(8,128)(2,1)}, u32[]{:S(2)}, u32[]{:S(2)}) collective-permute-start(bf16[128,4096]{1,0:T(8,128)(2,1)} %get-tuple-element.18), channel_id=1, source_target_pairs={{0,1},{1,0},{2,3},{3,2},{4,5},{5,4},{6,7},{7,6},{8,9},{9,8},{10,11... | collective-permute-start | bytes 3145736 | tf_op jit(solution)/shard_map/ppermute | solution.py:278
  58.2 2.2 %collective-permute-start.3 = (bf16[16,64,128]{2,1,0:T(8,128)(2,1)S(1)}, bf16[16,64,128]{2,1,0:T(8,128)(2,1)S(1)}, u32[]{:S(2)}, u32[]{:S(2)}) collective-permute-start(bf16[16,64,128]{2,1,0:T(8,128)(2,1)S(1)} %slice.4), channel_id=1, source_target_pairs={{0,64},{64,0},{128,192},{192,128},{256,320},{320,256},{384,448},{4... | collective-permute-start | bytes 786440 | tf_op jit(solution)/shard_map/ppermute | solution.py:328
  60.5 2.1 %collective-permute-start.2 = (bf16[128,128]{1,0:T(8,128)(2,1)S(1)}, bf16[128,128]{1,0:T(8,128)(2,1)S(1)}, u32[]{:S(2)}, u32[]{:S(2)}) collective-permute-start(bf16[128,128]{1,0:T(8,128)(2,1)S(1)} %copy-done), channel_id=1, source_target_pairs={{0,1},{1,0},{2,3},{3,2},{4,5},{5,4},{6,7},{7,6},{8,9},{9,8},{10,11... | collective-permute-start | bytes 98312 | tf_op jit(solution)/shard_map/ppermute | solution.py:278
  62.6 1.0 collective-permute-done.2.mate_ref
  63.6 5.2 %collective-permute-done.3.refs_0_ = bf16[16,64,128]{2,1,0:T(8,128)(2,1)S(1)} collective-permute-done((bf16[16,64,128]{2,1,0:T(8,128)(2,1)S(1)}, bf16[16,64,128]{2,1,0:T(8,128)(2,1)S(1)}, u32[]{:S(2)}, u32[]{:S(2)}) %collective-permute-start.3) | collective-permute-done | bytes 262176 | tf_op jit(solution)/shard_map/ppermute | solution.py:328
  68.8 0.8 shard_map.116
  69.6 1.9 %collective-permute-start.4 = (f32[256,256]{1,0:T(8,128)S(1)}, f32[256,256]{1,0:T(8,128)S(1)}, u32[]{:S(2)}, u32[]{:S(2)}) collective-permute-start(f32[256,256]{1,0:T(8,128)S(1)} %get-tuple-element.20.stat_ref), channel_id=1, source_target_pairs={{0,1},{1,0},{2,3},{3,2},{4,5},{5,4},{6,7},{7,6},{8,9},{9,8},{10,11... | collective-permute-start | bytes 786440 | tf_op jit(solution)/shard_map/ppermute | solution.py:278
  71.6 8.6 %all-to-all-done.1.blocks_ref = bf16[32,128,128]{2,1,0:T(8,128)(2,1)S(1)} async-done(((bf16[32,128,128]{2,1,0:T(8,128)(2,1)}), bf16[32,128,128]{2,1,0:T(8,128)(2,1)S(1)}, u32[]{:S(2)}, u32[]{:S(2)}) %all-to-all-start.1) | async-done | bytes 1048608 | tf_op jit(solution)/shard_map/all_to_all | solution.py:282
  80.2 2.1 %shard_map.115.part_ref = f32[128,256]{1,0:T(8,128)S(1)} custom-call(bf16[32,128,128]{2,1,0:T(8,128)(2,1)S(1)} %all-to-all-done.1.blocks_ref, bf16[128,4096]{1,0:T(8,128)(2,1)} %get-tuple-element.17.own_ref, bf16[128,4096]{1,0:T(8,128)(2,1)} %collective-permute-done.mate_ref), custom_call_target="tpu_custom_call" | custom-call | tf_op jit(solution)/shard_map/pallas_call | solution.py:41
  82.3 1.9 %collective-permute-start.1 = (f32[128,256]{1,0:T(8,128)S(1)}, f32[128,256]{1,0:T(8,128)S(1)}, u32[]{:S(2)}, u32[]{:S(2)}) collective-permute-start(f32[128,256]{1,0:T(8,128)S(1)} %shard_map.115.part_ref), channel_id=1, source_target_pairs={{0,1},{1,0},{2,3},{3,2},{4,5},{5,4},{6,7},{7,6},{8,9},{9,8},{10,11... | collective-permute-start | bytes 393224 | tf_op jit(solution)/shard_map/ppermute | solution.py:278
  84.2 0.0 collective-permute-done.4.seen_ref
  84.2 1.3 collective-permute-done.1.other_ref
  85.5 1.7 %shard_map.117 = (bf16[8,2,2,32,256]{4,3,2,1,0:T(8,128)(2,1)}, f32[128,128]{1,0:T(8,128)S(1)}, f32[128,128]{1,0:T(8,128)S(1)}) custom-call(f32[128,256]{1,0:T(8,128)S(1)} %shard_map.115.part_ref, f32[128,256]{1,0:T(8,128)S(1)} %collective-permute-done.1.other_ref, bf16[128,128]{1,0:T(8,128)(2,1)S(1)} %copy-done, ...), custom_call_target="tpu_custom_call" | custom-call | tf_op jit(solution)/shard_map/pallas_call | solution.py:41
  87.2 6.6 %all-to-all-start.2 = ((bf16[32,32,256]{2,1,0:T(8,128)(2,1)}), bf16[32,32,256]{2,1,0:T(8,128)(2,1)S(1)}, u32[]{:S(2)}, u32[]{:S(2)}) async-start(bf16[32,32,256]{2,1,0:T(8,128)(2,1)} %bitcast.1), calls=%async_computation.2 | async-start | bytes 1048576 | tf_op jit(solution)/shard_map/all_to_all | solution.py:282
  93.8 1.9 %collective-permute-start.5 = (f32[128,128]{1,0:T(8,128)S(1)}, f32[128,128]{1,0:T(8,128)S(1)}, u32[]{:S(2)}, u32[]{:S(2)}) collective-permute-start(f32[128,128]{1,0:T(8,128)S(1)} %get-tuple-element.22), channel_id=1, source_target_pairs={{0,1},{1,0},{2,3},{3,2},{4,5},{5,4},{6,7},{7,6},{8,9},{9,8},{10,11... | collective-permute-start | bytes 196616 | tf_op jit(solution)/shard_map/ppermute | solution.py:278
  95.7 15.8 %all-to-all-done.2.parts_ref = bf16[32,32,256]{2,1,0:T(8,128)(2,1)S(1)} async-done(((bf16[32,32,256]{2,1,0:T(8,128)(2,1)}), bf16[32,32,256]{2,1,0:T(8,128)(2,1)S(1)}, u32[]{:S(2)}, u32[]{:S(2)}) %all-to-all-start.2) | async-done | bytes 524320 | tf_op jit(solution)/shard_map/all_to_all | solution.py:282
  111.5 0.8 shard_map.118
  112.3 5.5 %all-to-all-start.3 = ((bf16[16,4,128]{2,1,0:T(4,128)(2,1)}), bf16[16,4,128]{2,1,0:T(4,128)(2,1)S(1)}, u32[]{:S(2)}, u32[]{:S(2)}) async-start(bf16[16,4,128]{2,1,0:T(4,128)(2,1)} %bitcast.2), calls=%async_computation.3 | async-start | bytes 32768 | tf_op jit(solution)/shard_map/all_to_all | solution.py:282
  117.8 0.0 collective-permute-done.5
  117.8 0.6 add_convert_fusion
  118.4 11.8 %all-to-all-done.3 = bf16[16,4,128]{2,1,0:T(4,128)(2,1)S(1)} async-done(((bf16[16,4,128]{2,1,0:T(4,128)(2,1)}), bf16[16,4,128]{2,1,0:T(4,128)(2,1)S(1)}, u32[]{:S(2)}, u32[]{:S(2)}) %all-to-all-start.3) | async-done | bytes 16416 | tf_op jit(solution)/shard_map/all_to_all | solution.py:282
  130.2 0.6 shard_map.119
  (7 shorter events, 0.0 us)
Async XLA Ops:
  0.6 23.0 %copy-start.2 = (f32[128,2]{0,1:T(2,128)S(1)}, f32[128,2]{0,1:T(2,128)}, u32[]{:S(2)}) copy-start(f32[128,2]{0,1:T(2,128)} %param.11) | copy-start | bytes 3076
  0.6 38.1 %copy-start.1 = (bf16[128,128]{1,0:T(8,128)(2,1)S(1)}, bf16[128,128]{1,0:T(8,128)(2,1)}, u32[]{:S(2)}) copy-start(bf16[128,128]{1,0:T(8,128)(2,1)} %grad_ref.1) | copy-start | bytes 98308
  2.4 36.3 %all-to-all-start = ((bf16[16,96,128]{2,1,0:T(8,128)(2,1)}), bf16[16,96,128]{2,1,0:T(8,128)(2,1)S(1)}, u32[]{:S(2)}, u32[]{:S(2)}) async-start(bf16[16,96,128]{2,1,0:T(8,128)(2,1)} %shard_map.111), calls=%async_computation | async-start | bytes 786432 | tf_op jit(solution)/shard_map/all_to_all | solution.py:282
  40.6 19.9 %copy-start = (bf16[128,128]{1,0:T(8,128)(2,1)S(1)}, bf16[128,128]{1,0:T(8,128)(2,1)}, u32[]{:S(2)}) copy-start(bf16[128,128]{1,0:T(8,128)(2,1)} %query_ref.3) | copy-start | bytes 98308
  40.6 39.6 %all-to-all-start.1 = ((bf16[32,128,128]{2,1,0:T(8,128)(2,1)}), bf16[32,128,128]{2,1,0:T(8,128)(2,1)S(1)}, u32[]{:S(2)}, u32[]{:S(2)}) async-start(bf16[32,128,128]{2,1,0:T(8,128)(2,1)} %get-tuple-element.16), calls=%async_computation.1 | async-start | bytes 2097152 | tf_op jit(solution)/shard_map/all_to_all | solution.py:282
  56.3 15.3 %collective-permute-start = (bf16[128,4096]{1,0:T(8,128)(2,1)}, bf16[128,4096]{1,0:T(8,128)(2,1)}, u32[]{:S(2)}, u32[]{:S(2)}) collective-permute-start(bf16[128,4096]{1,0:T(8,128)(2,1)} %get-tuple-element.18), channel_id=1, source_target_pairs={{0,1},{1,0},{2,3},{3,2},{4,5},{5,4},{6,7},{7,6},{8,9},{9,8},{10,11... | collective-permute-start | bytes 3145736 | tf_op jit(solution)/shard_map/ppermute | solution.py:278
  58.2 10.6 %collective-permute-start.3 = (bf16[16,64,128]{2,1,0:T(8,128)(2,1)S(1)}, bf16[16,64,128]{2,1,0:T(8,128)(2,1)S(1)}, u32[]{:S(2)}, u32[]{:S(2)}) collective-permute-start(bf16[16,64,128]{2,1,0:T(8,128)(2,1)S(1)} %slice.4), channel_id=1, source_target_pairs={{0,64},{64,0},{128,192},{192,128},{256,320},{320,256},{384,448},{4... | collective-permute-start | bytes 786440 | tf_op jit(solution)/shard_map/ppermute | solution.py:328
  60.5 3.1 %collective-permute-start.2 = (bf16[128,128]{1,0:T(8,128)(2,1)S(1)}, bf16[128,128]{1,0:T(8,128)(2,1)S(1)}, u32[]{:S(2)}, u32[]{:S(2)}) collective-permute-start(bf16[128,128]{1,0:T(8,128)(2,1)S(1)} %copy-done), channel_id=1, source_target_pairs={{0,1},{1,0},{2,3},{3,2},{4,5},{5,4},{6,7},{7,6},{8,9},{9,8},{10,11... | collective-permute-start | bytes 98312 | tf_op jit(solution)/shard_map/ppermute | solution.py:278
  69.6 14.6 %collective-permute-start.4 = (f32[256,256]{1,0:T(8,128)S(1)}, f32[256,256]{1,0:T(8,128)S(1)}, u32[]{:S(2)}, u32[]{:S(2)}) collective-permute-start(f32[256,256]{1,0:T(8,128)S(1)} %get-tuple-element.20.stat_ref), channel_id=1, source_target_pairs={{0,1},{1,0},{2,3},{3,2},{4,5},{5,4},{6,7},{7,6},{8,9},{9,8},{10,11... | collective-permute-start | bytes 786440 | tf_op jit(solution)/shard_map/ppermute | solution.py:278
  82.3 3.2 %collective-permute-start.1 = (f32[128,256]{1,0:T(8,128)S(1)}, f32[128,256]{1,0:T(8,128)S(1)}, u32[]{:S(2)}, u32[]{:S(2)}) collective-permute-start(f32[128,256]{1,0:T(8,128)S(1)} %shard_map.115.part_ref), channel_id=1, source_target_pairs={{0,1},{1,0},{2,3},{3,2},{4,5},{5,4},{6,7},{7,6},{8,9},{9,8},{10,11... | collective-permute-start | bytes 393224 | tf_op jit(solution)/shard_map/ppermute | solution.py:278
  87.2 24.2 %all-to-all-start.2 = ((bf16[32,32,256]{2,1,0:T(8,128)(2,1)}), bf16[32,32,256]{2,1,0:T(8,128)(2,1)S(1)}, u32[]{:S(2)}, u32[]{:S(2)}) async-start(bf16[32,32,256]{2,1,0:T(8,128)(2,1)} %bitcast.1), calls=%async_computation.2 | async-start | bytes 1048576 | tf_op jit(solution)/shard_map/all_to_all | solution.py:282
  93.8 24.0 %collective-permute-start.5 = (f32[128,128]{1,0:T(8,128)S(1)}, f32[128,128]{1,0:T(8,128)S(1)}, u32[]{:S(2)}, u32[]{:S(2)}) collective-permute-start(f32[128,128]{1,0:T(8,128)S(1)} %get-tuple-element.22), channel_id=1, source_target_pairs={{0,1},{1,0},{2,3},{3,2},{4,5},{5,4},{6,7},{7,6},{8,9},{9,8},{10,11... | collective-permute-start | bytes 196616 | tf_op jit(solution)/shard_map/ppermute | solution.py:278
  112.3 17.9 %all-to-all-start.3 = ((bf16[16,4,128]{2,1,0:T(4,128)(2,1)}), bf16[16,4,128]{2,1,0:T(4,128)(2,1)S(1)}, u32[]{:S(2)}, u32[]{:S(2)}) async-start(bf16[16,4,128]{2,1,0:T(4,128)(2,1)} %bitcast.2), calls=%async_computation.3 | async-start | bytes 32768 | tf_op jit(solution)/shard_map/all_to_all | solution.py:282

commit v6 on v5

--- a/solution.py
+++ b/solution.py
@@ -23,7 +23,7 @@
 N_PEERS = 32
 HALF = 64
 KEYS = N_CTX * HALF
-SPLIT = 2
+SPLIT = 4
 SHARE = HALF // SPLIT
 PACK = CAP + 2 * SHARE
 F32 = jnp.float32
@@ -37,14 +37,15 @@
     return pltpu.with_memory_space_constraint(array, pltpu.HBM)
 
 
-def call(kernel, outs, *operands, far=(), far_outs=(), scratch=()):
+def call(kernel, outs, *operands, far=(), free=(), far_outs=(), scratch=()):
+    spaces = {n: HBM for n in far} | {n: pl.BlockSpec(memory_space=pl.ANY) for n in free}
     return pl.pallas_call(
         kernel,
         out_shape=[
             pltpu.HBM(shape, kind) if n in far_outs else jax.ShapeDtypeStruct(shape, kind)
             for n, (shape, kind) in enumerate(outs)
         ],
-        in_specs=[HBM if n in far else VMEM for n in range(len(operands))],
+        in_specs=[spaces.get(n, VMEM) for n in range(len(operands))],
         out_specs=[HBM if n in far_outs else VMEM for n in range(len(outs))],
         scratch_shapes=scratch,
         compiler_params=PARAMS,
@@ -116,7 +117,7 @@
     store.wait()
 
 
-def weight_kernel(weight_ref, own_ref, send_ref, whole, parted, sems):
+def weight_kernel(weight_ref, own_ref, send_ref, token_ref, whole, parted, sems):
     core = lax.axis_index("core")
     span = 8
     loads = [
@@ -140,6 +141,7 @@
         pltpu.make_async_copy(parted.at[1], send_ref, sems.at[5]),
     ]
     start_all(stores)
+    token_ref[...] = jnp.zeros_like(token_ref)
     wait_all(stores)
 
 
@@ -157,20 +159,24 @@
         out_ref[k * ROWS : (k + 1) * ROWS] = wide.astype(BF16)
 
 
-def residual_kernel(grad_ref, pack_ref, onehot_ref, combine_ref, out_ref, send_ref, copied, sems):
+def residual_kernel(
+    grad_ref, pack_ref, onehot_ref, combine_ref, _token, out_ref, send_ref, copied, sems
+):
     rows = pack_ref[:, :CAP].reshape(EXPERTS * CAP, HD)
     picked = dot(onehot_ref[...], rows, (1, 0))
     combine = combine_ref[...]
     moe = combine[:, 0:1] * picked[:ROWS] + combine[:, 1:2] * picked[ROWS:]
     residual = (grad_ref[...].astype(F32) + moe).astype(BF16)
-    span = copied.shape[0]
-    for b in range(span):
-        copied[b] = residual
-    copies = [
-        pltpu.make_async_copy(copied, send_ref.at[a : a + span], sems.at[a // span])
-        for a in range(0, N_PEERS, span)
-    ]
-    start_all(copies)
+    span = 8
+    copies = []
+    for a in range(0, N_PEERS, span):
+        for b in range(a, a + span):
+            copied[b] = residual
+        copy = pltpu.make_async_copy(
+            copied.at[a : a + span], send_ref.at[a : a + span], sems.at[a // span]
+        )
+        copy.start()
+        copies.append(copy)
     out_ref[...] = residual
     wait_all(copies)
 
@@ -299,9 +305,9 @@
         ],
     )
     received = exchange(packed, CTX)
-    own_weight, send_weight = call(
+    own_weight, send_weight, token = call(
         weight_kernel,
-        [((ROWS, N_PEERS * HD), BF16)] * 2,
+        [((ROWS, N_PEERS * HD), BF16)] * 2 + [((8, HD), F32)],
         out_weight,
         far=(0,),
         far_outs=(0, 1),
@@ -321,8 +327,10 @@
         received,
         onehot,
         combine,
+        token,
+        free=(4,),
         far_outs=(1,),
-        scratch=[pltpu.VMEM((8, ROWS, HD), BF16), pltpu.SemaphoreType.DMA((4,))],
+        scratch=[pltpu.VMEM((N_PEERS, ROWS, HD), BF16), pltpu.SemaphoreType.DMA((4,))],
     )
     held = received[:, CAP:]
     near = [lax.ppermute(held, "y", [(n, n ^ p) for n in range(8)]) for p in range(1, SPLIT)]

time: 132 us -> 129 us (0.977)
  waiting for transfers between devices: 58.7 us -> 49.3 us
  starting transfers between devices: 56.7 us -> 62.9 us
    all_to_all x4, waiting for transfers between devices: 51.2 us -> 40 us  [exchange(): return lax.all_to_all(array, axes, split_axis=0, concat_axis=0, tiled=True)]
    ppermute x1 -> x3, starting transfers between devices: 2.23 us -> 9.21 us  [body(): lax.ppermute(held, 'y', [(n, n ^ p) for n in range(8)])]
    ppermute x1 -> x3, waiting for transfers between devices: 5.25 us -> 6.87 us  [body(): lax.ppermute(held, 'y', [(n, n ^ p) for n in range(8)])]
  transfers between devices with their start and end apart: 10 -> 12, of which waited for: 7 -> 8; matrix products, arithmetic and copies ran while one was open for 1% -> 2% of each run, Pallas kernels for 5% -> 6%
where the time goes in v6:
time: 129 us; the launch traced here: 128 us
  starting transfers between devices  62.9 us (49%)
  waiting for transfers between devices  49.3 us (38%)
  Pallas kernels  13 us (10%)
  local copies, waits for them, and re-layouts  1.59 us (1%)
    all_to_all x4, starting transfers between devices, exchange(): return lax.all_to_all(array, axes, split_axis=0, concat_axis=0, tiled=True)  44.1 us
    all_to_all x4, waiting for transfers between devices, exchange(): return lax.all_to_all(array, axes, split_axis=0, concat_axis=0, tiled=True)  40 us
    pallas_call x9, Pallas kernels, call(): pl.pallas_call(kernel, out_shape=[pltpu.HBM(shape, kind) if n in far_outs...  13 us
    ppermute x5, starting transfers between devices, swap(): return lax.ppermute(array, 'core', [(0, 1), (1, 0)])  9.6 us
    ppermute x3, starting transfers between devices, body(): lax.ppermute(held, 'y', [(n, n ^ p) for n in range(8)])  9.21 us
    ppermute x3, waiting for transfers between devices, body(): lax.ppermute(held, 'y', [(n, n ^ p) for n in range(8)])  6.87 us
  transfers between devices with their start and end apart: 12, of which 8 were waited for; matrix products, arithmetic and copies ran while one was open for 2% of the time, Pallas kernels for 6%

profile of v6, /device:TPU:16, one launch (start us, length us, event | category | flops | bytes accessed | tf_op | source)
XLA Modules:
  0.0 128.3 jit_solution(13961270669228470525)
XLA Ops:
  0.6 1.7 %shard_map.111 = bf16[16,64,128]{2,1,0:T(8,128)(2,1)} custom-call(bf16[16,32,128]{2,1,0:T(8,128)(2,1)} %bitcast.5, bf16[128,1024]{1,0:T(8,128)(2,1)} %key_ref.1, bf16[128,1024]{1,0:T(8,128)(2,1)} %value_ref.1), custom_call_target="tpu_custom_call" | custom-call | tf_op jit(solution)/shard_map/pallas_call | solution.py:42
  2.3 20.0 %all-to-all-start = ((bf16[16,64,128]{2,1,0:T(8,128)(2,1)}), bf16[16,64,128]{2,1,0:T(8,128)(2,1)S(1)}, u32[]{:S(2)}, u32[]{:S(2)}) async-start(bf16[16,64,128]{2,1,0:T(8,128)(2,1)} %shard_map.111), calls=%async_computation | async-start | bytes 524288 | tf_op jit(solution)/shard_map/all_to_all | solution.py:288
  22.3 0.8 copy.12.index_ref
  23.1 0.4 shard_map.112.onehot_ref
  23.6 0.8 copy.13.combine_ref
  24.4 3.0 %shard_map.113 = (bf16[128,4096]{1,0:T(8,128)(2,1)}, bf16[128,4096]{1,0:T(8,128)(2,1)}, f32[8,128]{1,0:T(8,128)S(1)}) custom-call(bf16[128,8192]{1,0:T(8,128)(2,1)} %weight_ref.1), custom_call_target="tpu_custom_call" | custom-call | tf_op jit(solution)/shard_map/pallas_call | solution.py:42
  27.4 8.9 %all-to-all-done.pack_ref = bf16[16,64,128]{2,1,0:T(8,128)(2,1)S(1)} async-done(((bf16[16,64,128]{2,1,0:T(8,128)(2,1)}), bf16[16,64,128]{2,1,0:T(8,128)(2,1)S(1)}, u32[]{:S(2)}, u32[]{:S(2)}) %all-to-all-start) | async-done | bytes 262176 | tf_op jit(solution)/shard_map/all_to_all | solution.py:288
  36.3 1.9 %shard_map.114 = (bf16[128,128]{1,0:T(8,128)(2,1)}, bf16[32,128,128]{2,1,0:T(8,128)(2,1)}) custom-call(bf16[128,128]{1,0:T(8,128)(2,1)S(1)} %copy-done.1, bf16[16,64,128]{2,1,0:T(8,128)(2,1)S(1)} %all-to-all-done.pack_ref, bf16[256,512]{1,0:T(8,128)(2,1)S(1)} %shard_map.112.onehot_ref, f32[128,2]{1,0:T(8,128)S(1)} %copy.13.combine_ref, ...), custom_call_target="tpu_custom_call" | custom-call | tf_op jit(solution)/shard_map/pallas_call | solution.py:42
  38.2 12.6 %all-to-all-start.1 = ((bf16[32,128,128]{2,1,0:T(8,128)(2,1)}), bf16[32,128,128]{2,1,0:T(8,128)(2,1)S(1)}, u32[]{:S(2)}, u32[]{:S(2)}) async-start(bf16[32,128,128]{2,1,0:T(8,128)(2,1)} %get-tuple-element.18), calls=%async_computation.1 | async-start | bytes 2097152 | tf_op jit(solution)/shard_map/all_to_all | solution.py:288
  50.8 1.9 %collective-permute-start = (bf16[128,4096]{1,0:T(8,128)(2,1)}, bf16[128,4096]{1,0:T(8,128)(2,1)}, u32[]{:S(2)}, u32[]{:S(2)}) collective-permute-start(bf16[128,4096]{1,0:T(8,128)(2,1)} %get-tuple-element.20), channel_id=1, source_target_pairs={{0,1},{1,0},{2,3},{3,2},{4,5},{5,4},{6,7},{7,6},{8,9},{9,8},{10,11... | collective-permute-start | bytes 3145736 | tf_op jit(solution)/shard_map/ppermute | solution.py:284
  52.7 2.1 %collective-permute-start.3 = (bf16[16,32,128]{2,1,0:T(8,128)(2,1)S(1)}, bf16[16,32,128]{2,1,0:T(8,128)(2,1)S(1)}, u32[]{:S(2)}, u32[]{:S(2)}) collective-permute-start(bf16[16,32,128]{2,1,0:T(8,128)(2,1)S(1)} %slice.4), channel_id=1, source_target_pairs={{0,64},{64,0},{128,192},{192,128},{256,320},{320,256},{384,448},{4... | collective-permute-start | bytes 393224 | tf_op jit(solution)/shard_map/ppermute | solution.py:336
  54.8 4.1 %collective-permute-start.4 = (bf16[16,32,128]{2,1,0:T(8,128)(2,1)S(1)}, bf16[16,32,128]{2,1,0:T(8,128)(2,1)S(1)}, u32[]{:S(2)}, u32[]{:S(2)}) collective-permute-start(bf16[16,32,128]{2,1,0:T(8,128)(2,1)S(1)} %slice.4), channel_id=1, source_target_pairs={{0,128},{64,192},{128,0},{192,64},{256,384},{320,448},{384,256},{4... | collective-permute-start | bytes 393224 | tf_op jit(solution)/shard_map/ppermute | solution.py:336
  58.9 3.0 %collective-permute-start.5 = (bf16[16,32,128]{2,1,0:T(8,128)(2,1)S(1)}, bf16[16,32,128]{2,1,0:T(8,128)(2,1)S(1)}, u32[]{:S(2)}, u32[]{:S(2)}) collective-permute-start(bf16[16,32,128]{2,1,0:T(8,128)(2,1)S(1)} %slice.4), channel_id=1, source_target_pairs={{0,192},{64,128},{128,64},{192,0},{256,448},{320,384},{384,320},{4... | collective-permute-start | bytes 393224 | tf_op jit(solution)/shard_map/ppermute | solution.py:336
  62.0 1.9 %collective-permute-start.2 = (bf16[128,128]{1,0:T(8,128)(2,1)S(1)}, bf16[128,128]{1,0:T(8,128)(2,1)S(1)}, u32[]{:S(2)}, u32[]{:S(2)}) collective-permute-start(bf16[128,128]{1,0:T(8,128)(2,1)S(1)} %copy-done), channel_id=1, source_target_pairs={{0,1},{1,0},{2,3},{3,2},{4,5},{5,4},{6,7},{7,6},{8,9},{9,8},{10,11... | collective-permute-start | bytes 98312 | tf_op jit(solution)/shard_map/ppermute | solution.py:284
  63.9 1.2 collective-permute-done.2.mate_ref
  65.1 2.9 %collective-permute-done.4.refs_1_ = bf16[16,32,128]{2,1,0:T(8,128)(2,1)S(1)} collective-permute-done((bf16[16,32,128]{2,1,0:T(8,128)(2,1)S(1)}, bf16[16,32,128]{2,1,0:T(8,128)(2,1)S(1)}, u32[]{:S(2)}, u32[]{:S(2)}) %collective-permute-start.4) | collective-permute-done | bytes 131104 | tf_op jit(solution)/shard_map/ppermute | solution.py:336
  68.0 4.0 %collective-permute-done.5.refs_2_ = bf16[16,32,128]{2,1,0:T(8,128)(2,1)S(1)} collective-permute-done((bf16[16,32,128]{2,1,0:T(8,128)(2,1)S(1)}, bf16[16,32,128]{2,1,0:T(8,128)(2,1)S(1)}, u32[]{:S(2)}, u32[]{:S(2)}) %collective-permute-start.5) | collective-permute-done | bytes 131104 | tf_op jit(solution)/shard_map/ppermute | solution.py:336
  72.0 0.8 shard_map.116
  72.8 1.9 %collective-permute-start.6 = (f32[256,256]{1,0:T(8,128)S(1)}, f32[256,256]{1,0:T(8,128)S(1)}, u32[]{:S(2)}, u32[]{:S(2)}) collective-permute-start(f32[256,256]{1,0:T(8,128)S(1)} %get-tuple-element.22.stat_ref), channel_id=1, source_target_pairs={{0,1},{1,0},{2,3},{3,2},{4,5},{5,4},{6,7},{7,6},{8,9},{9,8},{10,11... | collective-permute-start | bytes 786440 | tf_op jit(solution)/shard_map/ppermute | solution.py:284
  74.7 3.5 %all-to-all-done.1.blocks_ref = bf16[32,128,128]{2,1,0:T(8,128)(2,1)S(1)} async-done(((bf16[32,128,128]{2,1,0:T(8,128)(2,1)}), bf16[32,128,128]{2,1,0:T(8,128)(2,1)S(1)}, u32[]{:S(2)}, u32[]{:S(2)}) %all-to-all-start.1) | async-done | bytes 1048608 | tf_op jit(solution)/shard_map/all_to_all | solution.py:288
  78.2 2.1 %shard_map.115.part_ref = f32[128,256]{1,0:T(8,128)S(1)} custom-call(bf16[32,128,128]{2,1,0:T(8,128)(2,1)S(1)} %all-to-all-done.1.blocks_ref, bf16[128,4096]{1,0:T(8,128)(2,1)} %get-tuple-element.19.own_ref, bf16[128,4096]{1,0:T(8,128)(2,1)} %collective-permute-done.mate_ref), custom_call_target="tpu_custom_call" | custom-call | tf_op jit(solution)/shard_map/pallas_call | solution.py:42
  80.3 1.9 %collective-permute-start.1 = (f32[128,256]{1,0:T(8,128)S(1)}, f32[128,256]{1,0:T(8,128)S(1)}, u32[]{:S(2)}, u32[]{:S(2)}) collective-permute-start(f32[128,256]{1,0:T(8,128)S(1)} %shard_map.115.part_ref), channel_id=1, source_target_pairs={{0,1},{1,0},{2,3},{3,2},{4,5},{5,4},{6,7},{7,6},{8,9},{9,8},{10,11... | collective-permute-start | bytes 393224 | tf_op jit(solution)/shard_map/ppermute | solution.py:284
  82.3 1.3 %collective-permute-done.1.other_ref = f32[128,256]{1,0:T(8,128)S(1)} collective-permute-done((f32[128,256]{1,0:T(8,128)S(1)}, f32[128,256]{1,0:T(8,128)S(1)}, u32[]{:S(2)}, u32[]{:S(2)}) %collective-permute-start.1) | collective-permute-done | bytes 131104 | tf_op jit(solution)/shard_map/ppermute | solution.py:284
  83.6 1.7 %shard_map.117 = (bf16[8,4,1,32,256]{4,3,2,1,0:T(8,128)(2,1)}, f32[128,128]{1,0:T(8,128)S(1)}, f32[128,128]{1,0:T(8,128)S(1)}) custom-call(f32[128,256]{1,0:T(8,128)S(1)} %shard_map.115.part_ref, f32[128,256]{1,0:T(8,128)S(1)} %collective-permute-done.1.other_ref, bf16[128,128]{1,0:T(8,128)(2,1)S(1)} %copy-done, ...), custom_call_target="tpu_custom_call" | custom-call | tf_op jit(solution)/shard_map/pallas_call | solution.py:42
  85.3 6.2 %all-to-all-start.2 = ((bf16[32,32,256]{2,1,0:T(8,128)(2,1)}), bf16[32,32,256]{2,1,0:T(8,128)(2,1)S(1)}, u32[]{:S(2)}, u32[]{:S(2)}) async-start(bf16[32,32,256]{2,1,0:T(8,128)(2,1)} %bitcast.1), calls=%async_computation.2 | async-start | bytes 1048576 | tf_op jit(solution)/shard_map/all_to_all | solution.py:288
  91.4 1.9 %collective-permute-start.7 = (f32[128,128]{1,0:T(8,128)S(1)}, f32[128,128]{1,0:T(8,128)S(1)}, u32[]{:S(2)}, u32[]{:S(2)}) collective-permute-start(f32[128,128]{1,0:T(8,128)S(1)} %get-tuple-element.24), channel_id=1, source_target_pairs={{0,1},{1,0},{2,3},{3,2},{4,5},{5,4},{6,7},{7,6},{8,9},{9,8},{10,11... | collective-permute-start | bytes 196616 | tf_op jit(solution)/shard_map/ppermute | solution.py:284
  93.4 15.8 %all-to-all-done.2.parts_ref = bf16[32,32,256]{2,1,0:T(8,128)(2,1)S(1)} async-done(((bf16[32,32,256]{2,1,0:T(8,128)(2,1)}), bf16[32,32,256]{2,1,0:T(8,128)(2,1)S(1)}, u32[]{:S(2)}, u32[]{:S(2)}) %all-to-all-start.2) | async-done | bytes 524320 | tf_op jit(solution)/shard_map/all_to_all | solution.py:288
  109.1 0.8 shard_map.118
  109.9 5.3 %all-to-all-start.3 = ((bf16[16,4,128]{2,1,0:T(4,128)(2,1)}), bf16[16,4,128]{2,1,0:T(4,128)(2,1)S(1)}, u32[]{:S(2)}, u32[]{:S(2)}) async-start(bf16[16,4,128]{2,1,0:T(4,128)(2,1)} %bitcast.2), calls=%async_computation.3 | async-start | bytes 32768 | tf_op jit(solution)/shard_map/all_to_all | solution.py:288
  115.2 0.6 add_convert_fusion
  115.8 11.8 %all-to-all-done.3 = bf16[16,4,128]{2,1,0:T(4,128)(2,1)S(1)} async-done(((bf16[16,4,128]{2,1,0:T(4,128)(2,1)}), bf16[16,4,128]{2,1,0:T(4,128)(2,1)S(1)}, u32[]{:S(2)}, u32[]{:S(2)}) %all-to-all-start.3) | async-done | bytes 16416 | tf_op jit(solution)/shard_map/all_to_all | solution.py:288
  127.7 0.6 shard_map.119
  (9 shorter events, 0.0 us)
Async XLA Ops:
  0.6 35.7 %copy-start.1 = (bf16[128,128]{1,0:T(8,128)(2,1)S(1)}, bf16[128,128]{1,0:T(8,128)(2,1)}, u32[]{:S(2)}) copy-start(bf16[128,128]{1,0:T(8,128)(2,1)} %grad_ref.1) | copy-start | bytes 98308
  2.3 34.0 %all-to-all-start = ((bf16[16,64,128]{2,1,0:T(8,128)(2,1)}), bf16[16,64,128]{2,1,0:T(8,128)(2,1)S(1)}, u32[]{:S(2)}, u32[]{:S(2)}) async-start(bf16[16,64,128]{2,1,0:T(8,128)(2,1)} %shard_map.111), calls=%async_computation | async-start | bytes 524288 | tf_op jit(solution)/shard_map/all_to_all | solution.py:288
  24.3 37.6 %copy-start = (bf16[128,128]{1,0:T(8,128)(2,1)S(1)}, bf16[128,128]{1,0:T(8,128)(2,1)}, u32[]{:S(2)}) copy-start(bf16[128,128]{1,0:T(8,128)(2,1)} %query_ref.3) | copy-start | bytes 98308
  38.2 40.0 %all-to-all-start.1 = ((bf16[32,128,128]{2,1,0:T(8,128)(2,1)}), bf16[32,128,128]{2,1,0:T(8,128)(2,1)S(1)}, u32[]{:S(2)}, u32[]{:S(2)}) async-start(bf16[32,128,128]{2,1,0:T(8,128)(2,1)} %get-tuple-element.18), calls=%async_computation.1 | async-start | bytes 2097152 | tf_op jit(solution)/shard_map/all_to_all | solution.py:288
  50.8 23.9 %collective-permute-start = (bf16[128,4096]{1,0:T(8,128)(2,1)}, bf16[128,4096]{1,0:T(8,128)(2,1)}, u32[]{:S(2)}, u32[]{:S(2)}) collective-permute-start(bf16[128,4096]{1,0:T(8,128)(2,1)} %get-tuple-element.20), channel_id=1, source_target_pairs={{0,1},{1,0},{2,3},{3,2},{4,5},{5,4},{6,7},{7,6},{8,9},{9,8},{10,11... | collective-permute-start | bytes 3145736 | tf_op jit(solution)/shard_map/ppermute | solution.py:284
  52.7 12.4 %collective-permute-start.3 = (bf16[16,32,128]{2,1,0:T(8,128)(2,1)S(1)}, bf16[16,32,128]{2,1,0:T(8,128)(2,1)S(1)}, u32[]{:S(2)}, u32[]{:S(2)}) collective-permute-start(bf16[16,32,128]{2,1,0:T(8,128)(2,1)S(1)} %slice.4), channel_id=1, source_target_pairs={{0,64},{64,0},{128,192},{192,128},{256,320},{320,256},{384,448},{4... | collective-permute-start | bytes 393224 | tf_op jit(solution)/shard_map/ppermute | solution.py:336
  54.8 13.2 %collective-permute-start.4 = (bf16[16,32,128]{2,1,0:T(8,128)(2,1)S(1)}, bf16[16,32,128]{2,1,0:T(8,128)(2,1)S(1)}, u32[]{:S(2)}, u32[]{:S(2)}) collective-permute-start(bf16[16,32,128]{2,1,0:T(8,128)(2,1)S(1)} %slice.4), channel_id=1, source_target_pairs={{0,128},{64,192},{128,0},{192,64},{256,384},{320,448},{384,256},{4... | collective-permute-start | bytes 393224 | tf_op jit(solution)/shard_map/ppermute | solution.py:336
  58.9 13.0 %collective-permute-start.5 = (bf16[16,32,128]{2,1,0:T(8,128)(2,1)S(1)}, bf16[16,32,128]{2,1,0:T(8,128)(2,1)S(1)}, u32[]{:S(2)}, u32[]{:S(2)}) collective-permute-start(bf16[16,32,128]{2,1,0:T(8,128)(2,1)S(1)} %slice.4), channel_id=1, source_target_pairs={{0,192},{64,128},{128,64},{192,0},{256,448},{320,384},{384,320},{4... | collective-permute-start | bytes 393224 | tf_op jit(solution)/shard_map/ppermute | solution.py:336
  62.0 3.1 %collective-permute-start.2 = (bf16[128,128]{1,0:T(8,128)(2,1)S(1)}, bf16[128,128]{1,0:T(8,128)(2,1)S(1)}, u32[]{:S(2)}, u32[]{:S(2)}) collective-permute-start(bf16[128,128]{1,0:T(8,128)(2,1)S(1)} %copy-done), channel_id=1, source_target_pairs={{0,1},{1,0},{2,3},{3,2},{4,5},{5,4},{6,7},{7,6},{8,9},{9,8},{10,11... | collective-permute-start | bytes 98312 | tf_op jit(solution)/shard_map/ppermute | solution.py:284
  72.8 9.5 %collective-permute-start.6 = (f32[256,256]{1,0:T(8,128)S(1)}, f32[256,256]{1,0:T(8,128)S(1)}, u32[]{:S(2)}, u32[]{:S(2)}) collective-permute-start(f32[256,256]{1,0:T(8,128)S(1)} %get-tuple-element.22.stat_ref), channel_id=1, source_target_pairs={{0,1},{1,0},{2,3},{3,2},{4,5},{5,4},{6,7},{7,6},{8,9},{9,8},{10,11... | collective-permute-start | bytes 786440 | tf_op jit(solution)/shard_map/ppermute | solution.py:284
  80.3 3.2 %collective-permute-start.1 = (f32[128,256]{1,0:T(8,128)S(1)}, f32[128,256]{1,0:T(8,128)S(1)}, u32[]{:S(2)}, u32[]{:S(2)}) collective-permute-start(f32[128,256]{1,0:T(8,128)S(1)} %shard_map.115.part_ref), channel_id=1, source_target_pairs={{0,1},{1,0},{2,3},{3,2},{4,5},{5,4},{6,7},{7,6},{8,9},{9,8},{10,11... | collective-permute-start | bytes 393224 | tf_op jit(solution)/shard_map/ppermute | solution.py:284
  85.3 23.9 %all-to-all-start.2 = ((bf16[32,32,256]{2,1,0:T(8,128)(2,1)}), bf16[32,32,256]{2,1,0:T(8,128)(2,1)S(1)}, u32[]{:S(2)}, u32[]{:S(2)}) async-start(bf16[32,32,256]{2,1,0:T(8,128)(2,1)} %bitcast.1), calls=%async_computation.2 | async-start | bytes 1048576 | tf_op jit(solution)/shard_map/all_to_all | solution.py:288
  91.4 23.8 %collective-permute-start.7 = (f32[128,128]{1,0:T(8,128)S(1)}, f32[128,128]{1,0:T(8,128)S(1)}, u32[]{:S(2)}, u32[]{:S(2)}) collective-permute-start(f32[128,128]{1,0:T(8,128)S(1)} %get-tuple-element.24), channel_id=1, source_target_pairs={{0,1},{1,0},{2,3},{3,2},{4,5},{5,4},{6,7},{7,6},{8,9},{9,8},{10,11... | collective-permute-start | bytes 196616 | tf_op jit(solution)/shard_map/ppermute | solution.py:284
  109.9 17.7 %all-to-all-start.3 = ((bf16[16,4,128]{2,1,0:T(4,128)(2,1)}), bf16[16,4,128]{2,1,0:T(4,128)(2,1)S(1)}, u32[]{:S(2)}, u32[]{:S(2)}) async-start(bf16[16,4,128]{2,1,0:T(4,128)(2,1)} %bitcast.2), calls=%async_computation.3 | async-start | bytes 32768 | tf_op jit(solution)/shard_map/all_to_all | solution.py:288

commit v7 on v6

--- a/solution.py
+++ b/solution.py
@@ -23,6 +23,9 @@
 N_PEERS = 32
 HALF = 64
 KEYS = N_CTX * HALF
+SPAN = 8
+CHUNKS = N_PEERS // SPAN
+WEIGHTS = (CHUNKS, ROWS, SPAN * HD)
 SPLIT = 4
 SHARE = HALF // SPLIT
 PACK = CAP + 2 * SHARE
@@ -117,28 +120,26 @@
     store.wait()
 
 
-def weight_kernel(weight_ref, own_ref, send_ref, token_ref, whole, parted, sems):
+def weight_kernel(weight_ref, own_ref, send_ref, token_ref, whole, own, send, sems):
     core = lax.axis_index("core")
-    span = 8
+    wide = 2 * SPAN * HD
     loads = [
         pltpu.make_async_copy(
-            weight_ref.at[:, 2 * a * HD : 2 * (a + span) * HD],
-            whole.at[:, 2 * a * HD : 2 * (a + span) * HD],
-            sems.at[a // span],
+            weight_ref.at[:, k * wide : (k + 1) * wide], whole.at[:, k * wide : (k + 1) * wide], sems.at[k]
         )
-        for a in range(0, N_PEERS, span)
+        for k in range(CHUNKS)
     ]
     start_all(loads)
-    for a in range(0, N_PEERS, span):
-        loads[a // span].wait()
-        for b in range(a, a + span):
+    for k in range(CHUNKS):
+        loads[k].wait()
+        for b in range(SPAN):
+            column = 2 * (k * SPAN + b)
             there = slice(b * HD, (b + 1) * HD)
-            for kind in range(2):
-                column = 2 * b + (core if kind == 0 else 1 - core)
-                parted[kind, :, there] = whole[:, pl.ds(pl.multiple_of(column * HD, HD), HD)]
+            own[k, :, there] = whole[:, pl.ds(pl.multiple_of((column + core) * HD, HD), HD)]
+            send[k, :, there] = whole[:, pl.ds(pl.multiple_of((column + 1 - core) * HD, HD), HD)]
     stores = [
-        pltpu.make_async_copy(parted.at[0], own_ref, sems.at[4]),
-        pltpu.make_async_copy(parted.at[1], send_ref, sems.at[5]),
+        pltpu.make_async_copy(own, own_ref, sems.at[CHUNKS]),
+        pltpu.make_async_copy(send, send_ref, sems.at[CHUNKS + 1]),
     ]
     start_all(stores)
     token_ref[...] = jnp.zeros_like(token_ref)
@@ -201,24 +202,17 @@
 
 
 def project_kernel(blocks_ref, own_ref, mate_ref, out_ref, own, mate, sems):
-    span = 8
     copies = [
-        pltpu.make_async_copy(
-            far.at[:, a * HD : (a + span) * HD], near.at[:, a * HD : (a + span) * HD], sems.at[k, a // span]
-        )
-        for a in range(0, N_PEERS, span)
-        for k, (far, near) in enumerate(((own_ref, own), (mate_ref, mate)))
+        pltpu.make_async_copy(far.at[k], near.at[k], sems.at[kind, k])
+        for k in range(CHUNKS)
+        for kind, (far, near) in enumerate(((own_ref, own), (mate_ref, mate)))
     ]
     start_all(copies)
     total = [jnp.zeros((ROWS, HD), F32)] * 2
-    for a in range(0, N_PEERS, span):
-        part = jnp.concatenate([blocks_ref[b] for b in range(a, a + span)], axis=1)
-        there = slice(a * HD, (a + span) * HD)
-        wait_all(copies[a // span * 2 : a // span * 2 + 2])
-        total = [
-            total[0] + dot(part, own[:, there], (1, 1)),
-            total[1] + dot(part, mate[:, there], (1, 1)),
-        ]
+    for k in range(CHUNKS):
+        part = jnp.concatenate([blocks_ref[b] for b in range(k * SPAN, (k + 1) * SPAN)], axis=1)
+        wait_all(copies[2 * k : 2 * k + 2])
+        total = [total[0] + dot(part, own[k], (1, 1)), total[1] + dot(part, mate[k], (1, 1))]
     out_ref[:, :HD] = total[0]
     out_ref[:, HD:] = total[1]
 
@@ -226,7 +220,7 @@
 def backward_kernel(
     part_ref, other_ref, query_ref, mate_ref, probs_ref, stat_ref, seen_ref, pack_ref, *refs
 ):
-    *near_refs, kv_grad_ref, own_ref, send_ref = refs
+    *near_refs, kv_grad_ref, own_ref, send_ref, staged, sems = refs
     grad = jnp.concatenate(
         [
             part_ref[:, :HD] + other_ref[:, HD:],
@@ -246,28 +240,37 @@
     head_out = mine[:, :HD] * mine_gain + seen[:, :HD] * seen_gain
     delta = jnp.sum(grad.astype(F32) * head_out, axis=1, keepdims=True)
     probs = probs_ref[...] * mine_gain
-    score_grad = (probs * (dot(grad, values, (1, 1)) - delta)).astype(BF16)
-    shape = (SPLIT, 2, 8, 4 // SPLIT, 16, HD)
-    key_grad = (dot(score_grad, query, (0, 0)) * SCALE).astype(BF16).reshape(shape)
-    value_grad = dot(probs.astype(BF16), grad, (0, 0)).astype(BF16).reshape(shape)
-    for part in range(SPLIT):
-        share = share_of(part)
-        for zh in range(2):
-            there = slice(zh * 16, (zh + 1) * 16)
-            kv_grad_ref[:, share, :, there, :HD] = key_grad[part, zh]
-            kv_grad_ref[:, share, :, there, HD:] = value_grad[part, zh]
+    stores = []
+    for kind in (1, 0):
+        there = slice(kind * HD, (kind + 1) * HD)
+        if kind == 1:
+            total = dot(probs.astype(BF16), grad, (0, 0))
+        else:
+            score_grad = (probs * (dot(grad, values, (1, 1)) - delta)).astype(BF16)
+            total = dot(score_grad, query, (0, 0)) * SCALE
+        total = total.astype(BF16).reshape(SPLIT, 2, 8, 4 // SPLIT, 16, HD)
+        for part in range(SPLIT):
+            for zh in range(2):
+                rows = slice(zh * 16, (zh + 1) * 16)
+                staged[:, share_of(part), :, rows, there] = total[part, zh]
+        store = pltpu.make_async_copy(
+            staged.at[:, :, :, :, there], kv_grad_ref.at[:, :, :, :, there], sems.at[kind]
+        )
+        store.start()
+        stores.append(store)
     query_grad = dot(score_grad, keys, (1, 0)) * SCALE
     own_ref[...] = query_grad[:ROWS]
     send_ref[...] = query_grad[ROWS:]
+    wait_all(stores)
 
 
 def sum_kernel(parts_ref, out_ref):
     total = parts_ref[0].astype(F32)
-    for b in range(1, 32):
+    for b in range(1, 8):
         total = total + parts_ref[b].astype(F32)
     low = total.astype(BF16)
-    row, source = iota((64, 32), 0), iota((64, 32), 1)
-    place = row // 4 * 2 + row % 2
+    row, source = iota((256, 128), 0), iota((256, 128), 1)
+    place = row // 4 % 4 * 32 + row // 16 * 2 + row % 2
     pick_key = ((place == source) & (row // 2 % 2 == 0)).astype(BF16)
     pick_value = ((place == source) & (row // 2 % 2 == 1)).astype(BF16)
     out_ref[...] = (dot(pick_key, low[:, :HD], (1, 0)) + dot(pick_value, low[:, HD:], (1, 0))).astype(BF16)
@@ -275,9 +278,10 @@
 
 def last_kernel(parts_ref, key_ref, value_ref):
     parts = parts_ref[...].astype(F32)
-    total = parts[:32] + parts[32:]
-    key_ref[...] = jnp.concatenate([total[4 * g : 4 * g + 2] for g in range(8)], axis=1).astype(BF16)
-    value_ref[...] = jnp.concatenate([total[4 * g + 2 : 4 * g + 4] for g in range(8)], axis=1).astype(BF16)
+    both = parts[:128] + parts[128:]
+    total = [sum(both[16 * g + 4 * xl : 16 * g + 4 * xl + 4] for xl in range(4)) for g in range(8)]
+    key_ref[...] = jnp.concatenate([one[:2] for one in total], axis=1).astype(BF16)
+    value_ref[...] = jnp.concatenate([one[2:] for one in total], axis=1).astype(BF16)
 
 
 def swap(array):
@@ -307,14 +311,15 @@
     received = exchange(packed, CTX)
     own_weight, send_weight, token = call(
         weight_kernel,
-        [((ROWS, N_PEERS * HD), BF16)] * 2 + [((8, HD), F32)],
+        [(WEIGHTS, BF16)] * 2 + [((8, HD), F32)],
         out_weight,
         far=(0,),
         far_outs=(0, 1),
         scratch=[
             pltpu.VMEM((ROWS, 2 * N_PEERS * HD), BF16),
-            pltpu.VMEM((2, ROWS, N_PEERS * HD), BF16),
-            pltpu.SemaphoreType.DMA((6,)),
+            pltpu.VMEM(WEIGHTS, BF16),
+            pltpu.VMEM(WEIGHTS, BF16),
+            pltpu.SemaphoreType.DMA((CHUNKS + 2,)),
         ],
     )
     mate_weight = swap(send_weight)
@@ -352,9 +357,9 @@
         mate_weight,
         far=(1, 2),
         scratch=[
-            pltpu.VMEM((ROWS, N_PEERS * HD), BF16),
-            pltpu.VMEM((ROWS, N_PEERS * HD), BF16),
-            pltpu.SemaphoreType.DMA((2, 4)),
+            pltpu.VMEM(WEIGHTS, BF16),
+            pltpu.VMEM(WEIGHTS, BF16),
+            pltpu.SemaphoreType.DMA((2, CHUNKS)),
         ],
     )
     other = swap(part)
@@ -370,13 +375,18 @@
         seen,
         received,
         *near,
-    )
-    kv_parts = exchange(kv_grad.reshape(32, 32, 2 * HD), ("y", "xl"))
+        far_outs=(0,),
+        scratch=[
+            pltpu.VMEM((8, SPLIT, 4 // SPLIT, 32, 2 * HD), BF16),
+            pltpu.SemaphoreType.DMA((2,)),
+        ],
+    )
+    kv_parts = exchange(kv_grad.reshape(8, 128, 2 * HD), ("y",))
     query_grad = (own_grad + swap(send_grad)).astype(BF16)
-    (kv_sum,) = call(sum_kernel, [((64, HD), BF16)], kv_parts)
-    final = exchange(kv_sum.reshape(16, 4, HD), ("zh", "zl", "xh"))
+    (kv_sum,) = call(sum_kernel, [((256, HD), BF16)], kv_parts)
+    final = exchange(kv_sum.reshape(64, 4, HD), ("zh", "zl", "xh", "xl"))
     key_grad, value_grad = call(
-        last_kernel, [((2, 8 * HD), BF16), ((2, 8 * HD), BF16)], final.reshape(64, HD)
+        last_kernel, [((2, 8 * HD), BF16), ((2, 8 * HD), BF16)], final.reshape(256, HD)
     )
     return residual_grad, query_grad, key_grad, value_grad
 

time: 129 us -> 129 us (level)
  the two profiles are of different devices: /device:TPU:16 before, /device:TPU:1 now
where the time goes in v7:
time: 129 us; the launch traced here: 128 us
  starting transfers between devices  72.5 us (56%)
  waiting for transfers between devices  39.6 us (31%)
  Pallas kernels  13.1 us (10%)
  local copies, waits for them, and re-layouts  1.59 us (1%)
    all_to_all x4, starting transfers between devices, exchange(): return lax.all_to_all(array, axes, split_axis=0, concat_axis=0, tiled=True)  43.8 us
    all_to_all x4, waiting for transfers between devices, exchange(): return lax.all_to_all(array, axes, split_axis=0, concat_axis=0, tiled=True)  33.6 us
    ppermute x5, starting transfers between devices, swap(): return lax.ppermute(array, 'core', [(0, 1), (1, 0)])  19.3 us
    pallas_call x9, Pallas kernels, call(): pl.pallas_call(kernel, out_shape=[pltpu.HBM(shape, kind) if n in far_outs...  13.1 us
    ppermute x3, starting transfers between devices, body(): lax.ppermute(held, 'y', [(n, n ^ p) for n in range(8)])  9.41 us
    ppermute x3, waiting for transfers between devices, body(): lax.ppermute(held, 'y', [(n, n ^ p) for n in range(8)])  4.17 us
  transfers between devices with their start and end apart: 12, of which 6 were waited for; matrix products, arithmetic and copies ran while one was open for 2% of the time, Pallas kernels for 6%

profile of v7, /device:TPU:1, one launch (start us, length us, event | category | flops | bytes accessed | tf_op | source)
XLA Modules:
  0.0 128.3 jit_solution(2507368900091531525)
XLA Ops:
  0.6 1.7 %shard_map.111 = bf16[16,64,128]{2,1,0:T(8,128)(2,1)} custom-call(bf16[16,32,128]{2,1,0:T(8,128)(2,1)} %bitcast.6, bf16[128,1024]{1,0:T(8,128)(2,1)} %key_ref.1, bf16[128,1024]{1,0:T(8,128)(2,1)} %value_ref.1), custom_call_target="tpu_custom_call" | custom-call | tf_op jit(solution)/shard_map/pallas_call | solution.py:45
  2.3 20.3 %all-to-all-start = ((bf16[16,64,128]{2,1,0:T(8,128)(2,1)}), bf16[16,64,128]{2,1,0:T(8,128)(2,1)S(1)}, u32[]{:S(2)}, u32[]{:S(2)}) async-start(bf16[16,64,128]{2,1,0:T(8,128)(2,1)} %shard_map.111), calls=%async_computation | async-start | bytes 524288 | tf_op jit(solution)/shard_map/all_to_all | solution.py:292
  22.7 0.8 copy.12.index_ref
  23.4 0.4 shard_map.112.onehot_ref
  23.9 0.8 copy.13.combine_ref
  24.7 3.0 %shard_map.113 = (bf16[4,128,1024]{2,1,0:T(8,128)(2,1)}, bf16[4,128,1024]{2,1,0:T(8,128)(2,1)}, f32[8,128]{1,0:T(8,128)S(1)}) custom-call(bf16[128,8192]{1,0:T(8,128)(2,1)} %weight_ref.1), custom_call_target="tpu_custom_call" | custom-call | tf_op jit(solution)/shard_map/pallas_call | solution.py:45
  27.7 7.6 %all-to-all-done.pack_ref = bf16[16,64,128]{2,1,0:T(8,128)(2,1)S(1)} async-done(((bf16[16,64,128]{2,1,0:T(8,128)(2,1)}), bf16[16,64,128]{2,1,0:T(8,128)(2,1)S(1)}, u32[]{:S(2)}, u32[]{:S(2)}) %all-to-all-start) | async-done | bytes 262176 | tf_op jit(solution)/shard_map/all_to_all | solution.py:292
  35.3 1.8 %shard_map.114 = (bf16[128,128]{1,0:T(8,128)(2,1)}, bf16[32,128,128]{2,1,0:T(8,128)(2,1)}) custom-call(bf16[128,128]{1,0:T(8,128)(2,1)S(1)} %copy-done.1, bf16[16,64,128]{2,1,0:T(8,128)(2,1)S(1)} %all-to-all-done.pack_ref, bf16[256,512]{1,0:T(8,128)(2,1)S(1)} %shard_map.112.onehot_ref, f32[128,2]{1,0:T(8,128)S(1)} %copy.13.combine_ref, ...), custom_call_target="tpu_custom_call" | custom-call | tf_op jit(solution)/shard_map/pallas_call | solution.py:45
  37.2 12.3 %all-to-all-start.1 = ((bf16[32,128,128]{2,1,0:T(8,128)(2,1)}), bf16[32,128,128]{2,1,0:T(8,128)(2,1)S(1)}, u32[]{:S(2)}, u32[]{:S(2)}) async-start(bf16[32,128,128]{2,1,0:T(8,128)(2,1)} %get-tuple-element.18), calls=%async_computation.1 | async-start | bytes 2097152 | tf_op jit(solution)/shard_map/all_to_all | solution.py:292
  49.5 4.5 %collective-permute-start = (bf16[4,128,1024]{2,1,0:T(8,128)(2,1)}, bf16[4,128,1024]{2,1,0:T(8,128)(2,1)}, u32[]{:S(2)}, u32[]{:S(2)}) collective-permute-start(bf16[4,128,1024]{2,1,0:T(8,128)(2,1)} %get-tuple-element.20), channel_id=1, source_target_pairs={{0,1},{1,0},{2,3},{3,2},{4,5},{5,4},{6,7},{7,6},{8,9},{9,8},{10,11... | collective-permute-start | bytes 3145736 | tf_op jit(solution)/shard_map/ppermute | solution.py:288
  54.1 3.5 %collective-permute-start.3 = (bf16[16,32,128]{2,1,0:T(8,128)(2,1)S(1)}, bf16[16,32,128]{2,1,0:T(8,128)(2,1)S(1)}, u32[]{:S(2)}, u32[]{:S(2)}) collective-permute-start(bf16[16,32,128]{2,1,0:T(8,128)(2,1)S(1)} %slice.4), channel_id=1, source_target_pairs={{0,64},{64,0},{128,192},{192,128},{256,320},{320,256},{384,448},{4... | collective-permute-start | bytes 393224 | tf_op jit(solution)/shard_map/ppermute | solution.py:341
  57.6 2.8 %collective-permute-start.4 = (bf16[16,32,128]{2,1,0:T(8,128)(2,1)S(1)}, bf16[16,32,128]{2,1,0:T(8,128)(2,1)S(1)}, u32[]{:S(2)}, u32[]{:S(2)}) collective-permute-start(bf16[16,32,128]{2,1,0:T(8,128)(2,1)S(1)} %slice.4), channel_id=1, source_target_pairs={{0,128},{64,192},{128,0},{192,64},{256,384},{320,448},{384,256},{4... | collective-permute-start | bytes 393224 | tf_op jit(solution)/shard_map/ppermute | solution.py:341
  60.3 3.2 %collective-permute-start.5 = (bf16[16,32,128]{2,1,0:T(8,128)(2,1)S(1)}, bf16[16,32,128]{2,1,0:T(8,128)(2,1)S(1)}, u32[]{:S(2)}, u32[]{:S(2)}) collective-permute-start(bf16[16,32,128]{2,1,0:T(8,128)(2,1)S(1)} %slice.4), channel_id=1, source_target_pairs={{0,192},{64,128},{128,64},{192,0},{256,448},{320,384},{384,320},{4... | collective-permute-start | bytes 393224 | tf_op jit(solution)/shard_map/ppermute | solution.py:341
  63.5 2.6 %collective-permute-start.2 = (bf16[128,128]{1,0:T(8,128)(2,1)S(1)}, bf16[128,128]{1,0:T(8,128)(2,1)S(1)}, u32[]{:S(2)}, u32[]{:S(2)}) collective-permute-start(bf16[128,128]{1,0:T(8,128)(2,1)S(1)} %copy-done), channel_id=1, source_target_pairs={{0,1},{1,0},{2,3},{3,2},{4,5},{5,4},{6,7},{7,6},{8,9},{9,8},{10,11... | collective-permute-start | bytes 98312 | tf_op jit(solution)/shard_map/ppermute | solution.py:288
  66.1 0.8 collective-permute-done.2.mate_ref
  67.0 0.0 collective-permute-done.3.refs_0_
  67.0 4.2 %collective-permute-done.4.refs_1_ = bf16[16,32,128]{2,1,0:T(8,128)(2,1)S(1)} collective-permute-done((bf16[16,32,128]{2,1,0:T(8,128)(2,1)S(1)}, bf16[16,32,128]{2,1,0:T(8,128)(2,1)S(1)}, u32[]{:S(2)}, u32[]{:S(2)}) %collective-permute-start.4) | collective-permute-done | bytes 131104 | tf_op jit(solution)/shard_map/ppermute | solution.py:341
  71.1 0.8 shard_map.116
  72.0 2.8 %collective-permute-start.6 = (f32[256,256]{1,0:T(8,128)S(1)}, f32[256,256]{1,0:T(8,128)S(1)}, u32[]{:S(2)}, u32[]{:S(2)}) collective-permute-start(f32[256,256]{1,0:T(8,128)S(1)} %get-tuple-element.22.stat_ref), channel_id=1, source_target_pairs={{0,1},{1,0},{2,3},{3,2},{4,5},{5,4},{6,7},{7,6},{8,9},{9,8},{10,11... | collective-permute-start | bytes 786440 | tf_op jit(solution)/shard_map/ppermute | solution.py:288
  74.8 0.0 collective-permute-done.mate_ref
  74.8 2.1 %shard_map.115.part_ref = f32[128,256]{1,0:T(8,128)S(1)} custom-call(bf16[32,128,128]{2,1,0:T(8,128)(2,1)S(1)} %all-to-all-done.1.blocks_ref, bf16[4,128,1024]{2,1,0:T(8,128)(2,1)} %get-tuple-element.19.own_ref, bf16[4,128,1024]{2,1,0:T(8,128)(2,1)} %collective-permute-done.mate_ref), custom_call_target="tpu_custom_call" | custom-call | tf_op jit(solution)/shard_map/pallas_call | solution.py:45
  76.9 6.8 %collective-permute-start.1 = (f32[128,256]{1,0:T(8,128)S(1)}, f32[128,256]{1,0:T(8,128)S(1)}, u32[]{:S(2)}, u32[]{:S(2)}) collective-permute-start(f32[128,256]{1,0:T(8,128)S(1)} %shard_map.115.part_ref), channel_id=1, source_target_pairs={{0,1},{1,0},{2,3},{3,2},{4,5},{5,4},{6,7},{7,6},{8,9},{9,8},{10,11... | collective-permute-start | bytes 393224 | tf_op jit(solution)/shard_map/ppermute | solution.py:288
  83.8 1.0 collective-permute-done.1.other_ref
  84.7 1.8 %shard_map.117 = (bf16[8,4,1,32,256]{4,3,2,1,0:T(8,128)(2,1)}, f32[128,128]{1,0:T(8,128)S(1)}, f32[128,128]{1,0:T(8,128)S(1)}) custom-call(f32[128,256]{1,0:T(8,128)S(1)} %shard_map.115.part_ref, f32[128,256]{1,0:T(8,128)S(1)} %collective-permute-done.1.other_ref, bf16[128,128]{1,0:T(8,128)(2,1)S(1)} %copy-done, ...), custom_call_target="tpu_custom_call" | custom-call | tf_op jit(solution)/shard_map/pallas_call | solution.py:45
  86.5 4.3 %all-to-all-start.2 = ((bf16[8,128,256]{2,1,0:T(8,128)(2,1)}), bf16[8,128,256]{2,1,0:T(8,128)(2,1)S(1)}, u32[]{:S(2)}, u32[]{:S(2)}) async-start(bf16[8,128,256]{2,1,0:T(8,128)(2,1)} %bitcast.5), calls=%async_computation.2 | async-start | bytes 1048576 | tf_op jit(solution)/shard_map/all_to_all | solution.py:292
  90.8 2.5 %collective-permute-start.7 = (f32[128,128]{1,0:T(8,128)S(1)}, f32[128,128]{1,0:T(8,128)S(1)}, u32[]{:S(2)}, u32[]{:S(2)}) collective-permute-start(f32[128,128]{1,0:T(8,128)S(1)} %get-tuple-element.24), channel_id=1, source_target_pairs={{0,1},{1,0},{2,3},{3,2},{4,5},{5,4},{6,7},{7,6},{8,9},{9,8},{10,11... | collective-permute-start | bytes 196616 | tf_op jit(solution)/shard_map/ppermute | solution.py:288
  93.3 15.4 %all-to-all-done.2.parts_ref = bf16[8,128,256]{2,1,0:T(8,128)(2,1)S(1)} async-done(((bf16[8,128,256]{2,1,0:T(8,128)(2,1)}), bf16[8,128,256]{2,1,0:T(8,128)(2,1)S(1)}, u32[]{:S(2)}, u32[]{:S(2)}) %all-to-all-start.2) | async-done | bytes 524320 | tf_op jit(solution)/shard_map/all_to_all | solution.py:292
  108.7 0.9 shard_map.118
  109.6 6.9 %all-to-all-start.3 = ((bf16[64,4,128]{2,1,0:T(4,128)(2,1)}), bf16[64,4,128]{2,1,0:T(4,128)(2,1)S(1)}, u32[]{:S(2)}, u32[]{:S(2)}) async-start(bf16[64,4,128]{2,1,0:T(4,128)(2,1)} %bitcast.2), calls=%async_computation.3 | async-start | bytes 131072 | tf_op jit(solution)/shard_map/all_to_all | solution.py:292
  116.5 0.6 add_convert_fusion
  117.1 10.5 %all-to-all-done.3 = bf16[64,4,128]{2,1,0:T(4,128)(2,1)S(1)} async-done(((bf16[64,4,128]{2,1,0:T(4,128)(2,1)}), bf16[64,4,128]{2,1,0:T(4,128)(2,1)S(1)}, u32[]{:S(2)}, u32[]{:S(2)}) %all-to-all-start.3) | async-done | bytes 65568 | tf_op jit(solution)/shard_map/all_to_all | solution.py:292
  127.7 0.6 shard_map.119
  (9 shorter events, 0.0 us)
Async XLA Ops:
  0.6 34.7 %copy-start.1 = (bf16[128,128]{1,0:T(8,128)(2,1)S(1)}, bf16[128,128]{1,0:T(8,128)(2,1)}, u32[]{:S(2)}) copy-start(bf16[128,128]{1,0:T(8,128)(2,1)} %grad_ref.1) | copy-start | bytes 98308
  2.3 32.9 %all-to-all-start = ((bf16[16,64,128]{2,1,0:T(8,128)(2,1)}), bf16[16,64,128]{2,1,0:T(8,128)(2,1)S(1)}, u32[]{:S(2)}, u32[]{:S(2)}) async-start(bf16[16,64,128]{2,1,0:T(8,128)(2,1)} %shard_map.111), calls=%async_computation | async-start | bytes 524288 | tf_op jit(solution)/shard_map/all_to_all | solution.py:292
  24.7 38.8 %copy-start = (bf16[128,128]{1,0:T(8,128)(2,1)S(1)}, bf16[128,128]{1,0:T(8,128)(2,1)}, u32[]{:S(2)}) copy-start(bf16[128,128]{1,0:T(8,128)(2,1)} %query_ref.3) | copy-start | bytes 98308
  37.2 37.6 %all-to-all-start.1 = ((bf16[32,128,128]{2,1,0:T(8,128)(2,1)}), bf16[32,128,128]{2,1,0:T(8,128)(2,1)S(1)}, u32[]{:S(2)}, u32[]{:S(2)}) async-start(bf16[32,128,128]{2,1,0:T(8,128)(2,1)} %get-tuple-element.18), calls=%async_computation.1 | async-start | bytes 2097152 | tf_op jit(solution)/shard_map/all_to_all | solution.py:292
  49.5 25.3 %collective-permute-start = (bf16[4,128,1024]{2,1,0:T(8,128)(2,1)}, bf16[4,128,1024]{2,1,0:T(8,128)(2,1)}, u32[]{:S(2)}, u32[]{:S(2)}) collective-permute-start(bf16[4,128,1024]{2,1,0:T(8,128)(2,1)} %get-tuple-element.20), channel_id=1, source_target_pairs={{0,1},{1,0},{2,3},{3,2},{4,5},{5,4},{6,7},{7,6},{8,9},{9,8},{10,11... | collective-permute-start | bytes 3145736 | tf_op jit(solution)/shard_map/ppermute | solution.py:288
  54.1 12.9 %collective-permute-start.3 = (bf16[16,32,128]{2,1,0:T(8,128)(2,1)S(1)}, bf16[16,32,128]{2,1,0:T(8,128)(2,1)S(1)}, u32[]{:S(2)}, u32[]{:S(2)}) collective-permute-start(bf16[16,32,128]{2,1,0:T(8,128)(2,1)S(1)} %slice.4), channel_id=1, source_target_pairs={{0,64},{64,0},{128,192},{192,128},{256,320},{320,256},{384,448},{4... | collective-permute-start | bytes 393224 | tf_op jit(solution)/shard_map/ppermute | solution.py:341
  57.6 13.6 %collective-permute-start.4 = (bf16[16,32,128]{2,1,0:T(8,128)(2,1)S(1)}, bf16[16,32,128]{2,1,0:T(8,128)(2,1)S(1)}, u32[]{:S(2)}, u32[]{:S(2)}) collective-permute-start(bf16[16,32,128]{2,1,0:T(8,128)(2,1)S(1)} %slice.4), channel_id=1, source_target_pairs={{0,128},{64,192},{128,0},{192,64},{256,384},{320,448},{384,256},{4... | collective-permute-start | bytes 393224 | tf_op jit(solution)/shard_map/ppermute | solution.py:341
  60.3 10.8 %collective-permute-start.5 = (bf16[16,32,128]{2,1,0:T(8,128)(2,1)S(1)}, bf16[16,32,128]{2,1,0:T(8,128)(2,1)S(1)}, u32[]{:S(2)}, u32[]{:S(2)}) collective-permute-start(bf16[16,32,128]{2,1,0:T(8,128)(2,1)S(1)} %slice.4), channel_id=1, source_target_pairs={{0,192},{64,128},{128,64},{192,0},{256,448},{320,384},{384,320},{4... | collective-permute-start | bytes 393224 | tf_op jit(solution)/shard_map/ppermute | solution.py:341
  63.5 3.5 %collective-permute-start.2 = (bf16[128,128]{1,0:T(8,128)(2,1)S(1)}, bf16[128,128]{1,0:T(8,128)(2,1)S(1)}, u32[]{:S(2)}, u32[]{:S(2)}) collective-permute-start(bf16[128,128]{1,0:T(8,128)(2,1)S(1)} %copy-done), channel_id=1, source_target_pairs={{0,1},{1,0},{2,3},{3,2},{4,5},{5,4},{6,7},{7,6},{8,9},{9,8},{10,11... | collective-permute-start | bytes 98312 | tf_op jit(solution)/shard_map/ppermute | solution.py:288
  72.0 11.8 %collective-permute-start.6 = (f32[256,256]{1,0:T(8,128)S(1)}, f32[256,256]{1,0:T(8,128)S(1)}, u32[]{:S(2)}, u32[]{:S(2)}) collective-permute-start(f32[256,256]{1,0:T(8,128)S(1)} %get-tuple-element.22.stat_ref), channel_id=1, source_target_pairs={{0,1},{1,0},{2,3},{3,2},{4,5},{5,4},{6,7},{7,6},{8,9},{9,8},{10,11... | collective-permute-start | bytes 786440 | tf_op jit(solution)/shard_map/ppermute | solution.py:288
  76.9 7.8 %collective-permute-start.1 = (f32[128,256]{1,0:T(8,128)S(1)}, f32[128,256]{1,0:T(8,128)S(1)}, u32[]{:S(2)}, u32[]{:S(2)}) collective-permute-start(f32[128,256]{1,0:T(8,128)S(1)} %shard_map.115.part_ref), channel_id=1, source_target_pairs={{0,1},{1,0},{2,3},{3,2},{4,5},{5,4},{6,7},{7,6},{8,9},{9,8},{10,11... | collective-permute-start | bytes 393224 | tf_op jit(solution)/shard_map/ppermute | solution.py:288
  86.5 22.3 %all-to-all-start.2 = ((bf16[8,128,256]{2,1,0:T(8,128)(2,1)}), bf16[8,128,256]{2,1,0:T(8,128)(2,1)S(1)}, u32[]{:S(2)}, u32[]{:S(2)}) async-start(bf16[8,128,256]{2,1,0:T(8,128)(2,1)} %bitcast.5), calls=%async_computation.2 | async-start | bytes 1048576 | tf_op jit(solution)/shard_map/all_to_all | solution.py:292
  90.8 25.7 %collective-permute-start.7 = (f32[128,128]{1,0:T(8,128)S(1)}, f32[128,128]{1,0:T(8,128)S(1)}, u32[]{:S(2)}, u32[]{:S(2)}) collective-permute-start(f32[128,128]{1,0:T(8,128)S(1)} %get-tuple-element.24), channel_id=1, source_target_pairs={{0,1},{1,0},{2,3},{3,2},{4,5},{5,4},{6,7},{7,6},{8,9},{9,8},{10,11... | collective-permute-start | bytes 196616 | tf_op jit(solution)/shard_map/ppermute | solution.py:288
  109.6 18.0 %all-to-all-start.3 = ((bf16[64,4,128]{2,1,0:T(4,128)(2,1)}), bf16[64,4,128]{2,1,0:T(4,128)(2,1)S(1)}, u32[]{:S(2)}, u32[]{:S(2)}) async-start(bf16[64,4,128]{2,1,0:T(4,128)(2,1)} %bitcast.2), calls=%async_computation.3 | async-start | bytes 131072 | tf_op jit(solution)/shard_map/all_to_all | solution.py:292

commit v8 on v6

--- a/solution.py
+++ b/solution.py
@@ -117,7 +117,7 @@
     store.wait()
 
 
-def weight_kernel(weight_ref, own_ref, send_ref, token_ref, whole, parted, sems):
+def weight_kernel(weight_ref, own_ref, send_ref, token_ref, whole, own, send, sems):
     core = lax.axis_index("core")
     span = 8
     loads = [
@@ -132,13 +132,14 @@
     for a in range(0, N_PEERS, span):
         loads[a // span].wait()
         for b in range(a, a + span):
-            there = slice(b * HD, (b + 1) * HD)
-            for kind in range(2):
-                column = 2 * b + (core if kind == 0 else 1 - core)
-                parted[kind, :, there] = whole[:, pl.ds(pl.multiple_of(column * HD, HD), HD)]
+            within = slice((b - a) * HD, (b - a + 1) * HD)
+            own_at = pl.ds(pl.multiple_of((2 * b + core) * HD, HD), HD)
+            send_at = pl.ds(pl.multiple_of((2 * b + 1 - core) * HD, HD), HD)
+            own[a // span, :, within] = whole[:, own_at]
+            send[:, b * HD : (b + 1) * HD] = whole[:, send_at]
     stores = [
-        pltpu.make_async_copy(parted.at[0], own_ref, sems.at[4]),
-        pltpu.make_async_copy(parted.at[1], send_ref, sems.at[5]),
+        pltpu.make_async_copy(own, own_ref, sems.at[4]),
+        pltpu.make_async_copy(send, send_ref, sems.at[5]),
     ]
     start_all(stores)
     token_ref[...] = jnp.zeros_like(token_ref)
@@ -182,7 +183,7 @@
 
 
 def forward_kernel(query_ref, mate_ref, pack_ref, *refs):
-    *near_refs, probs_ref, stat_ref = refs
+    *near_refs, probs_ref, stat_ref, staged, sem = refs
     block = lax.axis_index("zh") * 8 + lax.axis_index("y")
     query = jnp.concatenate([query_ref[...], mate_ref[...]], axis=0)
     keys, values = joined_kv(pack_ref, *near_refs)
@@ -195,30 +196,30 @@
     top = jnp.max(scores, axis=1, keepdims=True)
     probs = jnp.where(allowed, jnp.exp(scores - top), 0.0)
     total = jnp.sum(probs, axis=1, keepdims=True)
-    probs_ref[...] = probs
+    staged[...] = probs
+    store = pltpu.make_async_copy(staged, probs_ref, sem.at[0])
+    store.start()
     stat_ref[:, :HD] = dot(probs.astype(BF16), values, (1, 0))
     stat_ref[:, HD:] = jnp.where(iota((2 * ROWS, HD), 1) < HALF, top, total)
-
-
-def project_kernel(blocks_ref, own_ref, mate_ref, out_ref, own, mate, sems):
+    store.wait()
+
+
+def project_kernel(blocks_ref, own_ref, mate_ref, out_ref, own, sems):
     span = 8
     copies = [
-        pltpu.make_async_copy(
-            far.at[:, a * HD : (a + span) * HD], near.at[:, a * HD : (a + span) * HD], sems.at[k, a // span]
-        )
+        pltpu.make_async_copy(own_ref.at[a // span], own.at[a // span], sems.at[a // span])
         for a in range(0, N_PEERS, span)
-        for k, (far, near) in enumerate(((own_ref, own), (mate_ref, mate)))
     ]
     start_all(copies)
     total = [jnp.zeros((ROWS, HD), F32)] * 2
+    parts = []
     for a in range(0, N_PEERS, span):
         part = jnp.concatenate([blocks_ref[b] for b in range(a, a + span)], axis=1)
-        there = slice(a * HD, (a + span) * HD)
-        wait_all(copies[a // span * 2 : a // span * 2 + 2])
-        total = [
-            total[0] + dot(part, own[:, there], (1, 1)),
-            total[1] + dot(part, mate[:, there], (1, 1)),
-        ]
+        parts.append(part)
+        total[1] = total[1] + dot(part, mate_ref[:, a * HD : (a + span) * HD], (1, 1))
+    for k, part in enumerate(parts):
+        copies[k].wait()
+        total[0] = total[0] + dot(part, own[k], (1, 1))
     out_ref[:, :HD] = total[0]
     out_ref[:, HD:] = total[1]
 
@@ -307,13 +308,14 @@
     received = exchange(packed, CTX)
     own_weight, send_weight, token = call(
         weight_kernel,
-        [((ROWS, N_PEERS * HD), BF16)] * 2 + [((8, HD), F32)],
+        [((4, ROWS, 8 * HD), BF16), ((ROWS, N_PEERS * HD), BF16), ((8, HD), F32)],
         out_weight,
         far=(0,),
         far_outs=(0, 1),
         scratch=[
             pltpu.VMEM((ROWS, 2 * N_PEERS * HD), BF16),
-            pltpu.VMEM((2, ROWS, N_PEERS * HD), BF16),
+            pltpu.VMEM((4, ROWS, 8 * HD), BF16),
+            pltpu.VMEM((ROWS, N_PEERS * HD), BF16),
             pltpu.SemaphoreType.DMA((6,)),
         ],
     )
@@ -342,6 +344,8 @@
         mate_query,
         received,
         *near,
+        far_outs=(0,),
+        scratch=[pltpu.VMEM((2 * ROWS, KEYS), F32), pltpu.SemaphoreType.DMA((1,))],
     )
     seen = swap(stat)
     (part,) = call(
@@ -350,12 +354,8 @@
         blocks,
         own_weight,
         mate_weight,
-        far=(1, 2),
-        scratch=[
-            pltpu.VMEM((ROWS, N_PEERS * HD), BF16),
-            pltpu.VMEM((ROWS, N_PEERS * HD), BF16),
-            pltpu.SemaphoreType.DMA((2, 4)),
-        ],
+        far=(1,),
+        scratch=[pltpu.VMEM((4, ROWS, 8 * HD), BF16), pltpu.SemaphoreType.DMA((4,))],
     )
     other = swap(part)
     kv_grad, own_grad, send_grad = call(

time: 129 us -> 132 us (1.023)
  Pallas kernels: 13 us -> 15.3 us
  starting transfers between devices: 62.9 us -> 64.5 us
  waiting for transfers between devices: 49.3 us -> 47.8 us
    pallas_call x9, Pallas kernels: 13 us -> 15.3 us  [call(): pl.pallas_call(kernel, out_shape=[pltpu.HBM(shape, kind) if n in far_outs...]
    all_to_all x4, waiting for transfers between devices: 40 us -> 38.4 us  [exchange(): return lax.all_to_all(array, axes, split_axis=0, concat_axis=0, tiled=True)]
    all_to_all x4, starting transfers between devices: 44.1 us -> 45.6 us  [exchange(): return lax.all_to_all(array, axes, split_axis=0, concat_axis=0, tiled=True)]
where the time goes in v8:
time: 132 us; the launch traced here: 131 us
  starting transfers between devices  64.5 us (49%)
  waiting for transfers between devices  47.8 us (36%)
  Pallas kernels  15.3 us (12%)
  local copies, waits for them, and re-layouts  1.62 us (1%)
    all_to_all x4, starting transfers between devices, exchange(): return lax.all_to_all(array, axes, split_axis=0, concat_axis=0, tiled=True)  45.6 us
    all_to_all x4, waiting for transfers between devices, exchange(): return lax.all_to_all(array, axes, split_axis=0, concat_axis=0, tiled=True)  38.4 us
    pallas_call x9, Pallas kernels, call(): pl.pallas_call(kernel, out_shape=[pltpu.HBM(shape, kind) if n in far_outs...  15.3 us
    ppermute x5, starting transfers between devices, swap(): return lax.ppermute(array, 'core', [(0, 1), (1, 0)])  9.73 us
    ppermute x3, starting transfers between devices, body(): lax.ppermute(held, 'y', [(n, n ^ p) for n in range(8)])  9.21 us
    ppermute x3, waiting for transfers between devices, body(): lax.ppermute(held, 'y', [(n, n ^ p) for n in range(8)])  6.86 us
  transfers between devices with their start and end apart: 12, of which 8 were waited for; matrix products, arithmetic and copies ran while one was open for 2% of the time, Pallas kernels for 6%

profile of v8, /device:TPU:16, one launch (start us, length us, event | category | flops | bytes accessed | tf_op | source)
XLA Modules:
  0.0 130.7 jit_solution(7665222648461938541)
XLA Ops:
  0.6 1.7 %shard_map.111 = bf16[16,64,128]{2,1,0:T(8,128)(2,1)} custom-call(bf16[16,32,128]{2,1,0:T(8,128)(2,1)} %bitcast.5, bf16[128,1024]{1,0:T(8,128)(2,1)} %key_ref.1, bf16[128,1024]{1,0:T(8,128)(2,1)} %value_ref.1), custom_call_target="tpu_custom_call" | custom-call | tf_op jit(solution)/shard_map/pallas_call | solution.py:42
  2.3 20.0 %all-to-all-start = ((bf16[16,64,128]{2,1,0:T(8,128)(2,1)}), bf16[16,64,128]{2,1,0:T(8,128)(2,1)S(1)}, u32[]{:S(2)}, u32[]{:S(2)}) async-start(bf16[16,64,128]{2,1,0:T(8,128)(2,1)} %shard_map.111), calls=%async_computation | async-start | bytes 524288 | tf_op jit(solution)/shard_map/all_to_all | solution.py:289
  22.3 0.8 copy.12.index_ref
  23.1 0.4 shard_map.112.onehot_ref
  23.6 0.8 copy.13.combine_ref
  24.4 3.0 %shard_map.113 = (bf16[4,128,1024]{2,1,0:T(8,128)(2,1)}, bf16[128,4096]{1,0:T(8,128)(2,1)}, f32[8,128]{1,0:T(8,128)S(1)}) custom-call(bf16[128,8192]{1,0:T(8,128)(2,1)} %weight_ref.1), custom_call_target="tpu_custom_call" | custom-call | tf_op jit(solution)/shard_map/pallas_call | solution.py:42
  27.4 8.9 %all-to-all-done.pack_ref = bf16[16,64,128]{2,1,0:T(8,128)(2,1)S(1)} async-done(((bf16[16,64,128]{2,1,0:T(8,128)(2,1)}), bf16[16,64,128]{2,1,0:T(8,128)(2,1)S(1)}, u32[]{:S(2)}, u32[]{:S(2)}) %all-to-all-start) | async-done | bytes 262176 | tf_op jit(solution)/shard_map/all_to_all | solution.py:289
  36.3 1.9 %shard_map.114 = (bf16[128,128]{1,0:T(8,128)(2,1)}, bf16[32,128,128]{2,1,0:T(8,128)(2,1)}) custom-call(bf16[128,128]{1,0:T(8,128)(2,1)S(1)} %copy-done.9, bf16[16,64,128]{2,1,0:T(8,128)(2,1)S(1)} %all-to-all-done.pack_ref, bf16[256,512]{1,0:T(8,128)(2,1)S(1)} %shard_map.112.onehot_ref, f32[128,2]{1,0:T(8,128)S(1)} %copy.13.combine_ref, ...), custom_call_target="tpu_custom_call" | custom-call | tf_op jit(solution)/shard_map/pallas_call | solution.py:42
  38.2 12.6 %all-to-all-start.1 = ((bf16[32,128,128]{2,1,0:T(8,128)(2,1)}), bf16[32,128,128]{2,1,0:T(8,128)(2,1)S(1)}, u32[]{:S(2)}, u32[]{:S(2)}) async-start(bf16[32,128,128]{2,1,0:T(8,128)(2,1)} %get-tuple-element.18), calls=%async_computation.1 | async-start | bytes 2097152 | tf_op jit(solution)/shard_map/all_to_all | solution.py:289
  50.8 1.9 %collective-permute-start = (bf16[128,4096]{1,0:T(8,128)(2,1)}, bf16[128,4096]{1,0:T(8,128)(2,1)S(1)}, u32[]{:S(2)}, u32[]{:S(2)}) collective-permute-start(bf16[128,4096]{1,0:T(8,128)(2,1)} %get-tuple-element.20), channel_id=1, source_target_pairs={{0,1},{1,0},{2,3},{3,2},{4,5},{5,4},{6,7},{7,6},{8,9},{9,8},{10,11... | collective-permute-start | bytes 3145736 | tf_op jit(solution)/shard_map/ppermute | solution.py:285
  52.8 2.1 %collective-permute-start.3 = (bf16[16,32,128]{2,1,0:T(8,128)(2,1)S(1)}, bf16[16,32,128]{2,1,0:T(8,128)(2,1)S(1)}, u32[]{:S(2)}, u32[]{:S(2)}) collective-permute-start(bf16[16,32,128]{2,1,0:T(8,128)(2,1)S(1)} %slice.4), channel_id=1, source_target_pairs={{0,64},{64,0},{128,192},{192,128},{256,320},{320,256},{384,448},{4... | collective-permute-start | bytes 393224 | tf_op jit(solution)/shard_map/ppermute | solution.py:338
  54.8 4.1 %collective-permute-start.4 = (bf16[16,32,128]{2,1,0:T(8,128)(2,1)S(1)}, bf16[16,32,128]{2,1,0:T(8,128)(2,1)S(1)}, u32[]{:S(2)}, u32[]{:S(2)}) collective-permute-start(bf16[16,32,128]{2,1,0:T(8,128)(2,1)S(1)} %slice.4), channel_id=1, source_target_pairs={{0,128},{64,192},{128,0},{192,64},{256,384},{320,448},{384,256},{4... | collective-permute-start | bytes 393224 | tf_op jit(solution)/shard_map/ppermute | solution.py:338
  58.9 3.0 %collective-permute-start.5 = (bf16[16,32,128]{2,1,0:T(8,128)(2,1)S(1)}, bf16[16,32,128]{2,1,0:T(8,128)(2,1)S(1)}, u32[]{:S(2)}, u32[]{:S(2)}) collective-permute-start(bf16[16,32,128]{2,1,0:T(8,128)(2,1)S(1)} %slice.4), channel_id=1, source_target_pairs={{0,192},{64,128},{128,64},{192,0},{256,448},{320,384},{384,320},{4... | collective-permute-start | bytes 393224 | tf_op jit(solution)/shard_map/ppermute | solution.py:338
  62.0 1.9 %collective-permute-start.2 = (bf16[128,128]{1,0:T(8,128)(2,1)S(1)}, bf16[128,128]{1,0:T(8,128)(2,1)S(1)}, u32[]{:S(2)}, u32[]{:S(2)}) collective-permute-start(bf16[128,128]{1,0:T(8,128)(2,1)S(1)} %copy-done.5), channel_id=1, source_target_pairs={{0,1},{1,0},{2,3},{3,2},{4,5},{5,4},{6,7},{7,6},{8,9},{9,8},{10,11... | collective-permute-start | bytes 98312 | tf_op jit(solution)/shard_map/ppermute | solution.py:285
  63.9 1.2 collective-permute-done.2.mate_ref
  65.1 2.9 %collective-permute-done.4.refs_1_ = bf16[16,32,128]{2,1,0:T(8,128)(2,1)S(1)} collective-permute-done((bf16[16,32,128]{2,1,0:T(8,128)(2,1)S(1)}, bf16[16,32,128]{2,1,0:T(8,128)(2,1)S(1)}, u32[]{:S(2)}, u32[]{:S(2)}) %collective-permute-start.4) | collective-permute-done | bytes 131104 | tf_op jit(solution)/shard_map/ppermute | solution.py:338
  68.0 4.0 %collective-permute-done.5.refs_2_ = bf16[16,32,128]{2,1,0:T(8,128)(2,1)S(1)} collective-permute-done((bf16[16,32,128]{2,1,0:T(8,128)(2,1)S(1)}, bf16[16,32,128]{2,1,0:T(8,128)(2,1)S(1)}, u32[]{:S(2)}, u32[]{:S(2)}) %collective-permute-start.5) | collective-permute-done | bytes 131104 | tf_op jit(solution)/shard_map/ppermute | solution.py:338
  72.0 2.3 %shard_map.116 = (f32[256,1024]{1,0:T(8,128)}, f32[256,256]{1,0:T(8,128)}) custom-call(bf16[128,128]{1,0:T(8,128)(2,1)S(1)} %copy-done.5, bf16[128,128]{1,0:T(8,128)(2,1)S(1)} %collective-permute-done.2.mate_ref, bf16[16,64,128]{2,1,0:T(8,128)(2,1)S(1)} %all-to-all-done.pack_ref, bf16[16,32,128]{2,1,0:T(8,128)(2,1)S(1)} %collective-permute-done.3.refs_0_, ...), custom_call_target="tpu_custom_call" | custom-call | tf_op jit(solution)/shard_map/pallas_call | solution.py:42
  74.3 2.1 %collective-permute-start.6 = (f32[256,256]{1,0:T(8,128)}, f32[256,256]{1,0:T(8,128)}, u32[]{:S(2)}, u32[]{:S(2)}) collective-permute-start(f32[256,256]{1,0:T(8,128)} %get-tuple-element.22.stat_ref), channel_id=1, source_target_pairs={{0,1},{1,0},{2,3},{3,2},{4,5},{5,4},{6,7},{7,6},{8,9},{9,8},{10,11... | collective-permute-start | bytes 786440 | tf_op jit(solution)/shard_map/ppermute | solution.py:285
  76.4 1.8 %all-to-all-done.1.blocks_ref = bf16[32,128,128]{2,1,0:T(8,128)(2,1)S(1)} async-done(((bf16[32,128,128]{2,1,0:T(8,128)(2,1)}), bf16[32,128,128]{2,1,0:T(8,128)(2,1)S(1)}, u32[]{:S(2)}, u32[]{:S(2)}) %all-to-all-start.1) | async-done | bytes 1048608 | tf_op jit(solution)/shard_map/all_to_all | solution.py:289
  78.2 1.9 %shard_map.115.part_ref = f32[128,256]{1,0:T(8,128)S(1)} custom-call(bf16[32,128,128]{2,1,0:T(8,128)(2,1)S(1)} %all-to-all-done.1.blocks_ref, bf16[4,128,1024]{2,1,0:T(8,128)(2,1)} %get-tuple-element.19.own_ref, bf16[128,4096]{1,0:T(8,128)(2,1)S(1)} %collective-permute-done.mate_ref), custom_call_target="tpu_custom_call" | custom-call | tf_op jit(solution)/shard_map/pallas_call | solution.py:42
  80.1 1.9 %collective-permute-start.1 = (f32[128,256]{1,0:T(8,128)S(1)}, f32[128,256]{1,0:T(8,128)S(1)}, u32[]{:S(2)}, u32[]{:S(2)}) collective-permute-start(f32[128,256]{1,0:T(8,128)S(1)} %shard_map.115.part_ref), channel_id=1, source_target_pairs={{0,1},{1,0},{2,3},{3,2},{4,5},{5,4},{6,7},{7,6},{8,9},{9,8},{10,11... | collective-permute-start | bytes 393224 | tf_op jit(solution)/shard_map/ppermute | solution.py:285
  82.0 1.3 collective-permute-done.1.other_ref
  83.4 2.7 %shard_map.117 = (bf16[8,4,1,32,256]{4,3,2,1,0:T(8,128)(2,1)}, f32[128,128]{1,0:T(8,128)S(1)}, f32[128,128]{1,0:T(8,128)S(1)}) custom-call(f32[128,256]{1,0:T(8,128)S(1)} %shard_map.115.part_ref, f32[128,256]{1,0:T(8,128)S(1)} %collective-permute-done.1.other_ref, bf16[128,128]{1,0:T(8,128)(2,1)S(1)} %copy-done.6, bf16[128,128]{1,0:T(8,128)(2,1)S(1)} %copy-done.8, ...), custom_call_target="tpu_custom_call" | custom-call | tf_op jit(solution)/shard_map/pallas_call | solution.py:42
  86.1 6.2 %all-to-all-start.2 = ((bf16[32,32,256]{2,1,0:T(8,128)(2,1)}), bf16[32,32,256]{2,1,0:T(8,128)(2,1)S(1)}, u32[]{:S(2)}, u32[]{:S(2)}) async-start(bf16[32,32,256]{2,1,0:T(8,128)(2,1)} %bitcast.1), calls=%async_computation.2 | async-start | bytes 1048576 | tf_op jit(solution)/shard_map/all_to_all | solution.py:289
  92.3 1.9 %collective-permute-start.7 = (f32[128,128]{1,0:T(8,128)S(1)}, f32[128,128]{1,0:T(8,128)S(1)}, u32[]{:S(2)}, u32[]{:S(2)}) collective-permute-start(f32[128,128]{1,0:T(8,128)S(1)} %get-tuple-element.24), channel_id=1, source_target_pairs={{0,1},{1,0},{2,3},{3,2},{4,5},{5,4},{6,7},{7,6},{8,9},{9,8},{10,11... | collective-permute-start | bytes 196616 | tf_op jit(solution)/shard_map/ppermute | solution.py:285
  94.2 15.8 %all-to-all-done.2.parts_ref = bf16[32,32,256]{2,1,0:T(8,128)(2,1)S(1)} async-done(((bf16[32,32,256]{2,1,0:T(8,128)(2,1)}), bf16[32,32,256]{2,1,0:T(8,128)(2,1)S(1)}, u32[]{:S(2)}, u32[]{:S(2)}) %all-to-all-start.2) | async-done | bytes 524320 | tf_op jit(solution)/shard_map/all_to_all | solution.py:289
  110.0 0.8 shard_map.118
  110.8 6.8 %all-to-all-start.3 = ((bf16[16,4,128]{2,1,0:T(4,128)(2,1)}), bf16[16,4,128]{2,1,0:T(4,128)(2,1)S(1)}, u32[]{:S(2)}, u32[]{:S(2)}) async-start(bf16[16,4,128]{2,1,0:T(4,128)(2,1)} %bitcast.2), calls=%async_computation.3 | async-start | bytes 32768 | tf_op jit(solution)/shard_map/all_to_all | solution.py:289
  117.7 0.6 add_convert_fusion
  118.3 11.8 %all-to-all-done.3 = bf16[16,4,128]{2,1,0:T(4,128)(2,1)S(1)} async-done(((bf16[16,4,128]{2,1,0:T(4,128)(2,1)}), bf16[16,4,128]{2,1,0:T(4,128)(2,1)S(1)}, u32[]{:S(2)}, u32[]{:S(2)}) %all-to-all-start.3) | async-done | bytes 16416 | tf_op jit(solution)/shard_map/all_to_all | solution.py:289
  130.1 0.6 shard_map.119
  (25 shorter events, 0.1 us)
Async XLA Ops:
  0.6 35.7 %copy-start.9 = (bf16[128,128]{1,0:T(8,128)(2,1)S(1)}, bf16[128,128]{1,0:T(8,128)(2,1)}, u32[]{:S(2)}) copy-start(bf16[128,128]{1,0:T(8,128)(2,1)} %grad_ref.1) | copy-start | bytes 98308
  2.3 34.0 %all-to-all-start = ((bf16[16,64,128]{2,1,0:T(8,128)(2,1)}), bf16[16,64,128]{2,1,0:T(8,128)(2,1)S(1)}, u32[]{:S(2)}, u32[]{:S(2)}) async-start(bf16[16,64,128]{2,1,0:T(8,128)(2,1)} %shard_map.111), calls=%async_computation | async-start | bytes 524288 | tf_op jit(solution)/shard_map/all_to_all | solution.py:289
  24.3 37.6 %copy-start.5 = (bf16[128,128]{1,0:T(8,128)(2,1)S(1)}, bf16[128,128]{1,0:T(8,128)(2,1)}, u32[]{:S(2)}) copy-start(bf16[128,128]{1,0:T(8,128)(2,1)} %query_ref.3) | copy-start | bytes 98308
  38.2 40.0 %all-to-all-start.1 = ((bf16[32,128,128]{2,1,0:T(8,128)(2,1)}), bf16[32,128,128]{2,1,0:T(8,128)(2,1)S(1)}, u32[]{:S(2)}, u32[]{:S(2)}) async-start(bf16[32,128,128]{2,1,0:T(8,128)(2,1)} %get-tuple-element.18), calls=%async_computation.1 | async-start | bytes 2097152 | tf_op jit(solution)/shard_map/all_to_all | solution.py:289
  50.8 25.6 %collective-permute-start = (bf16[128,4096]{1,0:T(8,128)(2,1)}, bf16[128,4096]{1,0:T(8,128)(2,1)S(1)}, u32[]{:S(2)}, u32[]{:S(2)}) collective-permute-start(bf16[128,4096]{1,0:T(8,128)(2,1)} %get-tuple-element.20), channel_id=1, source_target_pairs={{0,1},{1,0},{2,3},{3,2},{4,5},{5,4},{6,7},{7,6},{8,9},{9,8},{10,11... | collective-permute-start | bytes 3145736 | tf_op jit(solution)/shard_map/ppermute | solution.py:285
  52.8 12.4 %collective-permute-start.3 = (bf16[16,32,128]{2,1,0:T(8,128)(2,1)S(1)}, bf16[16,32,128]{2,1,0:T(8,128)(2,1)S(1)}, u32[]{:S(2)}, u32[]{:S(2)}) collective-permute-start(bf16[16,32,128]{2,1,0:T(8,128)(2,1)S(1)} %slice.4), channel_id=1, source_target_pairs={{0,64},{64,0},{128,192},{192,128},{256,320},{320,256},{384,448},{4... | collective-permute-start | bytes 393224 | tf_op jit(solution)/shard_map/ppermute | solution.py:338
  54.8 13.2 %collective-permute-start.4 = (bf16[16,32,128]{2,1,0:T(8,128)(2,1)S(1)}, bf16[16,32,128]{2,1,0:T(8,128)(2,1)S(1)}, u32[]{:S(2)}, u32[]{:S(2)}) collective-permute-start(bf16[16,32,128]{2,1,0:T(8,128)(2,1)S(1)} %slice.4), channel_id=1, source_target_pairs={{0,128},{64,192},{128,0},{192,64},{256,384},{320,448},{384,256},{4... | collective-permute-start | bytes 393224 | tf_op jit(solution)/shard_map/ppermute | solution.py:338
  58.9 13.0 %collective-permute-start.5 = (bf16[16,32,128]{2,1,0:T(8,128)(2,1)S(1)}, bf16[16,32,128]{2,1,0:T(8,128)(2,1)S(1)}, u32[]{:S(2)}, u32[]{:S(2)}) collective-permute-start(bf16[16,32,128]{2,1,0:T(8,128)(2,1)S(1)} %slice.4), channel_id=1, source_target_pairs={{0,192},{64,128},{128,64},{192,0},{256,448},{320,384},{384,320},{4... | collective-permute-start | bytes 393224 | tf_op jit(solution)/shard_map/ppermute | solution.py:338
  62.0 3.1 %collective-permute-start.2 = (bf16[128,128]{1,0:T(8,128)(2,1)S(1)}, bf16[128,128]{1,0:T(8,128)(2,1)S(1)}, u32[]{:S(2)}, u32[]{:S(2)}) collective-permute-start(bf16[128,128]{1,0:T(8,128)(2,1)S(1)} %copy-done.5), channel_id=1, source_target_pairs={{0,1},{1,0},{2,3},{3,2},{4,5},{5,4},{6,7},{7,6},{8,9},{9,8},{10,11... | collective-permute-start | bytes 98312 | tf_op jit(solution)/shard_map/ppermute | solution.py:285
  65.1 11.2 %copy-start.7 = (bf16[128,128]{1,0:T(8,128)(2,1)}, bf16[128,128]{1,0:T(8,128)(2,1)S(1)}, u32[]{:S(2)}) copy-start(bf16[128,128]{1,0:T(8,128)(2,1)S(1)} %collective-permute-done.2.mate_ref) | copy-start | bytes 98308
  68.0 8.3 %copy-start.1 = (bf16[16,32,128]{2,1,0:T(8,128)(2,1)}, bf16[16,32,128]{2,1,0:T(8,128)(2,1)S(1)}, u32[]{:S(2)}) copy-start(bf16[16,32,128]{2,1,0:T(8,128)(2,1)S(1)} %collective-permute-done.4.refs_1_) | copy-start | bytes 393220
  72.0 4.4 %copy-start.3 = (bf16[16,32,128]{2,1,0:T(8,128)(2,1)}, bf16[16,32,128]{2,1,0:T(8,128)(2,1)S(1)}, u32[]{:S(2)}) copy-start(bf16[16,32,128]{2,1,0:T(8,128)(2,1)S(1)} %collective-permute-done.5.refs_2_) | copy-start | bytes 393220
  74.3 9.1 %copy-start = (f32[256,1024]{1,0:T(8,128)S(1)}, f32[256,1024]{1,0:T(8,128)}, u32[]{:S(2)}) copy-start(f32[256,1024]{1,0:T(8,128)} %get-tuple-element.21.probs_ref) | copy-start | bytes 3145732
  74.3 7.8 %collective-permute-start.6 = (f32[256,256]{1,0:T(8,128)}, f32[256,256]{1,0:T(8,128)}, u32[]{:S(2)}, u32[]{:S(2)}) collective-permute-start(f32[256,256]{1,0:T(8,128)} %get-tuple-element.22.stat_ref), channel_id=1, source_target_pairs={{0,1},{1,0},{2,3},{3,2},{4,5},{5,4},{6,7},{7,6},{8,9},{9,8},{10,11... | collective-permute-start | bytes 786440 | tf_op jit(solution)/shard_map/ppermute | solution.py:285
  78.2 5.1 %copy-start.2 = (bf16[16,32,128]{2,1,0:T(8,128)(2,1)S(1)}, bf16[16,32,128]{2,1,0:T(8,128)(2,1)}, u32[]{:S(2)}) copy-start(bf16[16,32,128]{2,1,0:T(8,128)(2,1)} %copy-done.1) | copy-start | bytes 393220
  78.2 5.1 %copy-start.4 = (bf16[16,32,128]{2,1,0:T(8,128)(2,1)S(1)}, bf16[16,32,128]{2,1,0:T(8,128)(2,1)}, u32[]{:S(2)}) copy-start(bf16[16,32,128]{2,1,0:T(8,128)(2,1)} %copy-done.3) | copy-start | bytes 393220
  78.2 5.1 %copy-start.6 = (bf16[128,128]{1,0:T(8,128)(2,1)S(1)}, bf16[128,128]{1,0:T(8,128)(2,1)}, u32[]{:S(2)}) copy-start(bf16[128,128]{1,0:T(8,128)(2,1)} %query_ref.3) | copy-start | bytes 98308
  78.2 5.1 %copy-start.8 = (bf16[128,128]{1,0:T(8,128)(2,1)S(1)}, bf16[128,128]{1,0:T(8,128)(2,1)}, u32[]{:S(2)}) copy-start(bf16[128,128]{1,0:T(8,128)(2,1)} %copy-done.7) | copy-start | bytes 98308
  80.1 3.2 %collective-permute-start.1 = (f32[128,256]{1,0:T(8,128)S(1)}, f32[128,256]{1,0:T(8,128)S(1)}, u32[]{:S(2)}, u32[]{:S(2)}) collective-permute-start(f32[128,256]{1,0:T(8,128)S(1)} %shard_map.115.part_ref), channel_id=1, source_target_pairs={{0,1},{1,0},{2,3},{3,2},{4,5},{5,4},{6,7},{7,6},{8,9},{9,8},{10,11... | collective-permute-start | bytes 393224 | tf_op jit(solution)/shard_map/ppermute | solution.py:285
  86.1 23.9 %all-to-all-start.2 = ((bf16[32,32,256]{2,1,0:T(8,128)(2,1)}), bf16[32,32,256]{2,1,0:T(8,128)(2,1)S(1)}, u32[]{:S(2)}, u32[]{:S(2)}) async-start(bf16[32,32,256]{2,1,0:T(8,128)(2,1)} %bitcast.1), calls=%async_computation.2 | async-start | bytes 1048576 | tf_op jit(solution)/shard_map/all_to_all | solution.py:289
  92.3 25.4 %collective-permute-start.7 = (f32[128,128]{1,0:T(8,128)S(1)}, f32[128,128]{1,0:T(8,128)S(1)}, u32[]{:S(2)}, u32[]{:S(2)}) collective-permute-start(f32[128,128]{1,0:T(8,128)S(1)} %get-tuple-element.24), channel_id=1, source_target_pairs={{0,1},{1,0},{2,3},{3,2},{4,5},{5,4},{6,7},{7,6},{8,9},{9,8},{10,11... | collective-permute-start | bytes 196616 | tf_op jit(solution)/shard_map/ppermute | solution.py:285
  110.8 19.3 %all-to-all-start.3 = ((bf16[16,4,128]{2,1,0:T(4,128)(2,1)}), bf16[16,4,128]{2,1,0:T(4,128)(2,1)S(1)}, u32[]{:S(2)}, u32[]{:S(2)}) async-start(bf16[16,4,128]{2,1,0:T(4,128)(2,1)} %bitcast.2), calls=%async_computation.3 | async-start | bytes 32768 | tf_op jit(solution)/shard_map/all_to_all | solution.py:289
